TPU v7x, 32 devices: a whole 2x2x4 slice. The times are simulated.
32 devices in a mesh: pipe: 4 (over z), expert: 8 (over y, x, core).
Axes of the slice: x: 2, y: 2, z: 4, core: 2. Of those that a mesh axis runs over, the one named last changes fastest.
Arguments:
- grad_in: bfloat16 [4, 2, 1024, 7168], P('pipe', None, 'expert'), may hold values from -0.59765625 to 0.59765625
- route: int32 [4, 2, 8, 1], P('pipe'), may hold values from 0 to 1; in each aligned block of 8 rows (0 to 7, 8 to 15, ..., all dimensions but the last counted through in order) at most 8 rows name the same one
- stored: bfloat16 [4, 2, 1024, 4096], P('pipe', None, None, 'expert'), may hold values from -6 to 6
- down_weight: bfloat16 [4, 1024, 14336], P('pipe', None, 'expert'), as said below
Outputs:
- d_stored: bfloat16 [4, 2, 1024, 4096], P('pipe', None, None, 'expert')
- weight_grad: bfloat16 [4, 512, 14336], P('pipe', None, 'expert')
Inputs may be any that keep to these rules, and one draw needn't show every extreme that they name: `route`: the 1 entries of a block are different experts. In each micro-batch of each section at most 8 of the 8 blocks name one expert, and in some micro-batch one expert is named by exactly 8. `down_weight`: the copies of sections p and 3 - p are equal.
All inputs are finite; a program needn't handle non-finite values.
Results may differ from a plain program's by a relative error of at most 0.006.
Values may be sent and summed in bfloat16 or wider, within the bound.
No kernel may reach another device: no remote copies, remote signals or barrier semaphores. Data moves between devices by JAX's collectives and lax.ppermute only.
A program may use at most 128 MiB of HBM per device.

v0:
```python
import jax
import jax.numpy as jnp
from jax import lax
from jax.sharding import PartitionSpec as P


def swapped(value, axis, bit):
    mask = 2**bit
    pairs = [(source, source ^ mask) for source in range(lax.axis_size(axis))]
    return lax.ppermute(value, axis, pairs)


def gather_group(block_piece, quarter):
    for bit_number in (0, 1):
        partner_piece = swapped(block_piece, "expert", bit_number)
        low_side = quarter >> bit_number & 1 == 0
        block_piece = jnp.where(
            low_side,
            jnp.concatenate([block_piece, partner_piece], axis=1),
            jnp.concatenate([partner_piece, block_piece], axis=1),
        )
    return block_piece


def reduce_group(partial_value, quarter):
    for bit_number in (1, 0):
        half_cols = partial_value.shape[1] // 2
        keep_side = quarter >> bit_number & 1
        kept_cols = lax.dynamic_slice_in_dim(partial_value, keep_side * half_cols, half_cols, 1)
        given_cols = lax.dynamic_slice_in_dim(
            partial_value, (1 - keep_side) * half_cols, half_cols, 1
        )
        partial_value = kept_cols + swapped(given_cols, "expert", bit_number)
    return partial_value


def per_device(grad_in, route, stored, down_weight):
    grad_rows = grad_in[0]
    routes = route[0]
    saved_pre = stored[0]
    weight = down_weight[0]
    micro_count = grad_rows.shape[0]
    block_rows = grad_rows.shape[1]
    model_width = grad_rows.shape[2]
    quarter_width = model_width // 4
    capacity = saved_pre.shape[1]
    cap_blocks = capacity // block_rows
    quarter_hidden = saved_pre.shape[2] // 2
    rank_count = lax.axis_size("expert")
    rank_index = lax.axis_index("expert")
    group_index = rank_index // 4
    quarter = rank_index % 4
    group_count = rank_count // 4
    sender_ids = jnp.arange(rank_count, dtype=jnp.int32)
    slot_ids = jnp.arange(cap_blocks, dtype=jnp.int32)
    earlier = sender_ids[None, :] < sender_ids[:, None]
    stores = []
    weight_accum = jnp.zeros((weight.shape[0], quarter_width), jnp.float32)
    for batch_index in range(micro_count):
        own_route = lax.dynamic_index_in_dim(routes[batch_index], rank_index, keepdims=False)
        quarters = grad_rows[batch_index].reshape(block_rows, 4, quarter_width).transpose(1, 0, 2)
        build_named = jnp.any(
            jnp.arange(group_count, dtype=jnp.int32)[:, None] == own_route[None, :], axis=1
        )
        outgoing = jnp.where(
            build_named[:, None, None, None], quarters[None], jnp.zeros((), jnp.bfloat16)
        )
        received = lax.all_to_all(
            outgoing.reshape(rank_count, block_rows, quarter_width),
            "expert",
            split_axis=0,
            concat_axis=0,
            tiled=True,
        )
        named = jnp.any(routes[batch_index] == group_index, axis=1)
        slot_index = jnp.sum(named[None, :] & earlier, axis=1)
        matches = named[None, :] & (slot_index[None, :] == slot_ids[:, None])
        source = jnp.sum(jnp.where(matches, sender_ids[None, :], 0), axis=1)
        is_filled = jnp.any(matches, axis=1)
        picked = jnp.take(received, source, axis=0)
        picked = jnp.where(is_filled[:, None, None], picked, jnp.zeros((), jnp.bfloat16))
        picked = picked.reshape(capacity, quarter_width)
        gate_pre = saved_pre[batch_index][:, :quarter_hidden].astype(jnp.float32)
        up_pre = saved_pre[batch_index][:, quarter_hidden:].astype(jnp.float32)
        sigmoid_gate = jax.nn.sigmoid(gate_pre)
        hidden_own = (gate_pre * sigmoid_gate * up_pre).astype(jnp.bfloat16)
        hidden_full = gather_group(hidden_own, quarter)
        partial_value = lax.dot_general(
            picked, weight, (((1,), (1,)), ((), ())), preferred_element_type=jnp.float32
        )
        hidden_grad = reduce_group(partial_value, quarter)
        up_grad = hidden_grad * gate_pre * sigmoid_gate
        gate_grad = hidden_grad * up_pre * sigmoid_gate * (1.0 + gate_pre * (1.0 - sigmoid_gate))
        stores.append(jnp.concatenate([gate_grad, up_grad], axis=1).astype(jnp.bfloat16))
        weight_accum = weight_accum + lax.dot_general(
            hidden_full, picked, (((0,), (0,)), ((), ())), preferred_element_type=jnp.float32
        )
    section_grad = weight_accum.astype(jnp.bfloat16)
    sections = lax.axis_size("pipe")
    section_index = lax.axis_index("pipe")
    half_rows = section_grad.shape[0] // 2
    keep_side = (section_index >= sections // 2).astype(jnp.int32)
    kept_grad = lax.dynamic_slice_in_dim(section_grad, keep_side * half_rows, half_rows, 0)
    given_grad = lax.dynamic_slice_in_dim(section_grad, (1 - keep_side) * half_rows, half_rows, 0)
    pieces = given_grad.reshape(sections, half_rows // sections, quarter_width)
    across = lax.all_to_all(pieces, "pipe", split_axis=0, concat_axis=0, tiled=True)
    returned = lax.all_to_all(across[::-1], "pipe", split_axis=0, concat_axis=0, tiled=True)
    partner_grad = returned.reshape(half_rows, quarter_width)
    weight_grad = (kept_grad.astype(jnp.float32) + partner_grad.astype(jnp.float32)).astype(
        jnp.bfloat16
    )
    return (jnp.stack(stores)[None], weight_grad[None])


def solution(mesh):
    return jax.shard_map(
        per_device,
        mesh=mesh,
        in_specs=(
            P("pipe", None, "expert", None),
            P("pipe", None, None, None),
            P("pipe", None, None, "expert"),
            P("pipe", None, "expert"),
        ),
        out_specs=(P("pipe", None, None, "expert"), P("pipe", None, "expert")),
        check_vma=False,
    )
```

profile of v0, /device:TPU:8, one launch (start us, length us, event | category | flops | bytes accessed | tf_op | source)
XLA Modules:
  0.0 364.8 jit_solution(11735779689506747561)
XLA Ops:
  0.6 0.7 fusion.53
  1.3 0.6 constant_dynamic-slice_fusion.3
  1.9 0.6 iota_compare_fusion.3
  2.7 3.5 fusion.51
  6.3 4.5 %reshape_squeeze.7 = bf16[128,4,1792]{2,1,0:T(4,128)(2,1)} reshape(bf16[1,1,128,7168]{3,2,1,0:T(8,128)(2,1)} %get-tuple-element.12) | data formatting | bytes 3670016 | tf_op jit(solution)/shard_map/reshape;squeeze | solution.py:61
  10.8 1.7 copy.13
  12.4 2.2 bitcast_select_fusion
  14.6 4.5 %all-to-all-start.1 = ((bf16[8,128,1792]{2,1,0:T(8,128)(2,1)}), bf16[8,128,1792]{2,1,0:T(8,128)(2,1)}, u32[]{:S(2)}, u32[]{:S(2)}) async-start(bf16[8,128,1792]{2,1,0:T(8,128)(2,1)} %bitcast_select_fusion), calls=%async_computation.1 | async-start | bytes 7340032 | tf_op jit(solution)/shard_map/all_to_all | solution.py:68
  19.1 0.6 iota_compare_fusion.4
  19.9 2.3 reshape_squeeze.6
  22.3 1.7 copy.11
  24.0 2.1 bitcast_select_fusion.1
  26.1 0.1 convert_reduce_fusion
  26.3 0.1 select_reduce_fusion
  26.5 36.1 %all-to-all-done.1 = bf16[8,128,1792]{2,1,0:T(8,128)(2,1)} async-done(((bf16[8,128,1792]{2,1,0:T(8,128)(2,1)}), bf16[8,128,1792]{2,1,0:T(8,128)(2,1)}, u32[]{:S(2)}, u32[]{:S(2)}) %all-to-all-start.1) | async-done | bytes 3670048 | tf_op jit(solution)/shard_map/all_to_all | solution.py:68
  62.6 4.7 %all-to-all-start = ((bf16[8,128,1792]{2,1,0:T(8,128)(2,1)}), bf16[8,128,1792]{2,1,0:T(8,128)(2,1)}, u32[]{:S(2)}, u32[]{:S(2)}) async-start(bf16[8,128,1792]{2,1,0:T(8,128)(2,1)} %bitcast_select_fusion.1), calls=%async_computation | async-start | bytes 7340032 | tf_op jit(solution)/shard_map/all_to_all | solution.py:68
  67.3 0.1 select_reduce_fusion.1
  67.5 0.1 fusion.48
  67.6 0.1 fusion.46
  67.7 4.7 %gather_fusion.1 = bf16[8,128,1792]{2,1,0:T(8,128)(2,1)} fusion(bf16[8,128,1792]{2,1,0:T(8,128)(2,1)} %all-to-all-done.1, s32[1024]{0:T(1024)S(1)} %pad_clamp_fusion), kind=kCustom, calls=%fused_computation.1.clone | custom fusion | bytes 7340064 | tf_op jit(solution)/shard_map/jit(_take)/gather | solution.py:80
  72.4 2.6 select_select_fusion
  75.1 0.5 copy-done.12
  75.6 4.0 %fusion.1 = f32[1024,1024]{0,1:T(8,128)S(1)} fusion(bf16[1024,1792]{1,0:T(8,128)(2,1)S(1)} %bitcast.50, bf16[1,1024,1792]{2,1,0:T(8,128)(2,1)S(1)} %copy-done.12), kind=kOutput, calls=%fused_computation.6 | convolution fusion | flops 3758096384 | bytes 11534336 | tf_op jit(solution)/shard_map/dot_general | solution.py:88
  79.6 2.0 copy-done.1
  81.5 1.6 constant_dynamic-slice_fusion.2
  83.1 1.7 collective-permute-start.2
  84.8 26.3 %all-to-all-done = bf16[8,128,1792]{2,1,0:T(8,128)(2,1)} async-done(((bf16[8,128,1792]{2,1,0:T(8,128)(2,1)}), bf16[8,128,1792]{2,1,0:T(8,128)(2,1)}, u32[]{:S(2)}, u32[]{:S(2)}) %all-to-all-start) | async-done | bytes 3670048 | tf_op jit(solution)/shard_map/all_to_all | solution.py:68
  111.1 4.7 %gather_fusion = bf16[8,128,1792]{2,1,0:T(8,128)(2,1)} fusion(bf16[8,128,1792]{2,1,0:T(8,128)(2,1)} %all-to-all-done, s32[1024]{0:T(1024)S(1)} %pad_clamp_fusion.1), kind=kCustom, calls=%fused_computation.clone | custom fusion | bytes 7340064 | tf_op jit(solution)/shard_map/jit(_take)/gather | solution.py:80
  115.7 2.6 select_select_fusion.1
  118.4 0.5 copy-done.13
  118.9 4.0 %fusion.3 = f32[1024,1024]{0,1:T(8,128)S(1)} fusion(bf16[1024,1792]{1,0:T(8,128)(2,1)S(1)} %bitcast.52, bf16[1,1024,1792]{2,1,0:T(8,128)(2,1)S(1)} %copy-done.13), kind=kOutput, calls=%fused_computation.8 | convolution fusion | flops 3758096384 | bytes 11534336 | tf_op jit(solution)/shard_map/dot_general | solution.py:88
  122.9 2.0 copy-done.2
  124.9 1.6 constant_dynamic-slice_fusion.5
  126.4 28.6 %collective-permute-done.2 = f32[1024,512]{0,1:T(8,128)S(1)} collective-permute-done((f32[1024,512]{0,1:T(8,128)}, f32[1024,512]{0,1:T(8,128)S(1)}, u32[]{:S(2)}, u32[]{:S(2)}) %collective-permute-start.2) | collective-permute-done | bytes 2097184 | tf_op jit(solution)/shard_map/ppermute | solution.py:10
  155.0 2.0 dynamic-slice_add_fusion
  157.0 1.2 constant_dynamic-slice_fusion.1
  158.2 41.4 %collective-permute-done = f32[1024,512]{0,1:T(8,128)} collective-permute-done((f32[1024,512]{0,1:T(8,128)}, f32[1024,512]{0,1:T(8,128)}, u32[]{:S(2)}, u32[]{:S(2)}) %collective-permute-start) | collective-permute-done | bytes 2097184 | tf_op jit(solution)/shard_map/ppermute | solution.py:10
  199.6 2.0 dynamic-slice_add_fusion.1
  201.6 1.1 constant_dynamic-slice_fusion.4
  202.7 1.5 fusion.52
  204.1 1.5 copy.17
  205.6 3.3 fusion.41
  208.9 0.5 collective-permute-start.6
  209.4 1.5 copy.16
  210.9 0.4 collective-permute-done.6
  211.3 3.0 maximum_select_fusion.5
  214.2 0.4 collective-permute-start.7
  214.7 2.9 fusion.42
  217.6 1.8 collective-permute-done.4
  219.4 0.5 maximum_select_fusion.4
  219.9 1.7 collective-permute-start.5
  221.6 18.9 %collective-permute-done.7 = bf16[1024,512]{0,1:T(8,128)(2,1)} collective-permute-done((bf16[1024,512]{0,1:T(8,128)(2,1)}, bf16[1024,512]{0,1:T(8,128)(2,1)}, u32[]{:S(2)}, u32[]{:S(2)}) %collective-permute-start.7) | collective-permute-done | bytes 1048608 | tf_op jit(solution)/shard_map/ppermute | solution.py:10
  240.6 8.0 %fusion.10 = f32[1024,1792]{1,0:T(8,128)S(1)} fusion(bf16[1024,1792]{1,0:T(8,128)(2,1)} %bitcast.51, bf16[1024,512]{0,1:T(8,128)(2,1)} %collective-permute-done.7, bf16[1024,512]{0,1:T(8,128)(2,1)} %maximum_select_fusion.5, pred[]{:T(512)S(6)} %eq.107), kind=kOutput, calls=%fused_computation.21 | convolution fusion | flops 3767533568 | bytes 13107201 | tf_op jit(solution)/shard_map/dot_general | solution.py:95
  248.6 13.8 %collective-permute-done.5 = bf16[1024,512]{0,1:T(8,128)(2,1)S(1)} collective-permute-done((bf16[1024,512]{0,1:T(8,128)(2,1)S(1)}, bf16[1024,512]{0,1:T(8,128)(2,1)S(1)}, u32[]{:S(2)}, u32[]{:S(2)}) %collective-permute-start.5) | collective-permute-done | bytes 1048608 | tf_op jit(solution)/shard_map/ppermute | solution.py:10
  262.4 5.4 %add_convert_fusion = bf16[1024,1792]{1,0:T(8,128)(2,1)S(1)} fusion(f32[1024,1792]{1,0:T(8,128)S(1)} %fusion.10, bf16[1024,1792]{1,0:T(8,128)(2,1)S(1)} %bitcast.53, bf16[1024,512]{0,1:T(8,128)(2,1)S(1)} %collective-permute-done.5, bf16[1024,512]{0,1:T(8,128)(2,1)S(1)} %maximum_select_fusion.4, pred[]{:T(512)S(6)} %eq.107), kind=kOutput, calls=%fused_computation.2 | convolution fusion | flops 3771203584 | bytes 16777216 | tf_op jit(solution)/shard_map/dot_general | solution.py:95
  267.8 0.1 constant_dynamic-slice_fusion
  267.9 1.6 copy-done.7
  269.6 45.6 %all_to_all.20 = bf16[4,128,1792]{2,1,0:T(8,128)(2,1)S(1)} all-to-all(bf16[4,128,1792]{2,1,0:T(8,128)(2,1)S(1)} %bitcast.47), channel_id=1, replica_groups=mesh['pipe'=4,'expert'=8] {'pipe'}, dimensions={0} | all-to-all | bytes 3670016 | tf_op jit(solution)/shard_map/all_to_all | solution.py:106
  315.2 1.4 rev.3
  316.5 6.2 %all-to-all-start.3 = ((bf16[4,128,1792]{2,1,0:T(8,128)(2,1)}), bf16[4,128,1792]{2,1,0:T(8,128)(2,1)}, u32[]{:S(2)}, u32[]{:S(2)}) async-start(bf16[4,128,1792]{2,1,0:T(8,128)(2,1)} %rev.3), calls=%async_computation.3 | async-start | bytes 3670016 | tf_op jit(solution)/shard_map/all_to_all | solution.py:107
  322.7 1.4 maximum_bitcast_fusion
  324.1 2.6 copy.15
  326.6 34.4 %all-to-all-done.3 = bf16[4,128,1792]{2,1,0:T(8,128)(2,1)} async-done(((bf16[4,128,1792]{2,1,0:T(8,128)(2,1)}), bf16[4,128,1792]{2,1,0:T(8,128)(2,1)}, u32[]{:S(2)}, u32[]{:S(2)}) %all-to-all-start.3) | async-done | bytes 1835040 | tf_op jit(solution)/shard_map/all_to_all | solution.py:107
  361.1 3.7 %fusion.18 = bf16[1,512,1792]{2,1,0:T(8,128)(2,1)} fusion(bf16[4,128,1792]{2,1,0:T(8,128)(2,1)} %all-to-all-done.3, bf16[1024,1792]{1,0:T(8,128)(2,1)} %copy-done.7, s32[]{:T(128)S(6)} %mul.90), kind=kLoop, calls=%fused_computation.31 | loop fusion | flops 3670016 | bytes 5505028 | tf_op jit(solution)/shard_map/broadcast_in_dim | solution.py:112
  (41 shorter events, 0.7 us)
Async XLA Ops:
  14.6 48.0 %all-to-all-start.1 = ((bf16[8,128,1792]{2,1,0:T(8,128)(2,1)}), bf16[8,128,1792]{2,1,0:T(8,128)(2,1)}, u32[]{:S(2)}, u32[]{:S(2)}) async-start(bf16[8,128,1792]{2,1,0:T(8,128)(2,1)} %bitcast_select_fusion), calls=%async_computation.1 | async-start | bytes 7340032 | tf_op jit(solution)/shard_map/all_to_all | solution.py:68
  23.9 2.2 copy-start.11
  62.6 48.5 %all-to-all-start = ((bf16[8,128,1792]{2,1,0:T(8,128)(2,1)}), bf16[8,128,1792]{2,1,0:T(8,128)(2,1)}, u32[]{:S(2)}, u32[]{:S(2)}) async-start(bf16[8,128,1792]{2,1,0:T(8,128)(2,1)} %bitcast_select_fusion.1), calls=%async_computation | async-start | bytes 7340032 | tf_op jit(solution)/shard_map/all_to_all | solution.py:68
  72.4 3.1 copy-start.12
  75.1 4.5 %copy-start.4 = (bf16[8,128,1792]{2,1,0:T(8,128)(2,1)}, bf16[8,128,1792]{2,1,0:T(8,128)(2,1)S(1)}, u32[]{:S(2)}) copy-start(bf16[8,128,1792]{2,1,0:T(8,128)(2,1)S(1)} %select_select_fusion) | copy-start | bytes 11010052
  79.6 2.0 copy-start.1
  83.1 71.9 %collective-permute-start.2 = (f32[1024,512]{0,1:T(8,128)}, f32[1024,512]{0,1:T(8,128)S(1)}, u32[]{:S(2)}, u32[]{:S(2)}) collective-permute-start(f32[1024,512]{0,1:T(8,128)} %constant_dynamic-slice_fusion.2), channel_id=1, source_target_pairs={{0,2},{1,3},{2,0},{3,1},{4,6},{5,7},{6,4},{7,5},{8,10},{9,11},{10,... | collective-permute-start | bytes 6291464 | tf_op jit(solution)/shard_map/ppermute | solution.py:10
  115.7 3.1 copy-start.13
  118.4 4.5 %copy-start.5 = (bf16[8,128,1792]{2,1,0:T(8,128)(2,1)}, bf16[8,128,1792]{2,1,0:T(8,128)(2,1)S(1)}, u32[]{:S(2)}) copy-start(bf16[8,128,1792]{2,1,0:T(8,128)(2,1)S(1)} %select_select_fusion.1) | copy-start | bytes 11010052
  122.9 2.0 copy-start.2
  126.4 73.2 %collective-permute-start = (f32[1024,512]{0,1:T(8,128)}, f32[1024,512]{0,1:T(8,128)}, u32[]{:S(2)}, u32[]{:S(2)}) collective-permute-start(f32[1024,512]{0,1:T(8,128)} %constant_dynamic-slice_fusion.5), channel_id=1, source_target_pairs={{0,2},{1,3},{2,0},{3,1},{4,6},{5,7},{6,4},{7,5},{8,10},{9,11},{10,... | collective-permute-start | bytes 6291464 | tf_op jit(solution)/shard_map/ppermute | solution.py:10
  126.4 73.1 %copy-start.3 = (f32[1024,1024]{0,1:T(8,128)S(1)}, f32[1024,1024]{0,1:T(8,128)}, u32[]{:S(2)}) copy-start(f32[1024,1024]{0,1:T(8,128)} %copy-done.2) | copy-start | bytes 12582916
  157.0 44.6 %copy-start = (f32[1024,512]{0,1:T(8,128)}, f32[1024,512]{0,1:T(8,128)S(1)}, u32[]{:S(2)}) copy-start(f32[1024,512]{0,1:T(8,128)S(1)} %dynamic-slice_add_fusion) | copy-start | bytes 6291460
  158.2 44.5 %copy-start.8 = (bf16[1,2,1024,512]{3,2,1,0:T(8,128)(2,1)S(1)}, bf16[1,2,1024,512]{3,2,1,0:T(8,128)(2,1)}, u32[]{:S(2)}) copy-start(bf16[1,2,1024,512]{3,2,1,0:T(8,128)(2,1)} %param.8) | copy-start | bytes 6291460
  158.2 47.5 %collective-permute-start.3 = (f32[1024,256]{0,1:T(8,128)}, f32[1024,256]{0,1:T(8,128)}, u32[]{:S(2)}, u32[]{:S(2)}) collective-permute-start(f32[1024,256]{0,1:T(8,128)} %constant_dynamic-slice_fusion.1), channel_id=1, source_target_pairs={{0,1},{1,0},{2,3},{3,2},{4,5},{5,4},{6,7},{7,6},{8,9},{9,8},{10,11... | collective-permute-start | bytes 3145736 | tf_op jit(solution)/shard_map/ppermute | solution.py:10
  202.7 12.0 %collective-permute-start.1 = (f32[1024,256]{0,1:T(8,128)}, f32[1024,256]{0,1:T(8,128)}, u32[]{:S(2)}, u32[]{:S(2)}) collective-permute-start(f32[1024,256]{0,1:T(8,128)} %constant_dynamic-slice_fusion.4), channel_id=1, source_target_pairs={{0,1},{1,0},{2,3},{3,2},{4,5},{5,4},{6,7},{7,6},{8,9},{9,8},{10,11... | collective-permute-start | bytes 3145736 | tf_op jit(solution)/shard_map/ppermute | solution.py:10
  208.9 2.4 collective-permute-start.6
  214.2 26.3 %collective-permute-start.7 = (bf16[1024,512]{0,1:T(8,128)(2,1)}, bf16[1024,512]{0,1:T(8,128)(2,1)}, u32[]{:S(2)}, u32[]{:S(2)}) collective-permute-start(bf16[1024,512]{0,1:T(8,128)(2,1)} %maximum_select_fusion.5), channel_id=1, source_target_pairs={{0,2},{1,3},{2,0},{3,1},{4,6},{5,7},{6,4},{7,5},{8,10},{9,11},{10,... | collective-permute-start | bytes 3145736 | tf_op jit(solution)/shard_map/ppermute | solution.py:10
  217.5 1.9 collective-permute-start.4
  219.9 42.4 %collective-permute-start.5 = (bf16[1024,512]{0,1:T(8,128)(2,1)S(1)}, bf16[1024,512]{0,1:T(8,128)(2,1)S(1)}, u32[]{:S(2)}, u32[]{:S(2)}) collective-permute-start(bf16[1024,512]{0,1:T(8,128)(2,1)S(1)} %maximum_select_fusion.4), channel_id=1, source_target_pairs={{0,2},{1,3},{2,0},{3,1},{4,6},{5,7},{6,4},{7,5},{8,10},{9,11},{10,... | collective-permute-start | bytes 3145736 | tf_op jit(solution)/shard_map/ppermute | solution.py:10
  221.6 40.8 %copy-start.6 = (bf16[8,128,1792]{2,1,0:T(8,128)(2,1)S(1)}, bf16[8,128,1792]{2,1,0:T(8,128)(2,1)}, u32[]{:S(2)}) copy-start(bf16[8,128,1792]{2,1,0:T(8,128)(2,1)} %copy-done.5) | copy-start | bytes 11010052
  267.8 1.8 copy-start.7
  315.2 7.5 %copy-start.9 = (bf16[1,1024,256]{1,2,0:T(8,128)(2,1)S(1)}, bf16[1,1024,256]{1,2,0:T(8,128)(2,1)}, u32[]{:S(2)}) copy-start(bf16[1,1024,256]{1,2,0:T(8,128)(2,1)} %get-tuple-element.9) | copy-start | bytes 1572868
  315.2 7.5 %copy-start.10 = (bf16[1,1024,256]{1,2,0:T(8,128)(2,1)S(1)}, bf16[1,1024,256]{1,2,0:T(8,128)(2,1)}, u32[]{:S(2)}) copy-start(bf16[1,1024,256]{1,2,0:T(8,128)(2,1)} %get-tuple-element.10) | copy-start | bytes 1572868
  316.5 44.5 %all-to-all-start.3 = ((bf16[4,128,1792]{2,1,0:T(8,128)(2,1)}), bf16[4,128,1792]{2,1,0:T(8,128)(2,1)}, u32[]{:S(2)}, u32[]{:S(2)}) async-start(bf16[4,128,1792]{2,1,0:T(8,128)(2,1)} %rev.3), calls=%async_computation.3 | async-start | bytes 3670016 | tf_op jit(solution)/shard_map/all_to_all | solution.py:107
where the time goes:
time: 370 us; the launch traced here: 365 us
  waiting for transfers between devices  202 us (55%)
  blocking collectives  45.6 us (12%)
  local copies, waits for them, and re-layouts  45.1 us (12%)
  other arithmetic  30.3 us (8%)
  matrix products  21.4 us (6%)
  starting transfers between devices  19.8 us (5%)
    ppermute x8, waiting for transfers between devices, swapped(): return lax.ppermute(value, axis, pairs)  105 us
    all_to_all x2, waiting for transfers between devices, per_device(): lax.all_to_all(outgoing.reshape(rank_count, block_rows, quarter_width), '...  62.4 us
    all_to_all x1, blocking collectives, per_device(): lax.all_to_all(pieces, 'pipe', split_axis=0, concat_axis=0, tiled=True)  45.6 us
    all_to_all x1, waiting for transfers between devices, per_device(): lax.all_to_all(across[::-1], 'pipe', split_axis=0, concat_axis=0, tiled=T...  34.4 us
    dot_general x2, matrix products, per_device(): lax.dot_general(hidden_full, picked, (((0,), (0,)), ((), ())), preferred_...  13.4 us
    unnamed x31, local copies, waits for them, and re-layouts  12.1 us
    gather x2, local copies, waits for them, and re-layouts, per_device(): picked = jnp.take(received, source, axis=0)  9.39 us
    all_to_all x2, starting transfers between devices, per_device(): lax.all_to_all(outgoing.reshape(rank_count, block_rows, quarter_width), '...  9.17 us
  transfers between devices with their start and end apart: 11, of which 9 were waited for; matrix products, arithmetic and copies ran while one was open for 18% of the time, Pallas kernels for 0%

commit v1 on v0

v1 whole, which is shorter than its diff:
```python
import functools

import jax
import jax.numpy as jnp
from jax import lax
from jax.experimental import pallas as pl
from jax.experimental.pallas import tpu as pltpu
from jax.sharding import PartitionSpec as P

TILE = 128
GROUP = 4
VMEM_BYTES = 40 * 1024 * 1024
ANY = pl.BlockSpec(memory_space=pl.ANY)
SMEM = pl.BlockSpec(memory_space=pltpu.SMEM)
VMEM = pl.BlockSpec(memory_space=pltpu.VMEM)


def params():
    return pltpu.CompilerParams(vmem_limit_bytes=VMEM_BYTES)


def cost(flops, nbytes):
    return pl.CostEstimate(flops=flops, bytes_accessed=nbytes, transcendentals=0)


def column_chunks(width):
    tiles = width // TILE
    sizes = [2]
    while sum(sizes) < tiles:
        sizes.append(min(3, tiles - sum(sizes)))
    chunks, offset = [], 0
    for size in sizes:
        chunks.append((offset * TILE, size * TILE))
        offset += size
    return chunks


def after(value, *others):
    return lax.optimization_barrier((value, *others))[0]


def swap(value, mask):
    size = lax.axis_size("expert")
    return lax.ppermute(value, "expert", [(i, i ^ mask) for i in range(size)])


def from_group(value, step):
    size = lax.axis_size("expert")
    return lax.ppermute(value, "expert", [((i + step * GROUP) % size, i) for i in range(size)])


def mirror(value):
    size = lax.axis_size("pipe")
    return lax.ppermute(value, "pipe", [(i, size - 1 - i) for i in range(size)])


def place():
    rank = lax.axis_index("expert")
    return rank // GROUP, rank % GROUP


def named_and_slot(route_ref, micro, block, expert):
    ranks, top = route_ref.shape[1], route_ref.shape[2]

    def names(j):
        hit = route_ref[micro, j, 0] == expert
        for t in range(1, top):
            hit = jnp.logical_or(hit, route_ref[micro, j, t] == expert)
        return hit

    slot = jnp.int32(0)
    for j in range(ranks):
        slot = slot + jnp.where(jnp.logical_and(names(j), j < block), 1, 0)
    return names(block), slot


def act_kernel(route_ref, stored_ref, out_ref):
    micros, ranks = route_ref.shape[0], route_ref.shape[1]
    expert, _ = place()
    hidden = out_ref.shape[0]
    rows = out_ref.shape[1] // (micros * ranks)
    for micro in range(micros):
        for block in range(ranks):
            named, slot = named_and_slot(route_ref, micro, block, expert)
            columns = pl.ds((micro * ranks + block) * rows, rows)

            @pl.when(named)
            def _():
                pre = stored_ref[micro, pl.ds(pl.multiple_of(slot * rows, rows), rows), :]
                gate = pre[:, :hidden].astype(jnp.float32)
                up = pre[:, hidden:].astype(jnp.float32)
                act = gate * jax.nn.sigmoid(gate) * up
                out_ref[:, columns] = act.T.astype(out_ref.dtype)

            @pl.when(jnp.logical_not(named))
            def _():
                out_ref[:, columns] = jnp.zeros((hidden, rows), out_ref.dtype)


def hidden_acts(route, stored, rows):
    micros, ranks, _ = route.shape
    hidden = stored.shape[2] // 2
    shape = (hidden, micros * ranks * rows)
    return pl.pallas_call(
        act_kernel,
        out_shape=jax.ShapeDtypeStruct(shape, jnp.bfloat16),
        in_specs=[SMEM, VMEM],
        out_specs=VMEM,
        compiler_params=params(),
        cost_estimate=cost(shape[0] * shape[1] * 8, stored.size * 2 + shape[0] * shape[1] * 2),
        name="hidden_acts",
    )(route, stored)


def load_tokens(piece_refs, token_ref, sems):
    group, quarter = place()
    groups = len(piece_refs) // GROUP
    copies = []
    for step in range(groups):
        for mask in range(GROUP):
            block = lax.rem(group + step, groups) * GROUP + (quarter ^ mask)
            copy = pltpu.make_async_copy(
                piece_refs[step * GROUP + mask], token_ref.at[:, block], sems.at[step * GROUP + mask]
            )
            copy.start()
            copies.append(copy)
    return copies


def load_hidden(given, hidden_refs, hidden_ref, sems):
    _, quarter = place()
    upper = lax.axis_index("pipe") < lax.axis_size("pipe") // 2
    half = jnp.where(upper, 1, 0) if given else jnp.where(upper, 0, 1)
    here = half == quarter // 2
    units = hidden_refs[0].shape[0]
    copies = []
    for mask in range(2):
        core = (quarter % 2) ^ mask
        target = hidden_ref.at[pl.ds(pl.multiple_of(core * units, units), units)]

        @pl.when(here)
        def _():
            pltpu.make_async_copy(hidden_refs[mask], target, sems.at[mask]).start()

        @pl.when(jnp.logical_not(here))
        def _():
            pltpu.make_async_copy(hidden_refs[2 + mask], target, sems.at[mask]).start()

        copies.append(pltpu.make_async_copy(hidden_refs[mask], target, sems.at[mask]))
    return copies


def half_grad(given, refs, pieces, hidden_scratch, token_scratch, hidden_sems, token_sems):
    hidden_refs, piece_refs = refs[:GROUP], refs[GROUP : GROUP + pieces]
    copies = load_hidden(given, hidden_refs, hidden_scratch, hidden_sems)
    copies += load_tokens(piece_refs, token_scratch, token_sems)
    for copy in copies:
        copy.wait()
    rows = hidden_scratch.shape[1]
    return jnp.dot(
        hidden_scratch[...],
        token_scratch[...].reshape(rows, token_scratch.shape[3]),
        preferred_element_type=jnp.float32,
    )


def given_kernel(pieces, *refs):
    out_ref = refs[GROUP + pieces]
    out_ref[...] = half_grad(True, refs, pieces, *refs[GROUP + pieces + 1 :]).astype(out_ref.dtype)


def scratches(hidden_all, pieces):
    units, rows = hidden_all[0].shape
    micros, block_rows, width = pieces[0].shape
    return [
        pltpu.VMEM((2 * units, rows), jnp.bfloat16),
        pltpu.VMEM((micros, len(pieces), block_rows, width), jnp.bfloat16),
        pltpu.SemaphoreType.DMA((2,)),
        pltpu.SemaphoreType.DMA((len(pieces),)),
    ]


def grad_cost(hidden_all, pieces):
    units, rows = hidden_all[0].shape
    width = pieces[0].shape[2]
    return cost(4 * units * rows * width, 4 * units * rows + 2 * rows * width + 4 * units * width)


def given_half(hidden_all, pieces):
    units = hidden_all[0].shape[0]
    return pl.pallas_call(
        functools.partial(given_kernel, len(pieces)),
        out_shape=jax.ShapeDtypeStruct((2 * units, pieces[0].shape[2]), jnp.bfloat16),
        in_specs=[ANY] * (GROUP + len(pieces)),
        out_specs=VMEM,
        scratch_shapes=scratches(hidden_all, pieces),
        compiler_params=params(),
        cost_estimate=grad_cost(hidden_all, pieces),
        name="given_half",
    )(*hidden_all, *pieces)


def kept_kernel(pieces, offset, aliased, *refs):
    partner_ref = refs[GROUP + pieces]
    refs_after = refs[GROUP + pieces + (2 if aliased else 1) :]
    out_ref, sum_scratch, out_sem = refs_after[0], refs_after[5], refs_after[6]
    total = half_grad(False, refs, pieces, *refs_after[1:5]) + partner_ref[...].astype(jnp.float32)
    sum_scratch[...] = total.astype(sum_scratch.dtype)
    width = sum_scratch.shape[1]
    copy = pltpu.make_async_copy(sum_scratch, out_ref.at[:, pl.ds(offset, width)], out_sem)
    copy.start()
    copy.wait()


def kept_half(hidden_all, pieces, partner, total, offset, full_width):
    units = hidden_all[0].shape[0]
    width = pieces[0].shape[2]
    operands = [*hidden_all, *pieces, partner]
    specs = [ANY] * (GROUP + len(pieces)) + [VMEM]
    aliases = {}
    if total is not None:
        aliases = {len(operands): 0}
        operands.append(total)
        specs.append(ANY)
    return pl.pallas_call(
        functools.partial(kept_kernel, len(pieces), offset, total is not None),
        out_shape=jax.ShapeDtypeStruct((2 * units, full_width), jnp.bfloat16),
        in_specs=specs,
        out_specs=ANY,
        scratch_shapes=scratches(hidden_all, pieces)
        + [pltpu.VMEM((2 * units, width), jnp.bfloat16), pltpu.SemaphoreType.DMA],
        input_output_aliases=aliases,
        compiler_params=params(),
        cost_estimate=grad_cost(hidden_all, pieces),
        name="kept_half",
    )(*operands)


def partial_kernel(chunks, *refs):
    pieces = len(chunks) * GROUP
    piece_refs, weight_ref = refs[:pieces], refs[pieces]
    keep_ref, send_ref, token_scratch, sems = refs[pieces + 1 :]
    _, quarter = place()
    copies = []
    for i, (offset, width) in enumerate(chunks):
        for mask in range(GROUP):
            copy = pltpu.make_async_copy(
                piece_refs[i * GROUP + mask],
                token_scratch.at[:, quarter ^ mask, :, pl.ds(offset, width)],
                sems.at[i * GROUP + mask],
            )
            copy.start()
            copies.append(copy)
    for copy in copies:
        copy.wait()
    rows = keep_ref.shape[1]
    units = keep_ref.shape[2]
    tokens = token_scratch[...].reshape(rows, token_scratch.shape[3])
    for mask, out_ref, place_in in ((3, send_ref, 1), (2, keep_ref, 1), (1, send_ref, 0), (0, keep_ref, 0)):
        start = pl.multiple_of((quarter ^ mask) * units, units)
        out_ref[place_in] = lax.dot_general(
            tokens,
            weight_ref[pl.ds(start, units), :],
            (((1,), (1,)), ((), ())),
            preferred_element_type=jnp.float32,
        ).astype(out_ref.dtype)


def partial_grads(pieces, weight, chunks, micros, block_rows):
    rows = micros * GROUP * block_rows
    all_units, width = weight.shape
    units = all_units // GROUP
    return pl.pallas_call(
        functools.partial(partial_kernel, chunks),
        out_shape=(
            jax.ShapeDtypeStruct((2, rows, units), jnp.float32),
            jax.ShapeDtypeStruct((2, rows, units), jnp.bfloat16),
        ),
        in_specs=[ANY] * len(pieces) + [VMEM],
        out_specs=(VMEM, VMEM),
        scratch_shapes=[
            pltpu.VMEM((micros, GROUP, block_rows, width), jnp.bfloat16),
            pltpu.SemaphoreType.DMA((len(pieces),)),
        ],
        compiler_params=params(),
        cost_estimate=cost(2 * rows * width * all_units, 2 * (rows + all_units) * width + 6 * rows * all_units // 2),
        name="partial_grads",
    )(*pieces, weight)


def store_kernel(first, route_ref, group_ref, stored_ref, keep_ref, core_ref, across_ref, *refs):
    out_ref, scratch, zeros, sems, zero_sems = refs[-5:]
    micros, ranks = route_ref.shape[0], route_ref.shape[1]
    expert, _ = place()
    source = group_ref[0]
    block_rows = scratch.shape[2]
    hidden = scratch.shape[3] // 2
    slots = stored_ref.shape[1] // block_rows
    done = []

    def target(micro, slot):
        return out_ref.at[micro, pl.ds(pl.multiple_of(slot * block_rows, block_rows), block_rows)]

    if first:
        zeros[...] = jnp.zeros_like(zeros)
        for micro in range(micros):
            count = jnp.int32(0)
            for j in range(ranks):
                count = count + jnp.where(named_and_slot(route_ref, micro, j, expert)[0], 1, 0)
            for slot in range(slots):
                copy = pltpu.make_async_copy(zeros, target(micro, slot), zero_sems.at[micro * slots + slot])
                empty = slot >= count
                pl.when(empty)(copy.start)
                done.append((empty, copy))
    for micro in range(micros):
        for member in range(GROUP):
            block = source * GROUP + member
            named, slot = named_and_slot(route_ref, micro, block, expert)
            copy = pltpu.make_async_copy(
                scratch.at[micro, member], target(micro, slot), sems.at[micro * GROUP + member]
            )

            @pl.when(named)
            def _():
                rows = pl.ds((micro * GROUP + member) * block_rows, block_rows)
                grad = (
                    keep_ref[0, rows, :]
                    + core_ref[0, rows, :].astype(jnp.float32)
                    + across_ref[rows, :].astype(jnp.float32)
                )
                pre = stored_ref[micro, pl.ds(pl.multiple_of(slot * block_rows, block_rows), block_rows), :]
                gate = pre[:, :hidden].astype(jnp.float32)
                up = pre[:, hidden:].astype(jnp.float32)
                sigmoid = jax.nn.sigmoid(gate)
                scaled = grad * sigmoid
                scratch[micro, member, :, hidden:] = (scaled * gate).astype(scratch.dtype)
                scratch[micro, member, :, :hidden] = (
                    scaled * up * (1.0 + gate * (1.0 - sigmoid))
                ).astype(scratch.dtype)
                copy.start()

            done.append((named, copy))
    for started, copy in done:
        pl.when(started)(copy.wait)


def store_grads(route, group, stored, keep, core, across, total):
    micros = stored.shape[0]
    rows, units = across.shape
    block_rows = rows // (micros * GROUP)
    slots = stored.shape[1] // block_rows
    half = pl.BlockSpec((1, rows, units), lambda i: (0, 0, 0))
    operands = [route, group.reshape(1), stored, keep, core, across]
    whole = [pl.BlockSpec(v.shape, lambda i, n=v.ndim: (0,) * n) for v in (stored, across)]
    specs = [SMEM, SMEM, whole[0], half, half, whole[1]]
    aliases = {}
    if total is not None:
        aliases = {len(operands): 0}
        operands.append(total)
        specs.append(ANY)
    return pl.pallas_call(
        functools.partial(store_kernel, total is None),
        grid=(1,),
        out_shape=jax.ShapeDtypeStruct(stored.shape, jnp.bfloat16),
        in_specs=specs,
        out_specs=ANY,
        scratch_shapes=[
            pltpu.VMEM((micros, GROUP, block_rows, 2 * units), jnp.bfloat16),
            pltpu.VMEM((block_rows, 2 * units), jnp.bfloat16),
            pltpu.SemaphoreType.DMA((micros * GROUP,)),
            pltpu.SemaphoreType.DMA((micros * slots,)),
        ],
        input_output_aliases=aliases,
        compiler_params=params(),
        cost_estimate=cost(rows * units * 16, 8 * rows * units + stored.size * 4),
        name="store_grads",
    )(*operands)


def per_device(grad_in, route, stored, down_weight):
    grad_rows, routes, saved_pre, weight = grad_in[0], route[0], stored[0], down_weight[0]
    micros, block_rows, model_width = grad_rows.shape
    quarter_width = model_width // GROUP
    groups = lax.axis_size("expert") // GROUP
    group, quarter = place()
    chunks = column_chunks(quarter_width)

    def own_slice(mask, offset, width):
        start = (quarter ^ mask) * quarter_width + offset
        return lax.dynamic_slice(grad_rows, (0, 0, start), (micros, block_rows, width))

    hidden = hidden_acts(routes, saved_pre, block_rows)
    inside = []
    outside = []
    hidden_all = None
    for i, (offset, width) in enumerate(chunks):
        outgoing = [own_slice(mask, offset, width) for mask in range(GROUP)]
        if i >= 1:
            outgoing[2] = after(outgoing[2], inside[i - 1][2])
            outgoing[3] = after(outgoing[3], inside[i - 1][3])
            outgoing[1] = after(outgoing[1], inside[i - 1][1])
        inside.append([outgoing[0]] + [swap(outgoing[mask], mask) for mask in range(1, GROUP)])
        if i == 0:
            crossed = swap(hidden, 2)
            hidden_all = [hidden, swap(hidden, 1), crossed, swap(crossed, 1)]
        arrived = []
        for step in range(1, groups):
            for mask in range(GROUP):
                piece = inside[i][mask]
                if i >= 1:
                    piece = after(piece, outside[i - 1][(step - 1) * GROUP + mask])
                arrived.append(from_group(piece, step))
        outside.append(arrived)

    partners = []
    for inner, outer in zip(inside, outside):
        partners.append(mirror(given_half(hidden_all, inner + outer)))
    weight_grad = None
    for (offset, width), inner, outer, partner in zip(chunks, inside, outside, partners):
        weight_grad = kept_half(hidden_all, inner + outer, partner, weight_grad, offset, quarter_width)

    store_grad = None
    for step in range(groups):
        if step == 0:
            pieces = [piece for chunk in inside for piece in chunk]
        else:
            first = (step - 1) * GROUP
            pieces = [piece for chunk in outside for piece in chunk[first : first + GROUP]]
        keep, send = partial_grads(pieces, weight, chunks, micros, block_rows)
        core = swap(send, 1)
        across = swap((keep[1] + core[1].astype(jnp.float32)).astype(jnp.bfloat16), 2)
        source = lax.rem(group + step, groups).astype(jnp.int32)
        store_grad = store_grads(routes, source, saved_pre, keep, core, across, store_grad)
    return store_grad[None], weight_grad[None]


def solution(mesh):
    return jax.shard_map(
        per_device,
        mesh=mesh,
        in_specs=(
            P("pipe", None, "expert", None),
            P("pipe", None, None, None),
            P("pipe", None, None, "expert"),
            P("pipe", None, "expert"),
        ),
        out_specs=(P("pipe", None, None, "expert"), P("pipe", None, "expert")),
        check_vma=False,
    )
```

time: 370 us -> 215 us (0.58); the launches traced: 365 us -> 214 us
  waiting for transfers between devices: 202 us -> 93.5 us
  Pallas kernels: 0 us -> 53.1 us
  blocking collectives: 45.6 us -> 0 us
  other arithmetic: 30.3 us -> 2.12 us
  matrix products: 21.4 us -> 0 us
  local copies, waits for them, and re-layouts: 45.1 us -> 26.8 us
  starting transfers between devices: 19.8 us -> 36.5 us
    all_to_all x3 -> x0, waiting for transfers between devices: 96.8 us -> none  [the longest x2 62.4 us: per_device(): lax.all_to_all(outgoing.reshape(rank_count, block_rows, quarter_width), '...]
    pallas_call x0 -> x15, Pallas kernels: none -> 53.1 us  [the longest x5 20.4 us: kept_half(): pl.pallas_call(functools.partial(kept_kernel, len(pieces), offset, total...]
    all_to_all x1 -> x0, blocking collectives: 45.6 us -> none  [per_device(): lax.all_to_all(pieces, 'pipe', split_axis=0, concat_axis=0, tiled=True)]
    ppermute x8 -> x47, starting transfers between devices: 4.44 us -> 36.5 us  [the longest x20 21.6 us: from_group(): lax.ppermute(value, 'expert', [((i + step * GROUP) % size, i) for i in ra...]
    dot_general x4 -> x0, matrix products: 21.4 us -> none  [the longest x2 13.4 us: per_device(): lax.dot_general(hidden_full, picked, (((0,), (0,)), ((), ())), preferred_...]
    all_to_all x3 -> x0, starting transfers between devices: 15.3 us -> none  [the longest x2 9.17 us: per_device(): lax.all_to_all(outgoing.reshape(rank_count, block_rows, quarter_width), '...]
    select_n x8 -> x0, other arithmetic: 13.1 us -> none  [the longest x2 5.29 us: per_device(): jnp.where(is_filled[:, None, None], picked, jnp.zeros((), jnp.bfloat16))]
    ppermute x8 -> x47, waiting for transfers between devices: 105 us -> 93.5 us  [the longest x5 42.6 us: mirror(): return lax.ppermute(value, 'pipe', [(i, size - 1 - i) for i in range(size)])]
  transfers between devices with their start and end apart: 11 -> 47, of which waited for: 9 -> 16; matrix products, arithmetic and copies ran while one was open for 18% -> 3% of each run, Pallas kernels for 0% -> 24%
where the time goes in v1:
time: 215 us; the launch traced here: 214 us
  waiting for transfers between devices  93.5 us (43%)
  Pallas kernels  53.1 us (25%)
  starting transfers between devices  36.5 us (17%)
  local copies, waits for them, and re-layouts  26.8 us (12%)
    ppermute x5, waiting for transfers between devices, mirror(): return lax.ppermute(value, 'pipe', [(i, size - 1 - i) for i in range(size)])  42.6 us
    ppermute x20, waiting for transfers between devices, from_group(): lax.ppermute(value, 'expert', [((i + step * GROUP) % size, i) for i in ra...  39.7 us
    ppermute x20, starting transfers between devices, from_group(): lax.ppermute(value, 'expert', [((i + step * GROUP) % size, i) for i in ra...  21.6 us
    unnamed x198, local copies, waits for them, and re-layouts  21.5 us
    pallas_call x5, Pallas kernels, kept_half(): pl.pallas_call(functools.partial(kept_kernel, len(pieces), offset, total...  20.4 us
    pallas_call x5, Pallas kernels, given_half(): pl.pallas_call(functools.partial(given_kernel, len(pieces)), out_shape=ja...  15.5 us
    ppermute x22, waiting for transfers between devices, swap(): return lax.ppermute(value, 'expert', [(i, i ^ mask) for i in range(size)])  11.2 us
    pallas_call x2, Pallas kernels, partial_grads(): pl.pallas_call(functools.partial(partial_kernel, chunks), out_shape=(jax....  11 us
  transfers between devices with their start and end apart: 47, of which 16 were waited for; matrix products, arithmetic and copies ran while one was open for 3% of the time, Pallas kernels for 24%

profile of v1, /device:TPU:8, one launch (start us, length us, event | category | flops | bytes accessed | tf_op | source)
XLA Modules:
  0.0 213.9 jit_solution(16518804892401030744)
XLA Ops:
  0.7 1.8 dynamic-slice_bitcast_fusion.16
  2.5 0.9 collective-permute-start.5
  4.3 3.4 %dynamic-slice_bitcast_fusion = (bf16[2,128,384]{2,1,0:T(8,128)(2,1)}, bf16[2,128,384]{2,1,0:T(8,128)(2,1)}, bf16[2,128,384]{2,1,0:T(8,128)(2,1)S(1)}, bf16[2,12...) fusion(bf16[1,2,128,7168]{3,2,1,0:T(8,128)(2,1)} %param.4, ...), kind=kLoop, calls=%fused_computation.4 | loop fusion | bytes 6291520 | tf_op jit(solution)/shard_map/dynamic_slice | solution.py:390
  8.2 1.2 collective-permute-start.12
  9.5 1.5 collective-permute-start
  12.7 3.1 %collective-permute-done.refs_0_.refs_8_ = bf16[2,128,256]{2,1,0:T(8,128)(2,1)S(1)} collective-permute-done((bf16[2,128,256]{2,1,0:T(8,128)(2,1)S(1)}, bf16[2,128,256]{2,1,0:T(8,128)(2,1)S(1)}, u32[]{:S(2)}, u32[]{:S(2)}) %collective-permute-start) | collective-permute-done | bytes 131104 | tf_op jit(solution)/shard_map/ppermute | solution.py:49
  16.4 1.5 collective-permute-start.4
  19.2 1.1 collective-permute-start.2
  20.3 1.0 collective-permute-start.7
  23.1 2.8 %collective-permute-done.2.refs_1_.refs_9_ = bf16[2,128,256]{2,1,0:T(8,128)(2,1)S(1)} collective-permute-done((bf16[2,128,256]{2,1,0:T(8,128)(2,1)}, bf16[2,128,256]{2,1,0:T(8,128)(2,1)S(1)}, u32[]{:S(2)}, u32[]{:S(2)}) %collective-permute-start.2) | collective-permute-done | bytes 131104 | tf_op jit(solution)/shard_map/ppermute | solution.py:49
  26.5 1.0 collective-permute-start.13
  28.2 1.0 collective-permute-start.11
  30.6 1.3 collective-permute-start.9
  31.9 1.1 collective-permute-start.14
  33.0 1.4 collective-permute-done.13.refs_7_.refs_11_
  35.0 3.5 %collective-permute-done.11.refs_6_.refs_10_ = bf16[2,128,384]{2,1,0:T(8,128)(2,1)S(1)} collective-permute-done((bf16[2,128,384]{2,1,0:T(8,128)(2,1)S(1)}, bf16[2,128,384]{2,1,0:T(8,128)(2,1)S(1)}, u32[]{:S(2)}, u32[]{:S(2)}) %collective-permute-start.11) | collective-permute-done | bytes 196640 | tf_op jit(solution)/shard_map/ppermute | solution.py:49
  39.9 1.3 hidden_acts.1.refs_0_
  41.3 1.6 collective-permute-start.40
  42.9 2.5 %collective-permute-done.14.refs_8_ = bf16[2,128,384]{2,1,0:T(8,128)(2,1)} collective-permute-done((bf16[2,128,384]{2,1,0:T(8,128)(2,1)}, bf16[2,128,384]{2,1,0:T(8,128)(2,1)}, u32[]{:S(2)}, u32[]{:S(2)}) %collective-permute-start.14) | collective-permute-done | bytes 196640 | tf_op jit(solution)/shard_map/ppermute | solution.py:49
  45.4 1.5 collective-permute-start.20
  47.4 1.5 collective-permute-start.16
  49.4 3.8 %collective-permute-done.20.refs_11_ = bf16[2,128,384]{2,1,0:T(8,128)(2,1)S(1)} collective-permute-done((bf16[2,128,384]{2,1,0:T(8,128)(2,1)S(1)}, bf16[2,128,384]{2,1,0:T(8,128)(2,1)S(1)}, u32[]{:S(2)}, u32[]{:S(2)}) %collective-permute-start.20) | collective-permute-done | bytes 196640 | tf_op jit(solution)/shard_map/ppermute | solution.py:49
  53.2 4.2 %collective-permute-done.18.refs_10_ = bf16[2,128,384]{2,1,0:T(8,128)(2,1)S(1)} collective-permute-done((bf16[2,128,384]{2,1,0:T(8,128)(2,1)S(1)}, bf16[2,128,384]{2,1,0:T(8,128)(2,1)S(1)}, u32[]{:S(2)}, u32[]{:S(2)}) %collective-permute-start.18) | collective-permute-done | bytes 196640 | tf_op jit(solution)/shard_map/ppermute | solution.py:49
  57.9 3.5 %collective-permute-done.16.refs_9_ = bf16[2,128,384]{2,1,0:T(8,128)(2,1)S(1)} collective-permute-done((bf16[2,128,384]{2,1,0:T(8,128)(2,1)}, bf16[2,128,384]{2,1,0:T(8,128)(2,1)S(1)}, u32[]{:S(2)}, u32[]{:S(2)}) %collective-permute-start.16) | collective-permute-done | bytes 196640 | tf_op jit(solution)/shard_map/ppermute | solution.py:49
  61.4 2.1 collective-permute-done.21.refs_12_.refs_8_
  63.5 1.7 collective-permute-start.27
  65.2 6.7 %collective-permute-done.33.refs_19_.refs_7_ = bf16[2,128,384]{2,1,0:T(8,128)(2,1)S(1)} collective-permute-done((bf16[2,128,384]{2,1,0:T(8,128)(2,1)S(1)}, bf16[2,128,384]{2,1,0:T(8,128)(2,1)S(1)}, u32[]{:S(2)}, u32[]{:S(2)}) %collective-permute-start.33) | collective-permute-done | bytes 196640 | tf_op jit(solution)/shard_map/ppermute | solution.py:44
  72.0 1.0 collective-permute-start.25
  73.0 3.9 %collective-permute-done.31.refs_18_.refs_6_ = bf16[2,128,384]{2,1,0:T(8,128)(2,1)S(1)} collective-permute-done((bf16[2,128,384]{2,1,0:T(8,128)(2,1)S(1)}, bf16[2,128,384]{2,1,0:T(8,128)(2,1)S(1)}, u32[]{:S(2)}, u32[]{:S(2)}) %collective-permute-start.31) | collective-permute-done | bytes 196640 | tf_op jit(solution)/shard_map/ppermute | solution.py:44
  77.6 1.3 collective-permute-start.28
  78.9 2.0 copy-done.92
  81.0 5.7 %partial_grads.3 = (f32[2,1024,256]{2,1,0:T(8,128)S(1)}, bf16[2,1024,256]{2,1,0:T(8,128)(2,1)S(1)}) custom-call(bf16[2,128,256]{2,1,0:T(8,128)(2,1)S(1)} %copy-done.17, bf16[2,128,256]{2,1,0:T(8,128)(2,1)} %collective-permute-done.1.refs_1_.refs_5_, bf16[2,128,256]{2,1,0:T(8,128)(2,1)S(1)} %copy-done.74, bf16[2,128,256]{2,1,0:T(8,128)(2,1)S(1)} %copy-done.71, ...), custom_call_target="tpu_custom_call" | custom-call | flops 3758096384 | bytes 10485760 | tf_op jit(solution)/shard_map/partial_grads/pallas_call | solution.py:273
  87.7 1.3 collective-permute-start.32
  89.8 4.9 %collective-permute-done.34.refs_19_.refs_11_ = bf16[2,128,384]{2,1,0:T(8,128)(2,1)S(1)} collective-permute-done((bf16[2,128,384]{2,1,0:T(8,128)(2,1)S(1)}, bf16[2,128,384]{2,1,0:T(8,128)(2,1)S(1)}, u32[]{:S(2)}, u32[]{:S(2)}) %collective-permute-start.34) | collective-permute-done | bytes 196640 | tf_op jit(solution)/shard_map/ppermute | solution.py:49
  94.7 4.2 %collective-permute-done.32.refs_18_.refs_10_ = bf16[2,128,384]{2,1,0:T(8,128)(2,1)S(1)} collective-permute-done((bf16[2,128,384]{2,1,0:T(8,128)(2,1)S(1)}, bf16[2,128,384]{2,1,0:T(8,128)(2,1)S(1)}, u32[]{:S(2)}, u32[]{:S(2)}) %collective-permute-start.32) | collective-permute-done | bytes 196640 | tf_op jit(solution)/shard_map/ppermute | solution.py:49
  98.9 3.7 %collective-permute-done.30.refs_17_.refs_9_ = bf16[2,128,384]{2,1,0:T(8,128)(2,1)S(1)} collective-permute-done((bf16[2,128,384]{2,1,0:T(8,128)(2,1)S(1)}, bf16[2,128,384]{2,1,0:T(8,128)(2,1)S(1)}, u32[]{:S(2)}, u32[]{:S(2)}) %collective-permute-start.30) | collective-permute-done | bytes 196640 | tf_op jit(solution)/shard_map/ppermute | solution.py:49
  102.7 2.0 copy-done.93
  104.7 5.3 %partial_grads.2 = (f32[2,1024,256]{2,1,0:T(8,128)S(1)}, bf16[2,1024,256]{2,1,0:T(8,128)(2,1)S(1)}) custom-call(bf16[2,128,256]{2,1,0:T(8,128)(2,1)S(1)} %copy-done.77, bf16[2,128,256]{2,1,0:T(8,128)(2,1)S(1)} %copy-done.86, bf16[2,128,256]{2,1,0:T(8,128)(2,1)S(1)} %copy-done.83, bf16[2,128,256]{2,1,0:T(8,128)(2,1)S(1)} %copy-done.80, ...), custom_call_target="tpu_custom_call" | custom-call | flops 3758096384 | bytes 10485760 | tf_op jit(solution)/shard_map/partial_grads/pallas_call | solution.py:273
  110.1 1.2 fusion.1
  111.3 1.2 collective-permute-start.38
  112.6 3.2 %given_half.8 = bf16[512,384]{1,0:T(8,128)(2,1)S(1)} custom-call(bf16[256,2048]{1,0:T(8,128)(2,1)S(1)} %hidden_acts.1.refs_0_, bf16[256,2048]{1,0:T(8,128)(2,1)S(1)} %collective-permute-done.39.refs_1_, bf16[256,2048]{1,0:T(8,128)(2,1)S(1)} %collective-permute-done.40.refs_2_, bf16[256,2048]{1,0:T(8,128)(2,1)S(1)} %collective-permute-done.41.refs_3_, ...), custom_call_target="tpu_custom_call" | custom-call | flops 805306368 | bytes 4063232 | tf_op jit(solution)/shard_map/given_half/pallas_call | solution.py:191
  115.8 1.6 collective-permute-start.45
  117.4 2.0 given_half.9
  119.9 3.5 %given_half.7 = bf16[512,384]{1,0:T(8,128)(2,1)} custom-call(bf16[256,2048]{1,0:T(8,128)(2,1)S(1)} %hidden_acts.1.refs_0_, bf16[256,2048]{1,0:T(8,128)(2,1)S(1)} %collective-permute-done.39.refs_1_, bf16[256,2048]{1,0:T(8,128)(2,1)S(1)} %collective-permute-done.40.refs_2_, bf16[256,2048]{1,0:T(8,128)(2,1)S(1)} %collective-permute-done.41.refs_3_, ...), custom_call_target="tpu_custom_call" | custom-call | flops 805306368 | bytes 4063232 | tf_op jit(solution)/shard_map/given_half/pallas_call | solution.py:191
  123.4 1.6 collective-permute-start.44
  125.1 3.6 %given_half.6 = bf16[512,384]{1,0:T(8,128)(2,1)} custom-call(bf16[256,2048]{1,0:T(8,128)(2,1)S(1)} %hidden_acts.1.refs_0_, bf16[256,2048]{1,0:T(8,128)(2,1)S(1)} %collective-permute-done.39.refs_1_, bf16[256,2048]{1,0:T(8,128)(2,1)S(1)} %collective-permute-done.40.refs_2_, bf16[256,2048]{1,0:T(8,128)(2,1)S(1)} %collective-permute-done.41.refs_3_, ...), custom_call_target="tpu_custom_call" | custom-call | flops 805306368 | bytes 4063232 | tf_op jit(solution)/shard_map/given_half/pallas_call | solution.py:191
  129.2 0.9 fusion
  130.1 42.6 %collective-permute-done.46.refs_12_ = bf16[512,256]{1,0:T(8,128)(2,1)S(1)} collective-permute-done((bf16[512,256]{1,0:T(8,128)(2,1)S(1)}, bf16[512,256]{1,0:T(8,128)(2,1)S(1)}, u32[]{:S(2)}, u32[]{:S(2)}) %collective-permute-start.46) | collective-permute-done | bytes 262176 | tf_op jit(solution)/shard_map/ppermute | solution.py:54
  173.6 3.3 %given_half.5 = bf16[512,384]{1,0:T(8,128)(2,1)} custom-call(bf16[256,2048]{1,0:T(8,128)(2,1)S(1)} %hidden_acts.1.refs_0_, bf16[256,2048]{1,0:T(8,128)(2,1)S(1)} %collective-permute-done.39.refs_1_, bf16[256,2048]{1,0:T(8,128)(2,1)S(1)} %collective-permute-done.40.refs_2_, bf16[256,2048]{1,0:T(8,128)(2,1)S(1)} %collective-permute-done.41.refs_3_, ...), custom_call_target="tpu_custom_call" | custom-call | flops 805306368 | bytes 4063232 | tf_op jit(solution)/shard_map/given_half/pallas_call | solution.py:191
  177.7 1.6 collective-permute-start.42
  179.3 1.2 copy-done.1
  180.5 0.9 copy-done.18
  181.4 0.9 copy-done.72
  182.3 0.9 copy-done.75
  183.2 0.9 copy-done.78
  185.9 0.9 copy-done.87
  186.9 0.9 copy-done.91
  187.9 2.9 %kept_half.5.refs_13_ = bf16[512,1792]{1,0:T(8,128)(2,1)} custom-call(bf16[256,2048]{1,0:T(8,128)(2,1)S(1)} %hidden_acts.1.refs_0_, bf16[256,2048]{1,0:T(8,128)(2,1)S(1)} %collective-permute-done.39.refs_1_, bf16[256,2048]{1,0:T(8,128)(2,1)S(1)} %collective-permute-done.40.refs_2_, bf16[256,2048]{1,0:T(8,128)(2,1)S(1)} %copy-done.1, ...), custom_call_target="tpu_custom_call" | custom-call | flops 536870912 | bytes 3407872 | tf_op jit(solution)/shard_map/kept_half/pallas_call | solution.py:225
  190.8 3.7 %kept_half.6.refs_13_ = bf16[512,1792]{1,0:T(8,128)(2,1)} custom-call(bf16[256,2048]{1,0:T(8,128)(2,1)S(1)} %hidden_acts.1.refs_0_, bf16[256,2048]{1,0:T(8,128)(2,1)S(1)} %collective-permute-done.39.refs_1_, bf16[256,2048]{1,0:T(8,128)(2,1)S(1)} %collective-permute-done.40.refs_2_, bf16[256,2048]{1,0:T(8,128)(2,1)S(1)} %copy-done.2, ...), custom_call_target="tpu_custom_call", output_to_operand_aliasing={{}: (13, {})} | custom-call | flops 805306368 | bytes 4063232 | tf_op jit(solution)/shard_map/kept_half/pallas_call | solution.py:225
  194.7 4.7 %kept_half.7.refs_13_ = bf16[512,1792]{1,0:T(8,128)(2,1)} custom-call(bf16[256,2048]{1,0:T(8,128)(2,1)S(1)} %hidden_acts.1.refs_0_, bf16[256,2048]{1,0:T(8,128)(2,1)S(1)} %collective-permute-done.39.refs_1_, bf16[256,2048]{1,0:T(8,128)(2,1)S(1)} %collective-permute-done.40.refs_2_, bf16[256,2048]{1,0:T(8,128)(2,1)S(1)} %copy-done.2, ...), custom_call_target="tpu_custom_call", output_to_operand_aliasing={{}: (13, {})} | custom-call | flops 805306368 | bytes 4063232 | tf_op jit(solution)/shard_map/kept_half/pallas_call | solution.py:225
  199.5 4.7 %kept_half.8.refs_13_ = bf16[512,1792]{1,0:T(8,128)(2,1)} custom-call(bf16[256,2048]{1,0:T(8,128)(2,1)S(1)} %hidden_acts.1.refs_0_, bf16[256,2048]{1,0:T(8,128)(2,1)S(1)} %collective-permute-done.39.refs_1_, bf16[256,2048]{1,0:T(8,128)(2,1)S(1)} %collective-permute-done.40.refs_2_, bf16[256,2048]{1,0:T(8,128)(2,1)S(1)} %copy-done.2, ...), custom_call_target="tpu_custom_call", output_to_operand_aliasing={{}: (13, {})} | custom-call | flops 805306368 | bytes 4063232 | tf_op jit(solution)/shard_map/kept_half/pallas_call | solution.py:225
  204.3 4.4 %kept_half.9 = bf16[512,1792]{1,0:T(8,128)(2,1)} custom-call(bf16[256,2048]{1,0:T(8,128)(2,1)S(1)} %hidden_acts.1.refs_0_, bf16[256,2048]{1,0:T(8,128)(2,1)S(1)} %collective-permute-done.39.refs_1_, bf16[256,2048]{1,0:T(8,128)(2,1)S(1)} %collective-permute-done.40.refs_2_, bf16[256,2048]{1,0:T(8,128)(2,1)S(1)} %copy-done.2, ...), custom_call_target="tpu_custom_call", output_to_operand_aliasing={{}: (13, {})} | custom-call | flops 805306368 | bytes 4063232 | tf_op jit(solution)/shard_map/kept_half/pallas_call | solution.py:225
  208.8 2.7 %store_grads.2.refs_0_ = bf16[2,1024,512]{2,1,0:T(8,128)(2,1)} custom-call(s32[2,8,1]{2,1,0:T(8,128)S(1)} %copy.12.route_ref, s32[1]{0:T(128)} %bitcast.25.group_ref, bf16[2,1024,512]{2,1,0:T(8,128)(2,1)S(1)} %bitcast.52, f32[2,1024,256]{2,1,0:T(8,128)S(1)} %copy-done.6, bf16[2,1024,256]{2,1,0:T(8,128)(2,1)S(1)} %copy-done.10, ...), custom_call_target="tpu_custom_call" | custom-call | flops 4194304 | bytes 6291456 | tf_op jit(solution)/shard_map/store_grads/pallas_call | solution.py:361
  211.6 2.1 store_grads.3
  (248 shorter events, 20.2 us)
Async XLA Ops:
  2.5 5.8 %collective-permute-start.5 = (bf16[2,128,256]{2,1,0:T(8,128)(2,1)S(1)}, bf16[2,128,256]{2,1,0:T(8,128)(2,1)S(1)}, u32[]{:S(2)}, u32[]{:S(2)}) collective-permute-start(bf16[2,128,256]{2,1,0:T(8,128)(2,1)S(1)} %get-tuple-element.82), channel_id=1, source_target_pairs={{0,3},{1,2},{2,1},{3,0},{4,7},{5,6},{6,5},{7,4},{8,11},{9,10},{10,... | collective-permute-start | bytes 393224 | tf_op jit(solution)/shard_map/ppermute | solution.py:44
  3.4 8.8 %collective-permute-start.3 = (bf16[2,128,256]{2,1,0:T(8,128)(2,1)S(1)}, bf16[2,128,256]{2,1,0:T(8,128)(2,1)S(1)}, u32[]{:S(2)}, u32[]{:S(2)}) collective-permute-start(bf16[2,128,256]{2,1,0:T(8,128)(2,1)S(1)} %get-tuple-element.83), channel_id=1, source_target_pairs={{0,2},{1,3},{2,0},{3,1},{4,6},{5,7},{6,4},{7,5},{8,10},{9,11},{10,... | collective-permute-start | bytes 393224 | tf_op jit(solution)/shard_map/ppermute | solution.py:44
  4.0 8.7 %collective-permute-start.1 = (bf16[2,128,256]{2,1,0:T(8,128)(2,1)}, bf16[2,128,256]{2,1,0:T(8,128)(2,1)}, u32[]{:S(2)}, u32[]{:S(2)}) collective-permute-start(bf16[2,128,256]{2,1,0:T(8,128)(2,1)} %get-tuple-element.84), channel_id=1, source_target_pairs={{0,1},{1,0},{2,3},{3,2},{4,5},{5,4},{6,7},{7,6},{8,9},{9,8},{10,11... | collective-permute-start | bytes 393224 | tf_op jit(solution)/shard_map/ppermute | solution.py:44
  8.2 12.1 %collective-permute-start.12 = (bf16[2,128,384]{2,1,0:T(8,128)(2,1)S(1)}, bf16[2,128,384]{2,1,0:T(8,128)(2,1)S(1)}, u32[]{:S(2)}, u32[]{:S(2)}) collective-permute-start(bf16[2,128,384]{2,1,0:T(8,128)(2,1)S(1)} %get-tuple-element.39), channel_id=1, source_target_pairs={{0,3},{1,2},{2,1},{3,0},{4,7},{5,6},{6,5},{7,4},{8,11},{9,10},{10,... | collective-permute-start | bytes 589832 | tf_op jit(solution)/shard_map/ppermute | solution.py:44
  9.5 6.3 %collective-permute-start = (bf16[2,128,256]{2,1,0:T(8,128)(2,1)S(1)}, bf16[2,128,256]{2,1,0:T(8,128)(2,1)S(1)}, u32[]{:S(2)}, u32[]{:S(2)}) collective-permute-start(bf16[2,128,256]{2,1,0:T(8,128)(2,1)S(1)} %get-tuple-element.85.refs_0_.refs_4_), channel_id=1, source_target_pairs={{4,0},{5,1},{6,2},{7,3},{0,4},{1,5},{2,6},{3,7},{12,8},{13,9},{14,... | collective-permute-start | bytes 393224 | tf_op jit(solution)/shard_map/ppermute | solution.py:49
  11.0 7.6 %collective-permute-start.6 = (bf16[2,128,256]{2,1,0:T(8,128)(2,1)S(1)}, bf16[2,128,256]{2,1,0:T(8,128)(2,1)S(1)}, u32[]{:S(2)}, u32[]{:S(2)}) collective-permute-start(bf16[2,128,256]{2,1,0:T(8,128)(2,1)S(1)} %collective-permute-done.5.refs_3_.refs_7_), channel_id=1, source_target_pairs={{4,0},{5,1},{6,2},{7,3},{0,4},{1,5},{2,6},{3,7},{12,8},{13,9},{14,... | collective-permute-start | bytes 393224 | tf_op jit(solution)/shard_map/ppermute | solution.py:49
  12.1 9.8 %collective-permute-start.10 = (bf16[2,128,384]{2,1,0:T(8,128)(2,1)S(1)}, bf16[2,128,384]{2,1,0:T(8,128)(2,1)S(1)}, u32[]{:S(2)}, u32[]{:S(2)}) collective-permute-start(bf16[2,128,384]{2,1,0:T(8,128)(2,1)S(1)} %get-tuple-element.37), channel_id=1, source_target_pairs={{0,2},{1,3},{2,0},{3,1},{4,6},{5,7},{6,4},{7,5},{8,10},{9,11},{10,... | collective-permute-start | bytes 589832 | tf_op jit(solution)/shard_map/ppermute | solution.py:44
  12.7 15.5 %collective-permute-start.8 = (bf16[2,128,384]{2,1,0:T(8,128)(2,1)S(1)}, bf16[2,128,384]{2,1,0:T(8,128)(2,1)}, u32[]{:S(2)}, u32[]{:S(2)}) collective-permute-start(bf16[2,128,384]{2,1,0:T(8,128)(2,1)S(1)} %get-tuple-element.35), channel_id=1, source_target_pairs={{0,1},{1,0},{2,3},{3,2},{4,5},{5,4},{6,7},{7,6},{8,9},{9,8},{10,11... | collective-permute-start | bytes 589832 | tf_op jit(solution)/shard_map/ppermute | solution.py:44
  16.4 5.5 %collective-permute-start.4 = (bf16[2,128,256]{2,1,0:T(8,128)(2,1)S(1)}, bf16[2,128,256]{2,1,0:T(8,128)(2,1)S(1)}, u32[]{:S(2)}, u32[]{:S(2)}) collective-permute-start(bf16[2,128,256]{2,1,0:T(8,128)(2,1)S(1)} %collective-permute-done.3.refs_2_.refs_6_), channel_id=1, source_target_pairs={{4,0},{5,1},{6,2},{7,3},{0,4},{1,5},{2,6},{3,7},{12,8},{13,9},{14,... | collective-permute-start | bytes 393224 | tf_op jit(solution)/shard_map/ppermute | solution.py:49
  19.2 6.6 %collective-permute-start.2 = (bf16[2,128,256]{2,1,0:T(8,128)(2,1)}, bf16[2,128,256]{2,1,0:T(8,128)(2,1)S(1)}, u32[]{:S(2)}, u32[]{:S(2)}) collective-permute-start(bf16[2,128,256]{2,1,0:T(8,128)(2,1)} %collective-permute-done.1.refs_1_.refs_5_), channel_id=1, source_target_pairs={{4,0},{5,1},{6,2},{7,3},{0,4},{1,5},{2,6},{3,7},{12,8},{13,9},{14,... | collective-permute-start | bytes 393224 | tf_op jit(solution)/shard_map/ppermute | solution.py:49
  20.3 9.6 %collective-permute-start.7 = (bf16[2,128,384]{2,1,0:T(8,128)(2,1)S(1)}, bf16[2,128,384]{2,1,0:T(8,128)(2,1)S(1)}, u32[]{:S(2)}, u32[]{:S(2)}) collective-permute-start(bf16[2,128,384]{2,1,0:T(8,128)(2,1)S(1)} %get-tuple-element.34.refs_4_), channel_id=1, source_target_pairs={{4,0},{5,1},{6,2},{7,3},{0,4},{1,5},{2,6},{3,7},{12,8},{13,9},{14,... | collective-permute-start | bytes 589832 | tf_op jit(solution)/shard_map/ppermute | solution.py:49
  21.9 8.6 %collective-permute-start.19 = (bf16[2,128,384]{2,1,0:T(8,128)(2,1)S(1)}, bf16[2,128,384]{2,1,0:T(8,128)(2,1)S(1)}, u32[]{:S(2)}, u32[]{:S(2)}) collective-permute-start(bf16[2,128,384]{2,1,0:T(8,128)(2,1)S(1)} %get-tuple-element.46), channel_id=1, source_target_pairs={{0,3},{1,2},{2,1},{3,0},{4,7},{5,6},{6,5},{7,4},{8,11},{9,10},{10,... | collective-permute-start | bytes 589832 | tf_op jit(solution)/shard_map/ppermute | solution.py:44
  22.6 9.3 %collective-permute-start.17 = (bf16[2,128,384]{2,1,0:T(8,128)(2,1)S(1)}, bf16[2,128,384]{2,1,0:T(8,128)(2,1)S(1)}, u32[]{:S(2)}, u32[]{:S(2)}) collective-permute-start(bf16[2,128,384]{2,1,0:T(8,128)(2,1)S(1)} %get-tuple-element.44), channel_id=1, source_target_pairs={{0,2},{1,3},{2,0},{3,1},{4,6},{5,7},{6,4},{7,5},{8,10},{9,11},{10,... | collective-permute-start | bytes 589832 | tf_op jit(solution)/shard_map/ppermute | solution.py:44
  26.5 7.8 %collective-permute-start.13 = (bf16[2,128,384]{2,1,0:T(8,128)(2,1)S(1)}, bf16[2,128,384]{2,1,0:T(8,128)(2,1)S(1)}, u32[]{:S(2)}, u32[]{:S(2)}) collective-permute-start(bf16[2,128,384]{2,1,0:T(8,128)(2,1)S(1)} %collective-permute-done.12.refs_7_), channel_id=1, source_target_pairs={{4,0},{5,1},{6,2},{7,3},{0,4},{1,5},{2,6},{3,7},{12,8},{13,9},{14,... | collective-permute-start | bytes 589832 | tf_op jit(solution)/shard_map/ppermute | solution.py:49
  28.2 10.4 %collective-permute-start.11 = (bf16[2,128,384]{2,1,0:T(8,128)(2,1)S(1)}, bf16[2,128,384]{2,1,0:T(8,128)(2,1)S(1)}, u32[]{:S(2)}, u32[]{:S(2)}) collective-permute-start(bf16[2,128,384]{2,1,0:T(8,128)(2,1)S(1)} %collective-permute-done.10.refs_6_), channel_id=1, source_target_pairs={{4,0},{5,1},{6,2},{7,3},{0,4},{1,5},{2,6},{3,7},{12,8},{13,9},{14,... | collective-permute-start | bytes 589832 | tf_op jit(solution)/shard_map/ppermute | solution.py:49
  30.6 10.7 %collective-permute-start.15 = (bf16[2,128,384]{2,1,0:T(8,128)(2,1)}, bf16[2,128,384]{2,1,0:T(8,128)(2,1)}, u32[]{:S(2)}, u32[]{:S(2)}) collective-permute-start(bf16[2,128,384]{2,1,0:T(8,128)(2,1)} %get-tuple-element.42), channel_id=1, source_target_pairs={{0,1},{1,0},{2,3},{3,2},{4,5},{5,4},{6,7},{7,6},{8,9},{9,8},{10,11... | collective-permute-start | bytes 589832 | tf_op jit(solution)/shard_map/ppermute | solution.py:44
  30.6 12.3 %collective-permute-start.9 = (bf16[2,128,384]{2,1,0:T(8,128)(2,1)}, bf16[2,128,384]{2,1,0:T(8,128)(2,1)}, u32[]{:S(2)}, u32[]{:S(2)}) collective-permute-start(bf16[2,128,384]{2,1,0:T(8,128)(2,1)} %collective-permute-done.8.refs_5_), channel_id=1, source_target_pairs={{4,0},{5,1},{6,2},{7,3},{0,4},{1,5},{2,6},{3,7},{12,8},{13,9},{14,... | collective-permute-start | bytes 589832 | tf_op jit(solution)/shard_map/ppermute | solution.py:49
  31.9 13.5 %collective-permute-start.14 = (bf16[2,128,384]{2,1,0:T(8,128)(2,1)}, bf16[2,128,384]{2,1,0:T(8,128)(2,1)}, u32[]{:S(2)}, u32[]{:S(2)}) collective-permute-start(bf16[2,128,384]{2,1,0:T(8,128)(2,1)} %get-tuple-element.41.refs_8_.refs_4_), channel_id=1, source_target_pairs={{4,0},{5,1},{6,2},{7,3},{0,4},{1,5},{2,6},{3,7},{12,8},{13,9},{14,... | collective-permute-start | bytes 589832 | tf_op jit(solution)/shard_map/ppermute | solution.py:49
  35.0 11.9 %collective-permute-start.26 = (bf16[2,128,384]{2,1,0:T(8,128)(2,1)}, bf16[2,128,384]{2,1,0:T(8,128)(2,1)}, u32[]{:S(2)}, u32[]{:S(2)}) collective-permute-start(bf16[2,128,384]{2,1,0:T(8,128)(2,1)} %get-tuple-element.53), channel_id=1, source_target_pairs={{0,3},{1,2},{2,1},{3,0},{4,7},{5,6},{6,5},{7,4},{8,11},{9,10},{10,... | collective-permute-start | bytes 589832 | tf_op jit(solution)/shard_map/ppermute | solution.py:44
  39.2 8.2 %collective-permute-start.24 = (bf16[2,128,384]{2,1,0:T(8,128)(2,1)}, bf16[2,128,384]{2,1,0:T(8,128)(2,1)}, u32[]{:S(2)}, u32[]{:S(2)}) collective-permute-start(bf16[2,128,384]{2,1,0:T(8,128)(2,1)} %get-tuple-element.51), channel_id=1, source_target_pairs={{0,2},{1,3},{2,0},{3,1},{4,6},{5,7},{6,4},{7,5},{8,10},{9,11},{10,... | collective-permute-start | bytes 589832 | tf_op jit(solution)/shard_map/ppermute | solution.py:44
  39.9 39.0 %copy-start.14 = (bf16[2,128,384]{2,1,0:T(8,128)(2,1)S(1)}, bf16[2,128,384]{2,1,0:T(8,128)(2,1)}, u32[]{:S(2)}) copy-start(bf16[2,128,384]{2,1,0:T(8,128)(2,1)} %copy-done.13) | copy-start | bytes 589828
  39.9 39.0 %copy-start.17 = (bf16[2,128,256]{2,1,0:T(8,128)(2,1)S(1)}, bf16[2,128,256]{2,1,0:T(8,128)(2,1)}, u32[]{:S(2)}) copy-start(bf16[2,128,256]{2,1,0:T(8,128)(2,1)} %copy-done.16) | copy-start | bytes 393220
  39.9 39.0 %copy-start.20 = (bf16[2,128,384]{2,1,0:T(8,128)(2,1)S(1)}, bf16[2,128,384]{2,1,0:T(8,128)(2,1)}, u32[]{:S(2)}) copy-start(bf16[2,128,384]{2,1,0:T(8,128)(2,1)} %copy-done.19) | copy-start | bytes 589828
  41.3 48.5 %collective-permute-start.40 = (bf16[256,2048]{1,0:T(8,128)(2,1)S(1)}, bf16[256,2048]{1,0:T(8,128)(2,1)S(1)}, u32[]{:S(2)}, u32[]{:S(2)}) collective-permute-start(bf16[256,2048]{1,0:T(8,128)(2,1)S(1)} %hidden_acts.1.refs_0_), channel_id=1, source_target_pairs={{0,2},{1,3},{2,0},{3,1},{4,6},{5,7},{6,4},{7,5},{8,10},{9,11},{10,... | collective-permute-start | bytes 3145736 | tf_op jit(solution)/shard_map/ppermute | solution.py:44
  42.9 6.0 %collective-permute-start.22 = (bf16[2,128,384]{2,1,0:T(8,128)(2,1)S(1)}, bf16[2,128,384]{2,1,0:T(8,128)(2,1)S(1)}, u32[]{:S(2)}, u32[]{:S(2)}) collective-permute-start(bf16[2,128,384]{2,1,0:T(8,128)(2,1)S(1)} %copy-done.97), channel_id=1, source_target_pairs={{0,1},{1,0},{2,3},{3,2},{4,5},{5,4},{6,7},{7,6},{8,9},{9,8},{10,11... | collective-permute-start | bytes 589832 | tf_op jit(solution)/shard_map/ppermute | solution.py:44
  45.4 7.8 %collective-permute-start.20 = (bf16[2,128,384]{2,1,0:T(8,128)(2,1)S(1)}, bf16[2,128,384]{2,1,0:T(8,128)(2,1)S(1)}, u32[]{:S(2)}, u32[]{:S(2)}) collective-permute-start(bf16[2,128,384]{2,1,0:T(8,128)(2,1)S(1)} %copy-done.26), channel_id=1, source_target_pairs={{4,0},{5,1},{6,2},{7,3},{0,4},{1,5},{2,6},{3,7},{12,8},{13,9},{14,... | collective-permute-start | bytes 589832 | tf_op jit(solution)/shard_map/ppermute | solution.py:49
  46.9 10.5 %collective-permute-start.18 = (bf16[2,128,384]{2,1,0:T(8,128)(2,1)S(1)}, bf16[2,128,384]{2,1,0:T(8,128)(2,1)S(1)}, u32[]{:S(2)}, u32[]{:S(2)}) collective-permute-start(bf16[2,128,384]{2,1,0:T(8,128)(2,1)S(1)} %copy-done.32), channel_id=1, source_target_pairs={{4,0},{5,1},{6,2},{7,3},{0,4},{1,5},{2,6},{3,7},{12,8},{13,9},{14,... | collective-permute-start | bytes 589832 | tf_op jit(solution)/shard_map/ppermute | solution.py:49
  47.4 14.0 %collective-permute-start.16 = (bf16[2,128,384]{2,1,0:T(8,128)(2,1)}, bf16[2,128,384]{2,1,0:T(8,128)(2,1)S(1)}, u32[]{:S(2)}, u32[]{:S(2)}) collective-permute-start(bf16[2,128,384]{2,1,0:T(8,128)(2,1)} %collective-permute-done.15.refs_9_.refs_5_), channel_id=1, source_target_pairs={{4,0},{5,1},{6,2},{7,3},{0,4},{1,5},{2,6},{3,7},{12,8},{13,9},{14,... | collective-permute-start | bytes 589832 | tf_op jit(solution)/shard_map/ppermute | solution.py:49
  48.9 76.1 %copy-start.40 = (bf16[2,128,384]{2,1,0:T(8,128)(2,1)}, bf16[2,128,384]{2,1,0:T(8,128)(2,1)S(1)}, u32[]{:S(2)}) copy-start(bf16[2,128,384]{2,1,0:T(8,128)(2,1)S(1)} %collective-permute-done.22.refs_13_.refs_5_) | copy-start | bytes 589828
  48.9 14.6 %collective-permute-start.21 = (bf16[2,128,384]{2,1,0:T(8,128)(2,1)S(1)}, bf16[2,128,384]{2,1,0:T(8,128)(2,1)S(1)}, u32[]{:S(2)}, u32[]{:S(2)}) collective-permute-start(bf16[2,128,384]{2,1,0:T(8,128)(2,1)S(1)} %get-tuple-element.48.refs_12_.refs_4_), channel_id=1, source_target_pairs={{4,0},{5,1},{6,2},{7,3},{0,4},{1,5},{2,6},{3,7},{12,8},{13,9},{14,... | collective-permute-start | bytes 589832 | tf_op jit(solution)/shard_map/ppermute | solution.py:49
  53.2 66.7 %copy-start.42 = (bf16[2,128,384]{2,1,0:T(8,128)(2,1)}, bf16[2,128,384]{2,1,0:T(8,128)(2,1)S(1)}, u32[]{:S(2)}) copy-start(bf16[2,128,384]{2,1,0:T(8,128)(2,1)S(1)} %collective-permute-done.20.refs_11_) | copy-start | bytes 589828
  53.2 18.8 %collective-permute-start.33 = (bf16[2,128,384]{2,1,0:T(8,128)(2,1)S(1)}, bf16[2,128,384]{2,1,0:T(8,128)(2,1)S(1)}, u32[]{:S(2)}, u32[]{:S(2)}) collective-permute-start(bf16[2,128,384]{2,1,0:T(8,128)(2,1)S(1)} %copy-done.96), channel_id=1, source_target_pairs={{0,3},{1,2},{2,1},{3,0},{4,7},{5,6},{6,5},{7,4},{8,11},{9,10},{10,... | collective-permute-start | bytes 589832 | tf_op jit(solution)/shard_map/ppermute | solution.py:44
  57.4 62.5 %copy-start.46 = (bf16[2,128,384]{2,1,0:T(8,128)(2,1)}, bf16[2,128,384]{2,1,0:T(8,128)(2,1)S(1)}, u32[]{:S(2)}) copy-start(bf16[2,128,384]{2,1,0:T(8,128)(2,1)S(1)} %collective-permute-done.18.refs_10_) | copy-start | bytes 589828
  57.4 19.5 %collective-permute-start.31 = (bf16[2,128,384]{2,1,0:T(8,128)(2,1)S(1)}, bf16[2,128,384]{2,1,0:T(8,128)(2,1)S(1)}, u32[]{:S(2)}, u32[]{:S(2)}) collective-permute-start(bf16[2,128,384]{2,1,0:T(8,128)(2,1)S(1)} %copy-done.95), channel_id=1, source_target_pairs={{0,2},{1,3},{2,0},{3,1},{4,6},{5,7},{6,4},{7,5},{8,10},{9,11},{10,... | collective-permute-start | bytes 589832 | tf_op jit(solution)/shard_map/ppermute | solution.py:44
  61.4 58.5 %copy-start.52 = (bf16[2,128,384]{2,1,0:T(8,128)(2,1)}, bf16[2,128,384]{2,1,0:T(8,128)(2,1)S(1)}, u32[]{:S(2)}) copy-start(bf16[2,128,384]{2,1,0:T(8,128)(2,1)S(1)} %collective-permute-done.16.refs_9_) | copy-start | bytes 589828
  61.4 16.2 %collective-permute-start.29 = (bf16[2,128,384]{2,1,0:T(8,128)(2,1)S(1)}, bf16[2,128,384]{2,1,0:T(8,128)(2,1)S(1)}, u32[]{:S(2)}, u32[]{:S(2)}) collective-permute-start(bf16[2,128,384]{2,1,0:T(8,128)(2,1)S(1)} %copy-done.94), channel_id=1, source_target_pairs={{0,1},{1,0},{2,3},{3,2},{4,5},{5,4},{6,7},{7,6},{8,9},{9,8},{10,11... | collective-permute-start | bytes 589832 | tf_op jit(solution)/shard_map/ppermute | solution.py:44
  63.5 61.5 %copy-start.50 = (bf16[2,128,384]{2,1,0:T(8,128)(2,1)}, bf16[2,128,384]{2,1,0:T(8,128)(2,1)S(1)}, u32[]{:S(2)}) copy-start(bf16[2,128,384]{2,1,0:T(8,128)(2,1)S(1)} %collective-permute-done.21.refs_12_.refs_8_) | copy-start | bytes 589828
  63.5 23.3 %collective-permute-start.27 = (bf16[2,128,384]{2,1,0:T(8,128)(2,1)}, bf16[2,128,384]{2,1,0:T(8,128)(2,1)S(1)}, u32[]{:S(2)}, u32[]{:S(2)}) collective-permute-start(bf16[2,128,384]{2,1,0:T(8,128)(2,1)} %collective-permute-done.26.refs_15_.refs_7_), channel_id=1, source_target_pairs={{4,0},{5,1},{6,2},{7,3},{0,4},{1,5},{2,6},{3,7},{12,8},{13,9},{14,... | collective-permute-start | bytes 589832 | tf_op jit(solution)/shard_map/ppermute | solution.py:49
  72.0 101.5 %copy-start.44 = (bf16[2,128,384]{2,1,0:T(8,128)(2,1)}, bf16[2,128,384]{2,1,0:T(8,128)(2,1)S(1)}, u32[]{:S(2)}) copy-start(bf16[2,128,384]{2,1,0:T(8,128)(2,1)S(1)} %collective-permute-done.33.refs_19_.refs_7_) | copy-start | bytes 589828
  72.0 14.9 %collective-permute-start.25 = (bf16[2,128,384]{2,1,0:T(8,128)(2,1)}, bf16[2,128,384]{2,1,0:T(8,128)(2,1)S(1)}, u32[]{:S(2)}, u32[]{:S(2)}) collective-permute-start(bf16[2,128,384]{2,1,0:T(8,128)(2,1)} %collective-permute-done.24.refs_14_.refs_6_), channel_id=1, source_target_pairs={{4,0},{5,1},{6,2},{7,3},{0,4},{1,5},{2,6},{3,7},{12,8},{13,9},{14,... | collective-permute-start | bytes 589832 | tf_op jit(solution)/shard_map/ppermute | solution.py:49
  76.9 96.7 %copy-start.48 = (bf16[2,128,384]{2,1,0:T(8,128)(2,1)}, bf16[2,128,384]{2,1,0:T(8,128)(2,1)S(1)}, u32[]{:S(2)}) copy-start(bf16[2,128,384]{2,1,0:T(8,128)(2,1)S(1)} %collective-permute-done.31.refs_18_.refs_6_) | copy-start | bytes 589828
  76.9 10.8 %collective-permute-start.23 = (bf16[2,128,384]{2,1,0:T(8,128)(2,1)S(1)}, bf16[2,128,384]{2,1,0:T(8,128)(2,1)S(1)}, u32[]{:S(2)}, u32[]{:S(2)}) collective-permute-start(bf16[2,128,384]{2,1,0:T(8,128)(2,1)S(1)} %collective-permute-done.22.refs_13_.refs_5_), channel_id=1, source_target_pairs={{4,0},{5,1},{6,2},{7,3},{0,4},{1,5},{2,6},{3,7},{12,8},{13,9},{14,... | collective-permute-start | bytes 589832 | tf_op jit(solution)/shard_map/ppermute | solution.py:49
  77.6 95.9 %copy-start.54 = (bf16[2,128,384]{2,1,0:T(8,128)(2,1)}, bf16[2,128,384]{2,1,0:T(8,128)(2,1)S(1)}, u32[]{:S(2)}) copy-start(bf16[2,128,384]{2,1,0:T(8,128)(2,1)S(1)} %collective-permute-done.29.refs_17_.refs_5_) | copy-start | bytes 589828
  77.6 11.4 %collective-permute-start.28 = (bf16[2,128,384]{2,1,0:T(8,128)(2,1)S(1)}, bf16[2,128,384]{2,1,0:T(8,128)(2,1)S(1)}, u32[]{:S(2)}, u32[]{:S(2)}) collective-permute-start(bf16[2,128,384]{2,1,0:T(8,128)(2,1)S(1)} %get-tuple-element.55.refs_16_.refs_4_), channel_id=1, source_target_pairs={{4,0},{5,1},{6,2},{7,3},{0,4},{1,5},{2,6},{3,7},{12,8},{13,9},{14,... | collective-permute-start | bytes 589832 | tf_op jit(solution)/shard_map/ppermute | solution.py:49
  86.8 23.3 %collective-permute-start.37 = (bf16[2,1024,256]{2,1,0:T(8,128)(2,1)S(1)}, bf16[2,1024,256]{2,1,0:T(8,128)(2,1)S(1)}, u32[]{:S(2)}, u32[]{:S(2)}) collective-permute-start(bf16[2,1024,256]{2,1,0:T(8,128)(2,1)S(1)} %get-tuple-element.65), channel_id=1, source_target_pairs={{0,1},{1,0},{2,3},{3,2},{4,5},{5,4},{6,7},{7,6},{8,9},{9,8},{10,11... | collective-permute-start | bytes 3145736 | tf_op jit(solution)/shard_map/ppermute | solution.py:44
  86.9 7.8 %collective-permute-start.34 = (bf16[2,128,384]{2,1,0:T(8,128)(2,1)S(1)}, bf16[2,128,384]{2,1,0:T(8,128)(2,1)S(1)}, u32[]{:S(2)}, u32[]{:S(2)}) collective-permute-start(bf16[2,128,384]{2,1,0:T(8,128)(2,1)S(1)} %collective-permute-done.33.refs_19_.refs_7_), channel_id=1, source_target_pairs={{4,0},{5,1},{6,2},{7,3},{0,4},{1,5},{2,6},{3,7},{12,8},{13,9},{14,... | collective-permute-start | bytes 589832 | tf_op jit(solution)/shard_map/ppermute | solution.py:49
  87.7 11.2 %collective-permute-start.32 = (bf16[2,128,384]{2,1,0:T(8,128)(2,1)S(1)}, bf16[2,128,384]{2,1,0:T(8,128)(2,1)S(1)}, u32[]{:S(2)}, u32[]{:S(2)}) collective-permute-start(bf16[2,128,384]{2,1,0:T(8,128)(2,1)S(1)} %collective-permute-done.31.refs_18_.refs_6_), channel_id=1, source_target_pairs={{4,0},{5,1},{6,2},{7,3},{0,4},{1,5},{2,6},{3,7},{12,8},{13,9},{14,... | collective-permute-start | bytes 589832 | tf_op jit(solution)/shard_map/ppermute | solution.py:49
  89.0 84.6 %copy-start.60 = (bf16[2,128,384]{2,1,0:T(8,128)(2,1)}, bf16[2,128,384]{2,1,0:T(8,128)(2,1)S(1)}, u32[]{:S(2)}) copy-start(bf16[2,128,384]{2,1,0:T(8,128)(2,1)S(1)} %collective-permute-done.28.refs_16_.refs_8_) | copy-start | bytes 589828
  89.0 13.6 %collective-permute-start.30 = (bf16[2,128,384]{2,1,0:T(8,128)(2,1)S(1)}, bf16[2,128,384]{2,1,0:T(8,128)(2,1)S(1)}, u32[]{:S(2)}, u32[]{:S(2)}) collective-permute-start(bf16[2,128,384]{2,1,0:T(8,128)(2,1)S(1)} %collective-permute-done.29.refs_17_.refs_5_), channel_id=1, source_target_pairs={{4,0},{5,1},{6,2},{7,3},{0,4},{1,5},{2,6},{3,7},{12,8},{13,9},{14,... | collective-permute-start | bytes 589832 | tf_op jit(solution)/shard_map/ppermute | solution.py:49
  89.8 22.8 %collective-permute-start.39 = (bf16[256,2048]{1,0:T(8,128)(2,1)S(1)}, bf16[256,2048]{1,0:T(8,128)(2,1)S(1)}, u32[]{:S(2)}, u32[]{:S(2)}) collective-permute-start(bf16[256,2048]{1,0:T(8,128)(2,1)S(1)} %hidden_acts.1.refs_0_), channel_id=1, source_target_pairs={{0,1},{1,0},{2,3},{3,2},{4,5},{5,4},{6,7},{7,6},{8,9},{9,8},{10,11... | collective-permute-start | bytes 3145736 | tf_op jit(solution)/shard_map/ppermute | solution.py:44
  94.7 78.9 %copy-start.64 = (bf16[2,128,384]{2,1,0:T(8,128)(2,1)}, bf16[2,128,384]{2,1,0:T(8,128)(2,1)S(1)}, u32[]{:S(2)}) copy-start(bf16[2,128,384]{2,1,0:T(8,128)(2,1)S(1)} %collective-permute-done.34.refs_19_.refs_11_) | copy-start | bytes 589828
  94.7 17.9 %collective-permute-start.41 = (bf16[256,2048]{1,0:T(8,128)(2,1)S(1)}, bf16[256,2048]{1,0:T(8,128)(2,1)S(1)}, u32[]{:S(2)}, u32[]{:S(2)}) collective-permute-start(bf16[256,2048]{1,0:T(8,128)(2,1)S(1)} %collective-permute-done.40.refs_2_), channel_id=1, source_target_pairs={{0,1},{1,0},{2,3},{3,2},{4,5},{5,4},{6,7},{7,6},{8,9},{9,8},{10,11... | collective-permute-start | bytes 3145736 | tf_op jit(solution)/shard_map/ppermute | solution.py:44
  98.9 74.7 %copy-start.66 = (bf16[2,128,384]{2,1,0:T(8,128)(2,1)}, bf16[2,128,384]{2,1,0:T(8,128)(2,1)S(1)}, u32[]{:S(2)}) copy-start(bf16[2,128,384]{2,1,0:T(8,128)(2,1)S(1)} %collective-permute-done.32.refs_18_.refs_10_) | copy-start | bytes 589828
  104.7 68.9 %copy-start.68 = (bf16[2,128,384]{2,1,0:T(8,128)(2,1)}, bf16[2,128,384]{2,1,0:T(8,128)(2,1)S(1)}, u32[]{:S(2)}) copy-start(bf16[2,128,384]{2,1,0:T(8,128)(2,1)S(1)} %collective-permute-done.30.refs_17_.refs_9_) | copy-start | bytes 589828
  110.0 18.6 %collective-permute-start.35 = (bf16[2,1024,256]{2,1,0:T(8,128)(2,1)S(1)}, bf16[2,1024,256]{2,1,0:T(8,128)(2,1)S(1)}, u32[]{:S(2)}, u32[]{:S(2)}) collective-permute-start(bf16[2,1024,256]{2,1,0:T(8,128)(2,1)S(1)} %get-tuple-element.63), channel_id=1, source_target_pairs={{0,1},{1,0},{2,3},{3,2},{4,5},{5,4},{6,7},{7,6},{8,9},{9,8},{10,11... | collective-permute-start | bytes 3145736 | tf_op jit(solution)/shard_map/ppermute | solution.py:44
  111.3 97.5 %collective-permute-start.38 = (bf16[1024,256]{1,0:T(8,128)(2,1)}, bf16[1024,256]{1,0:T(8,128)(2,1)}, u32[]{:S(2)}, u32[]{:S(2)}) collective-permute-start(bf16[1024,256]{1,0:T(8,128)(2,1)} %fusion.1), channel_id=1, source_target_pairs={{0,2},{1,3},{2,0},{3,1},{4,6},{5,7},{6,4},{7,5},{8,10},{9,11},{10,... | collective-permute-start | bytes 1572872 | tf_op jit(solution)/shard_map/ppermute | solution.py:44
  112.6 61.0 %copy-start = (bf16[256,2048]{1,0:T(8,128)(2,1)}, bf16[256,2048]{1,0:T(8,128)(2,1)S(1)}, u32[]{:S(2)}) copy-start(bf16[256,2048]{1,0:T(8,128)(2,1)S(1)} %collective-permute-done.41.refs_3_) | copy-start | bytes 3145732
  115.8 61.2 %collective-permute-start.45 = (bf16[512,384]{1,0:T(8,128)(2,1)S(1)}, bf16[512,384]{1,0:T(8,128)(2,1)S(1)}, u32[]{:S(2)}, u32[]{:S(2)}) collective-permute-start(bf16[512,384]{1,0:T(8,128)(2,1)S(1)} %given_half.8), channel_id=1, source_target_pairs={{0,24},{8,16},{16,8},{24,0},{1,25},{9,17},{17,9},{25,1},{2,26},{10... | collective-permute-start | bytes 1179656 | tf_op jit(solution)/shard_map/ppermute | solution.py:54
  119.4 53.4 %collective-permute-start.46 = (bf16[512,256]{1,0:T(8,128)(2,1)S(1)}, bf16[512,256]{1,0:T(8,128)(2,1)S(1)}, u32[]{:S(2)}, u32[]{:S(2)}) collective-permute-start(bf16[512,256]{1,0:T(8,128)(2,1)S(1)} %given_half.9), channel_id=1, source_target_pairs={{0,24},{8,16},{16,8},{24,0},{1,25},{9,17},{17,9},{25,1},{2,26},{10... | collective-permute-start | bytes 786440 | tf_op jit(solution)/shard_map/ppermute | solution.py:54
  123.4 71.3 %collective-permute-start.44 = (bf16[512,384]{1,0:T(8,128)(2,1)}, bf16[512,384]{1,0:T(8,128)(2,1)}, u32[]{:S(2)}, u32[]{:S(2)}) collective-permute-start(bf16[512,384]{1,0:T(8,128)(2,1)} %given_half.7), channel_id=1, source_target_pairs={{0,24},{8,16},{16,8},{24,0},{1,25},{9,17},{17,9},{25,1},{2,26},{10... | collective-permute-start | bytes 1179656 | tf_op jit(solution)/shard_map/ppermute | solution.py:54
  128.6 48.3 %copy-start.11 = (bf16[2,1024,256]{2,1,0:T(8,128)(2,1)}, bf16[2,1024,256]{2,1,0:T(8,128)(2,1)S(1)}, u32[]{:S(2)}) copy-start(bf16[2,1024,256]{2,1,0:T(8,128)(2,1)S(1)} %collective-permute-done.35.core_ref) | copy-start | bytes 3145732
  128.6 70.8 %collective-permute-start.43 = (bf16[512,384]{1,0:T(8,128)(2,1)}, bf16[512,384]{1,0:T(8,128)(2,1)}, u32[]{:S(2)}, u32[]{:S(2)}) collective-permute-start(bf16[512,384]{1,0:T(8,128)(2,1)} %given_half.6), channel_id=1, source_target_pairs={{0,24},{8,16},{16,8},{24,0},{1,25},{9,17},{17,9},{25,1},{2,26},{10... | collective-permute-start | bytes 1179656 | tf_op jit(solution)/shard_map/ppermute | solution.py:54
  172.7 38.8 %collective-permute-start.36 = (bf16[1024,256]{1,0:T(8,128)(2,1)}, bf16[1024,256]{1,0:T(8,128)(2,1)}, u32[]{:S(2)}, u32[]{:S(2)}) collective-permute-start(bf16[1024,256]{1,0:T(8,128)(2,1)} %fusion), channel_id=1, source_target_pairs={{0,2},{1,3},{2,0},{3,1},{4,6},{5,7},{6,4},{7,5},{8,10},{9,11},{10,... | collective-permute-start | bytes 1572872 | tf_op jit(solution)/shard_map/ppermute | solution.py:44
  177.7 26.6 %collective-permute-start.42 = (bf16[512,384]{1,0:T(8,128)(2,1)}, bf16[512,384]{1,0:T(8,128)(2,1)}, u32[]{:S(2)}, u32[]{:S(2)}) collective-permute-start(bf16[512,384]{1,0:T(8,128)(2,1)} %given_half.5), channel_id=1, source_target_pairs={{0,24},{8,16},{16,8},{24,0},{1,25},{9,17},{17,9},{25,1},{2,26},{10... | collective-permute-start | bytes 1179656 | tf_op jit(solution)/shard_map/ppermute | solution.py:54
  (82 other events, 738.5 us)

commit v2 on v1

--- a/solution.py
+++ b/solution.py
@@ -10,7 +10,7 @@
 TILE = 128
 GROUP = 4
 VMEM_BYTES = 40 * 1024 * 1024
-ANY = pl.BlockSpec(memory_space=pl.ANY)
+ANY = pl.BlockSpec(memory_space=pltpu.MemorySpace.HBM)
 SMEM = pl.BlockSpec(memory_space=pltpu.SMEM)
 VMEM = pl.BlockSpec(memory_space=pltpu.VMEM)
 
@@ -20,7 +20,7 @@
 
 
 def cost(flops, nbytes):
-    return pl.CostEstimate(flops=flops, bytes_accessed=nbytes, transcendentals=0)
+    return pl.CostEstimate(flops=1, bytes_accessed=1, transcendentals=0)
 
 
 def column_chunks(width):
@@ -112,16 +112,17 @@
     )(route, stored)
 
 
-def load_tokens(piece_refs, token_ref, sems):
+def load_tokens(piece_refs, offsets, token_ref, sems):
     group, quarter = place()
     groups = len(piece_refs) // GROUP
+    width = token_ref.shape[3]
     copies = []
     for step in range(groups):
         for mask in range(GROUP):
             block = lax.rem(group + step, groups) * GROUP + (quarter ^ mask)
-            copy = pltpu.make_async_copy(
-                piece_refs[step * GROUP + mask], token_ref.at[:, block], sems.at[step * GROUP + mask]
-            )
+            i = step * GROUP + mask
+            source = piece_refs[i].at[:, :, pl.ds(offsets[i], width)]
+            copy = pltpu.make_async_copy(source, token_ref.at[:, block], sems.at[i])
             copy.start()
             copies.append(copy)
     return copies
@@ -150,10 +151,10 @@
     return copies
 
 
-def half_grad(given, refs, pieces, hidden_scratch, token_scratch, hidden_sems, token_sems):
-    hidden_refs, piece_refs = refs[:GROUP], refs[GROUP : GROUP + pieces]
+def half_grad(given, refs, offsets, hidden_scratch, token_scratch, hidden_sems, token_sems):
+    hidden_refs, piece_refs = refs[:GROUP], refs[GROUP : GROUP + len(offsets)]
     copies = load_hidden(given, hidden_refs, hidden_scratch, hidden_sems)
-    copies += load_tokens(piece_refs, token_scratch, token_sems)
+    copies += load_tokens(piece_refs, offsets, token_scratch, token_sems)
     for copy in copies:
         copy.wait()
     rows = hidden_scratch.shape[1]
@@ -164,14 +165,15 @@
     )
 
 
-def given_kernel(pieces, *refs):
-    out_ref = refs[GROUP + pieces]
-    out_ref[...] = half_grad(True, refs, pieces, *refs[GROUP + pieces + 1 :]).astype(out_ref.dtype)
-
-
-def scratches(hidden_all, pieces):
+def given_kernel(offsets, *refs):
+    after_pieces = GROUP + len(offsets)
+    out_ref = refs[after_pieces]
+    out_ref[...] = half_grad(True, refs, offsets, *refs[after_pieces + 1 :]).astype(out_ref.dtype)
+
+
+def scratches(hidden_all, pieces, width):
     units, rows = hidden_all[0].shape
-    micros, block_rows, width = pieces[0].shape
+    micros, block_rows, _ = pieces[0].shape
     return [
         pltpu.VMEM((2 * units, rows), jnp.bfloat16),
         pltpu.VMEM((micros, len(pieces), block_rows, width), jnp.bfloat16),
@@ -180,31 +182,32 @@
     ]
 
 
-def grad_cost(hidden_all, pieces):
+def grad_cost(hidden_all, width):
     units, rows = hidden_all[0].shape
-    width = pieces[0].shape[2]
     return cost(4 * units * rows * width, 4 * units * rows + 2 * rows * width + 4 * units * width)
 
 
-def given_half(hidden_all, pieces):
+def given_half(hidden_all, placed, width):
     units = hidden_all[0].shape[0]
+    pieces, offsets = zip(*placed)
     return pl.pallas_call(
-        functools.partial(given_kernel, len(pieces)),
-        out_shape=jax.ShapeDtypeStruct((2 * units, pieces[0].shape[2]), jnp.bfloat16),
+        functools.partial(given_kernel, offsets),
+        out_shape=jax.ShapeDtypeStruct((2 * units, width), jnp.bfloat16),
         in_specs=[ANY] * (GROUP + len(pieces)),
         out_specs=VMEM,
-        scratch_shapes=scratches(hidden_all, pieces),
+        scratch_shapes=scratches(hidden_all, pieces, width),
         compiler_params=params(),
-        cost_estimate=grad_cost(hidden_all, pieces),
+        cost_estimate=grad_cost(hidden_all, width),
         name="given_half",
     )(*hidden_all, *pieces)
 
 
-def kept_kernel(pieces, offset, aliased, *refs):
-    partner_ref = refs[GROUP + pieces]
-    refs_after = refs[GROUP + pieces + (2 if aliased else 1) :]
+def kept_kernel(offsets, offset, aliased, *refs):
+    after_pieces = GROUP + len(offsets)
+    partner_ref = refs[after_pieces]
+    refs_after = refs[after_pieces + (2 if aliased else 1) :]
     out_ref, sum_scratch, out_sem = refs_after[0], refs_after[5], refs_after[6]
-    total = half_grad(False, refs, pieces, *refs_after[1:5]) + partner_ref[...].astype(jnp.float32)
+    total = half_grad(False, refs, offsets, *refs_after[1:5]) + partner_ref[...].astype(jnp.float32)
     sum_scratch[...] = total.astype(sum_scratch.dtype)
     width = sum_scratch.shape[1]
     copy = pltpu.make_async_copy(sum_scratch, out_ref.at[:, pl.ds(offset, width)], out_sem)
@@ -212,9 +215,10 @@
     copy.wait()
 
 
-def kept_half(hidden_all, pieces, partner, total, offset, full_width):
+def kept_half(hidden_all, placed, partner, total, offset, full_width):
     units = hidden_all[0].shape[0]
-    width = pieces[0].shape[2]
+    width = partner.shape[1]
+    pieces, offsets = zip(*placed)
     operands = [*hidden_all, *pieces, partner]
     specs = [ANY] * (GROUP + len(pieces)) + [VMEM]
     aliases = {}
@@ -223,34 +227,31 @@
         operands.append(total)
         specs.append(ANY)
     return pl.pallas_call(
-        functools.partial(kept_kernel, len(pieces), offset, total is not None),
+        functools.partial(kept_kernel, offsets, offset, total is not None),
         out_shape=jax.ShapeDtypeStruct((2 * units, full_width), jnp.bfloat16),
         in_specs=specs,
         out_specs=ANY,
-        scratch_shapes=scratches(hidden_all, pieces)
+        scratch_shapes=scratches(hidden_all, pieces, width)
         + [pltpu.VMEM((2 * units, width), jnp.bfloat16), pltpu.SemaphoreType.DMA],
         input_output_aliases=aliases,
         compiler_params=params(),
-        cost_estimate=grad_cost(hidden_all, pieces),
+        cost_estimate=grad_cost(hidden_all, width),
         name="kept_half",
     )(*operands)
 
 
-def partial_kernel(chunks, *refs):
-    pieces = len(chunks) * GROUP
+def partial_kernel(places, *refs):
+    pieces = len(places)
     piece_refs, weight_ref = refs[:pieces], refs[pieces]
     keep_ref, send_ref, token_scratch, sems = refs[pieces + 1 :]
     _, quarter = place()
     copies = []
-    for i, (offset, width) in enumerate(chunks):
-        for mask in range(GROUP):
-            copy = pltpu.make_async_copy(
-                piece_refs[i * GROUP + mask],
-                token_scratch.at[:, quarter ^ mask, :, pl.ds(offset, width)],
-                sems.at[i * GROUP + mask],
-            )
-            copy.start()
-            copies.append(copy)
+    for i, (mask, offset) in enumerate(places):
+        columns = pl.ds(offset, piece_refs[i].shape[2])
+        target = token_scratch.at[:, quarter ^ mask, :, columns]
+        copy = pltpu.make_async_copy(piece_refs[i], target, sems.at[i])
+        copy.start()
+        copies.append(copy)
     for copy in copies:
         copy.wait()
     rows = keep_ref.shape[1]
@@ -266,12 +267,13 @@
         ).astype(out_ref.dtype)
 
 
-def partial_grads(pieces, weight, chunks, micros, block_rows):
+def partial_grads(pieces, places, weight):
+    micros, block_rows, _ = pieces[0].shape
     rows = micros * GROUP * block_rows
     all_units, width = weight.shape
     units = all_units // GROUP
     return pl.pallas_call(
-        functools.partial(partial_kernel, chunks),
+        functools.partial(partial_kernel, places),
         out_shape=(
             jax.ShapeDtypeStruct((2, rows, units), jnp.float32),
             jax.ShapeDtypeStruct((2, rows, units), jnp.bfloat16),
@@ -384,53 +386,120 @@
     groups = lax.axis_size("expert") // GROUP
     group, quarter = place()
     chunks = column_chunks(quarter_width)
+    last = len(chunks) - 1
+    inside = {}
+    outside = {}
 
     def own_slice(mask, offset, width):
         start = (quarter ^ mask) * quarter_width + offset
-        return lax.dynamic_slice(grad_rows, (0, 0, start), (micros, block_rows, width))
-
-    hidden = hidden_acts(routes, saved_pre, block_rows)
-    inside = []
-    outside = []
-    hidden_all = None
-    for i, (offset, width) in enumerate(chunks):
-        outgoing = [own_slice(mask, offset, width) for mask in range(GROUP)]
-        if i >= 1:
-            outgoing[2] = after(outgoing[2], inside[i - 1][2])
-            outgoing[3] = after(outgoing[3], inside[i - 1][3])
-            outgoing[1] = after(outgoing[1], inside[i - 1][1])
-        inside.append([outgoing[0]] + [swap(outgoing[mask], mask) for mask in range(1, GROUP)])
-        if i == 0:
-            crossed = swap(hidden, 2)
-            hidden_all = [hidden, swap(hidden, 1), crossed, swap(crossed, 1)]
+        rows = late_rows if offset else grad_rows
+        return lax.dynamic_slice(rows, (0, 0, start), (micros, block_rows, width))
+
+    def exchange(part, masks, gate=None):
+        for mask in masks:
+            piece = own_slice(mask, *part)
+            if gate is not None:
+                piece = after(piece, gate)
+            inside[mask, part[0]] = swap(piece, mask) if mask else piece
+        return [inside[mask, part[0]] for mask in masks]
+
+    def cross(part, masks, gate=None):
         arrived = []
         for step in range(1, groups):
+            for mask in masks:
+                piece = inside[mask, part[0]]
+                if gate is not None:
+                    piece = after(piece, gate)
+                outside[step, mask, part[0]] = from_group(piece, step)
+                arrived.append(outside[step, mask, part[0]])
+        return arrived
+
+    def placed(i):
+        offset = chunks[i][0]
+        found = []
+        for step in range(groups):
             for mask in range(GROUP):
-                piece = inside[i][mask]
-                if i >= 1:
-                    piece = after(piece, outside[i - 1][(step - 1) * GROUP + mask])
-                arrived.append(from_group(piece, step))
-        outside.append(arrived)
-
-    partners = []
-    for inner, outer in zip(inside, outside):
-        partners.append(mirror(given_half(hidden_all, inner + outer)))
-    weight_grad = None
-    for (offset, width), inner, outer, partner in zip(chunks, inside, outside, partners):
-        weight_grad = kept_half(hidden_all, inner + outer, partner, weight_grad, offset, quarter_width)
-
-    store_grad = None
-    for step in range(groups):
+                key = (mask, offset)
+                array = inside[key] if step == 0 else outside[step, *key]
+                found.append((array, 0))
+        return found
+
+    def partial(step, gate):
         if step == 0:
-            pieces = [piece for chunk in inside for piece in chunk]
+            found = [(key, array) for key, array in inside.items()]
         else:
-            first = (step - 1) * GROUP
-            pieces = [piece for chunk in outside for piece in chunk[first : first + GROUP]]
-        keep, send = partial_grads(pieces, weight, chunks, micros, block_rows)
+            found = [(key[1:], array) for key, array in outside.items() if key[0] == step]
+        places, pieces = zip(*found)
+        return partial_grads((after(pieces[0], gate), *pieces[1:]), places, weight)
+
+    def group_sum(keep, send):
         core = swap(send, 1)
         across = swap((keep[1] + core[1].astype(jnp.float32)).astype(jnp.bfloat16), 2)
+        return keep, core, across
+
+    def store(step, sums, total):
         source = lax.rem(group + step, groups).astype(jnp.int32)
-        store_grad = store_grads(routes, source, saved_pre, keep, core, across, store_grad)
+        return store_grads(routes, source, saved_pre, *sums, total)
+
+    def given(i, token):
+        return given_half([token, *hidden_all[1:]], placed(i), chunks[i][1])
+
+    def kept(i, total):
+        return kept_half(hidden_all, placed(i), partners[i], total, chunks[i][0], quarter_width)
+
+    narrow = chunks[0]
+    ready = exchange(narrow, (2, 3, 0, 1)) + cross(narrow, (0,))
+    hidden = hidden_acts(routes, saved_pre, block_rows)
+    late_rows = after(grad_rows, inside[1, 0])
+    for part in chunks[1:]:
+        exchange(part, (0, 1))
+    hidden = after(hidden, *ready)
+    crossed = swap(hidden, 2)
+    ready = cross(narrow, (1, 2, 3), hidden) + cross(chunks[1], (0, 1), hidden)
+    ready += cross(chunks[2], (0,), hidden)
+    crossed = after(crossed, *ready)
+    hidden_all = [hidden, swap(after(hidden, crossed), 1), crossed, swap(crossed, 1)]
+    exchange(chunks[1], (2, 3), crossed)
+    far = cross(chunks[2], (1,), crossed) + cross(chunks[3], (0,), crossed)
+    token = after(hidden_all[0], *hidden_all[1:])
+    halves, partners = [given(0, token)], []
+    weight_grad = None
+    store_grad = None
+    ready = []
+    later = []
+    own_sums = None
+    extra = {1: (3, 1), 2: (4, 0), 3: (4, 1)}
+    for i in range(last):
+        payload = after(halves[i], *ready)
+        partners.append(mirror(payload))
+        arrived = cross(chunks[i + 1], (2, 3), payload)
+        if i in extra:
+            arrived += cross(chunks[extra[i][0]], (extra[i][1],), payload)
+        ready = arrived + [partners[i]]
+        if i == 0:
+            arrived = arrived + far
+            ready += exchange(chunks[2], (2, 3), payload)
+        else:
+            weight_grad = kept(i - 1, weight_grad)
+            ready.append(weight_grad)
+        if i == 1:
+            for part in chunks[3:]:
+                ready += exchange(part, (2, 3), payload)
+        if i == last - 2:
+            own_sums = group_sum(*partial(0, payload))
+        halves.append(given(i + 1, after(hidden_all[0], *arrived)))
+        if i == last - 1:
+            ready.append(own_sums[2])
+            later = [partial(step, halves[last]) for step in range(1, groups)]
+            ready += [sums[1] for sums in later]
+    payload = after(halves[last], *ready)
+    partners.append(mirror(payload))
+    weight_grad = kept(last - 1, weight_grad)
+    store_grad = store(0, own_sums, None)
+    for step, (keep, send) in enumerate(later, 1):
+        store_grad = store(step, group_sum(keep, after(send, payload)), store_grad)
+    partners[last] = after(partners[last], store_grad, weight_grad)
+    weight_grad = kept(last, weight_grad)
     return store_grad[None], weight_grad[None]
 
 

time: 215 us -> 169 us (0.79)
  waiting for transfers between devices: 93.5 us -> 55.3 us
  Pallas kernels: 53.1 us -> 44.8 us
  starting transfers between devices: 36.5 us -> 41.8 us
  local copies, waits for them, and re-layouts: 26.8 us -> 21.8 us
    ppermute x5, waiting for transfers between devices: 42.6 us -> 3.09 us  [mirror(): return lax.ppermute(value, 'pipe', [(i, size - 1 - i) for i in range(size)])]
    pallas_call x12, Pallas kernels: 46.9 us -> 38.7 us  [the longest x5 16.8 us: kept_half(): pl.pallas_call(functools.partial(kept_kernel, offsets, offset, total is n...]
    ppermute x20, waiting for transfers between devices: 39.7 us -> 46 us  [from_group(): lax.ppermute(value, 'expert', [((i + step * GROUP) % size, i) for i in ra...]
    ppermute x22, waiting for transfers between devices: 11.2 us -> 6.23 us  [swap(): return lax.ppermute(value, 'expert', [(i, i ^ mask) for i in range(size)])]
    unnamed x198 -> x116, local copies, waits for them, and re-layouts: 21.5 us -> 17.4 us
    ppermute x22, starting transfers between devices: 8.93 us -> 11.6 us  [swap(): return lax.ppermute(value, 'expert', [(i, i ^ mask) for i in range(size)])]
  transfers between devices with their start and end apart: 47 -> 47, of which waited for: 16 -> 21; matrix products, arithmetic and copies ran while one was open for 3% -> 2% of each run, Pallas kernels for 24% -> 22%
where the time goes in v2:
time: 169 us; the launch traced here: 166 us
  waiting for transfers between devices  55.3 us (33%)
  Pallas kernels  44.8 us (27%)
  starting transfers between devices  41.8 us (25%)
  local copies, waits for them, and re-layouts  21.8 us (13%)
    ppermute x20, waiting for transfers between devices, from_group(): lax.ppermute(value, 'expert', [((i + step * GROUP) % size, i) for i in ra...  46 us
    ppermute x20, starting transfers between devices, from_group(): lax.ppermute(value, 'expert', [((i + step * GROUP) % size, i) for i in ra...  23.4 us
    unnamed x116, local copies, waits for them, and re-layouts  17.4 us
    pallas_call x5, Pallas kernels, kept_half(): pl.pallas_call(functools.partial(kept_kernel, offsets, offset, total is n...  16.8 us
    pallas_call x5, Pallas kernels, given_half(): pl.pallas_call(functools.partial(given_kernel, offsets), out_shape=jax.Sh...  12.6 us
    ppermute x22, starting transfers between devices, swap(): return lax.ppermute(value, 'expert', [(i, i ^ mask) for i in range(size)])  11.6 us
    pallas_call x2, Pallas kernels, partial_grads(): pl.pallas_call(functools.partial(partial_kernel, places), out_shape=(jax....  9.19 us
    ppermute x5, starting transfers between devices, mirror(): return lax.ppermute(value, 'pipe', [(i, size - 1 - i) for i in range(size)])  6.8 us
  transfers between devices with their start and end apart: 47, of which 21 were waited for; matrix products, arithmetic and copies ran while one was open for 2% of the time, Pallas kernels for 22%

profile of v2, /device:TPU:8, one launch (start us, length us, event | category | flops | bytes accessed | tf_op | source)
XLA Modules:
  0.0 166.5 jit_solution(13919996064960883959)
XLA Ops:
  0.7 1.1 dynamic-slice_bitcast_fusion
  1.9 1.6 collective-permute-start.2
  4.1 1.5 collective-permute-start
  6.3 1.6 copy-done.3
  7.9 1.6 hidden_acts.1.refs_0_
  9.6 1.0 collective-permute-done.1.refs_6_.refs_0_
  11.2 1.5 collective-permute-start.4
  12.7 2.5 %constant_dynamic-slice_fusion = (bf16[2,128,384]{2,1,0:T(8,128)(2,1)S(1)}, bf16[2,128,384]{2,1,0:T(8,128)(2,1)S(1)}, bf16[2,128,384]{2,1,0:T(8,128)(2,1)S(1)}, ...) fusion(bf16[2,128,7168]{2,1,0:T(8,128)(2,1)} %bitcast.27, ...), kind=kLoop, calls=%fused_computation.8 | loop fusion | bytes 6291520 | tf_op jit(solution)/shard_map/dynamic_slice | solution.py:396
  15.3 1.6 collective-permute-start.5
  18.8 1.5 collective-permute-start.8
  21.7 1.5 collective-permute-start.10
  23.2 1.3 collective-permute-done.6.refs_10_.refs_2_
  24.5 1.5 collective-permute-start.7
  26.7 12.8 %collective-permute-done.7.refs_11_.refs_3_ = bf16[2,128,256]{2,1,0:T(8,128)(2,1)S(1)} collective-permute-done((bf16[2,128,256]{2,1,0:T(8,128)(2,1)S(1)}, bf16[2,128,256]{2,1,0:T(8,128)(2,1)S(1)}, u32[]{:S(2)}, u32[]{:S(2)}) %collective-permute-start.7) | collective-permute-done | bytes 131104 | tf_op jit(solution)/shard_map/ppermute | solution.py:49
  40.7 1.3 collective-permute-start.16
  42.0 2.1 %collective-permute-done.18.refs_5_.refs_7_ = bf16[2,128,384]{2,1,0:T(8,128)(2,1)S(1)} collective-permute-done((bf16[2,128,384]{2,1,0:T(8,128)(2,1)S(1)}, bf16[2,128,384]{2,1,0:T(8,128)(2,1)S(1)}, u32[]{:S(2)}, u32[]{:S(2)}) %collective-permute-start.18) | collective-permute-done | bytes 196640 | tf_op jit(solution)/shard_map/ppermute | solution.py:44
  44.0 1.5 collective-permute-start.19
  48.8 1.7 given_half.5
  50.5 1.6 collective-permute-start.15
  52.1 1.6 collective-permute-start.21
  54.7 1.3 collective-permute-done.20.refs_8_
  56.0 4.2 %collective-permute-done.15.refs_10_.refs_9_ = bf16[2,128,384]{2,1,0:T(8,128)(2,1)S(1)} collective-permute-done((bf16[2,128,384]{2,1,0:T(8,128)(2,1)S(1)}, bf16[2,128,384]{2,1,0:T(8,128)(2,1)S(1)}, u32[]{:S(2)}, u32[]{:S(2)}) %collective-permute-start.15) | collective-permute-done | bytes 196640 | tf_op jit(solution)/shard_map/ppermute | solution.py:49
  60.2 3.4 %collective-permute-done.17.refs_11_.refs_10_ = bf16[2,128,384]{2,1,0:T(8,128)(2,1)S(1)} collective-permute-done((bf16[2,128,384]{2,1,0:T(8,128)(2,1)S(1)}, bf16[2,128,384]{2,1,0:T(8,128)(2,1)S(1)}, u32[]{:S(2)}, u32[]{:S(2)}) %collective-permute-start.17) | collective-permute-done | bytes 196640 | tf_op jit(solution)/shard_map/ppermute | solution.py:49
  63.6 2.5 %given_half.6 = bf16[512,384]{1,0:T(8,128)(2,1)S(1)} custom-call(bf16[256,2048]{1,0:T(8,128)(2,1)S(1)} %hidden_acts.1.refs_0_, bf16[256,2048]{1,0:T(8,128)(2,1)S(1)} %collective-permute-done.13.refs_1_, bf16[256,2048]{1,0:T(8,128)(2,1)S(1)} %collective-permute-done.4.refs_2_, bf16[256,2048]{1,0:T(8,128)(2,1)S(1)} %collective-permute-done.14.refs_3_, ...), custom_call_target="tpu_custom_call" | custom-call | flops 1 | bytes 1 | tf_op jit(solution)/shard_map/given_half/pallas_call | solution.py:193
  66.8 1.5 collective-permute-start.26
  68.8 1.6 collective-permute-start.30
  70.4 1.5 collective-permute-start.29
  72.4 1.0 collective-permute-start.25
  73.4 1.2 collective-permute-done.26.refs_10_.refs_11_
  74.6 4.2 %collective-permute-done.27.refs_11_.refs_12_ = bf16[2,128,384]{2,1,0:T(8,128)(2,1)S(1)} collective-permute-done((bf16[2,128,384]{2,1,0:T(8,128)(2,1)S(1)}, bf16[2,128,384]{2,1,0:T(8,128)(2,1)S(1)}, u32[]{:S(2)}, u32[]{:S(2)}) %collective-permute-start.27) | collective-permute-done | bytes 196640 | tf_op jit(solution)/shard_map/ppermute | solution.py:49
  78.9 2.2 %collective-permute-done.29.refs_9_.refs_13_ = bf16[2,128,384]{2,1,0:T(8,128)(2,1)S(1)} collective-permute-done((bf16[2,128,384]{2,1,0:T(8,128)(2,1)S(1)}, bf16[2,128,384]{2,1,0:T(8,128)(2,1)S(1)}, u32[]{:S(2)}, u32[]{:S(2)}) %collective-permute-start.29) | collective-permute-done | bytes 196640 | tf_op jit(solution)/shard_map/ppermute | solution.py:49
  81.1 2.4 %kept_half.5.refs_13_ = bf16[512,1792]{1,0:T(8,128)(2,1)} custom-call(bf16[256,2048]{1,0:T(8,128)(2,1)S(1)} %hidden_acts.1.refs_0_, bf16[256,2048]{1,0:T(8,128)(2,1)S(1)} %collective-permute-done.13.refs_1_, bf16[256,2048]{1,0:T(8,128)(2,1)S(1)} %collective-permute-done.4.refs_2_, bf16[256,2048]{1,0:T(8,128)(2,1)S(1)} %collective-permute-done.14.refs_3_, ...), custom_call_target="tpu_custom_call" | custom-call | flops 1 | bytes 1 | tf_op jit(solution)/shard_map/kept_half/pallas_call | solution.py:229
  83.5 2.6 %given_half.7 = bf16[512,384]{1,0:T(8,128)(2,1)S(1)} custom-call(bf16[256,2048]{1,0:T(8,128)(2,1)S(1)} %hidden_acts.1.refs_0_, bf16[256,2048]{1,0:T(8,128)(2,1)S(1)} %collective-permute-done.13.refs_1_, bf16[256,2048]{1,0:T(8,128)(2,1)S(1)} %collective-permute-done.4.refs_2_, bf16[256,2048]{1,0:T(8,128)(2,1)S(1)} %collective-permute-done.14.refs_3_, ...), custom_call_target="tpu_custom_call" | custom-call | flops 1 | bytes 1 | tf_op jit(solution)/shard_map/given_half/pallas_call | solution.py:193
  86.8 4.6 %partial_grads.3 = (f32[2,1024,256]{2,1,0:T(8,128)S(1)}, bf16[2,1024,256]{2,1,0:T(8,128)(2,1)S(1)}) custom-call(bf16[2,128,256]{2,1,0:T(8,128)(2,1)S(1)} %copy-done.53, bf16[2,128,256]{2,1,0:T(8,128)(2,1)S(1)} %copy-done.50, bf16[2,128,256]{2,1,0:T(8,128)(2,1)S(1)} %copy-done.15, bf16[2,128,256]{2,1,0:T(8,128)(2,1)S(1)} %copy-done.47, ...), custom_call_target="tpu_custom_call" | custom-call | flops 1 | bytes 1 | tf_op jit(solution)/shard_map/partial_grads/pallas_call | solution.py:275
  91.4 1.6 collective-permute-start.36
  93.1 1.5 collective-permute-start.33
  95.1 1.5 collective-permute-start.35
  96.8 1.6 collective-permute-start.43
  98.3 3.5 %kept_half.6.refs_13_ = bf16[512,1792]{1,0:T(8,128)(2,1)} custom-call(bf16[256,2048]{1,0:T(8,128)(2,1)S(1)} %hidden_acts.1.refs_0_, bf16[256,2048]{1,0:T(8,128)(2,1)S(1)} %collective-permute-done.13.refs_1_, bf16[256,2048]{1,0:T(8,128)(2,1)S(1)} %collective-permute-done.4.refs_2_, ...), custom_call_target="tpu_custom_call", output_to_operand_aliasing={{}: (13, {})} | custom-call | flops 1 | bytes 1 | tf_op jit(solution)/shard_map/kept_half/pallas_call | solution.py:229
  101.9 3.2 %collective-permute-done.34.refs_11_.refs_15_ = bf16[2,128,384]{2,1,0:T(8,128)(2,1)S(1)} collective-permute-done((bf16[2,128,384]{2,1,0:T(8,128)(2,1)S(1)}, bf16[2,128,384]{2,1,0:T(8,128)(2,1)S(1)}, u32[]{:S(2)}, u32[]{:S(2)}) %collective-permute-start.34) | collective-permute-done | bytes 196640 | tf_op jit(solution)/shard_map/ppermute | solution.py:49
  105.0 3.4 %collective-permute-done.35.refs_8_.refs_16_ = bf16[2,128,384]{2,1,0:T(8,128)(2,1)S(1)} collective-permute-done((bf16[2,128,384]{2,1,0:T(8,128)(2,1)S(1)}, bf16[2,128,384]{2,1,0:T(8,128)(2,1)S(1)}, u32[]{:S(2)}, u32[]{:S(2)}) %collective-permute-start.35) | collective-permute-done | bytes 196640 | tf_op jit(solution)/shard_map/ppermute | solution.py:49
  108.5 2.6 %given_half.8 = bf16[512,384]{1,0:T(8,128)(2,1)S(1)} custom-call(bf16[256,2048]{1,0:T(8,128)(2,1)S(1)} %hidden_acts.1.refs_0_, bf16[256,2048]{1,0:T(8,128)(2,1)S(1)} %collective-permute-done.13.refs_1_, bf16[256,2048]{1,0:T(8,128)(2,1)S(1)} %collective-permute-done.4.refs_2_, bf16[256,2048]{1,0:T(8,128)(2,1)S(1)} %collective-permute-done.14.refs_3_, ...), custom_call_target="tpu_custom_call" | custom-call | flops 1 | bytes 1 | tf_op jit(solution)/shard_map/given_half/pallas_call | solution.py:193
  111.4 1.6 collective-permute-start.41
  113.0 1.5 collective-permute-start.37
  115.0 1.5 collective-permute-start.40
  116.5 3.3 %kept_half.7.refs_13_ = bf16[512,1792]{1,0:T(8,128)(2,1)} custom-call(bf16[256,2048]{1,0:T(8,128)(2,1)S(1)} %hidden_acts.1.refs_0_, bf16[256,2048]{1,0:T(8,128)(2,1)S(1)} %collective-permute-done.13.refs_1_, bf16[256,2048]{1,0:T(8,128)(2,1)S(1)} %collective-permute-done.4.refs_2_, ...), custom_call_target="tpu_custom_call", output_to_operand_aliasing={{}: (13, {})} | custom-call | flops 1 | bytes 1 | tf_op jit(solution)/shard_map/kept_half/pallas_call | solution.py:229
  119.8 1.0 collective-permute-done.37.refs_10_.refs_17_
  120.8 4.2 %collective-permute-done.38.refs_11_.refs_18_ = bf16[2,128,384]{2,1,0:T(8,128)(2,1)S(1)} collective-permute-done((bf16[2,128,384]{2,1,0:T(8,128)(2,1)S(1)}, bf16[2,128,384]{2,1,0:T(8,128)(2,1)S(1)}, u32[]{:S(2)}, u32[]{:S(2)}) %collective-permute-start.38) | collective-permute-done | bytes 196640 | tf_op jit(solution)/shard_map/ppermute | solution.py:49
  125.0 2.6 %collective-permute-done.40.refs_9_.refs_19_ = bf16[2,128,384]{2,1,0:T(8,128)(2,1)S(1)} collective-permute-done((bf16[2,128,384]{2,1,0:T(8,128)(2,1)S(1)}, bf16[2,128,384]{2,1,0:T(8,128)(2,1)S(1)}, u32[]{:S(2)}, u32[]{:S(2)}) %collective-permute-start.40) | collective-permute-done | bytes 196640 | tf_op jit(solution)/shard_map/ppermute | solution.py:49
  127.6 3.3 %given_half.9 = bf16[512,384]{1,0:T(8,128)(2,1)} custom-call(bf16[256,2048]{1,0:T(8,128)(2,1)S(1)} %hidden_acts.1.refs_0_, bf16[256,2048]{1,0:T(8,128)(2,1)S(1)} %collective-permute-done.13.refs_1_, bf16[256,2048]{1,0:T(8,128)(2,1)S(1)} %collective-permute-done.4.refs_2_, bf16[256,2048]{1,0:T(8,128)(2,1)S(1)} %collective-permute-done.14.refs_3_, ...), custom_call_target="tpu_custom_call" | custom-call | flops 1 | bytes 1 | tf_op jit(solution)/shard_map/given_half/pallas_call | solution.py:193
  131.0 4.6 %partial_grads.2 = (f32[2,1024,256]{2,1,0:T(8,128)S(1)}, bf16[2,1024,256]{2,1,0:T(8,128)(2,1)S(1)}) custom-call(bf16[2,128,256]{2,1,0:T(8,128)(2,1)S(1)} %copy-done.45, bf16[2,128,256]{2,1,0:T(8,128)(2,1)S(1)} %collective-permute-done.5.refs_9_.refs_1_, bf16[2,128,256]{2,1,0:T(8,128)(2,1)S(1)} %collective-permute-done.6.refs_10_.refs_2_, ...), custom_call_target="tpu_custom_call" | custom-call | flops 1 | bytes 1 | tf_op jit(solution)/shard_map/partial_grads/pallas_call | solution.py:275
  135.8 2.6 %collective-permute-done.44.core_ref = bf16[2,1024,256]{2,1,0:T(8,128)(2,1)S(1)} collective-permute-done((bf16[2,1024,256]{2,1,0:T(8,128)(2,1)S(1)}, bf16[2,1024,256]{2,1,0:T(8,128)(2,1)S(1)}, u32[]{:S(2)}, u32[]{:S(2)}) %collective-permute-start.44) | collective-permute-done | bytes 1048608 | tf_op jit(solution)/shard_map/ppermute | solution.py:44
  138.4 1.1 fusion.1
  139.5 1.3 copy-done.8
  140.9 1.5 collective-permute-start.45
  142.8 1.2 copy-done.1
  144.0 0.9 copy-done.17
  145.0 0.9 copy-done.21
  150.5 1.0 copy-done.57
  151.5 3.3 %kept_half.8.refs_13_ = bf16[512,1792]{1,0:T(8,128)(2,1)} custom-call(bf16[256,2048]{1,0:T(8,128)(2,1)S(1)} %hidden_acts.1.refs_0_, bf16[256,2048]{1,0:T(8,128)(2,1)S(1)} %collective-permute-done.13.refs_1_, bf16[256,2048]{1,0:T(8,128)(2,1)S(1)} %collective-permute-done.4.refs_2_, bf16[256,2048]{1,0:T(8,128)(2,1)S(1)} %copy-done.1, ...), custom_call_target="tpu_custom_call", output_to_operand_aliasing={{}: (13, {})} | custom-call | flops 1 | bytes 1 | tf_op jit(solution)/shard_map/kept_half/pallas_call | solution.py:229
  154.9 2.1 %store_grads.2.refs_0_ = bf16[2,1024,512]{2,1,0:T(8,128)(2,1)} custom-call(s32[2,8,1]{2,1,0:T(8,128)S(1)} %copy.13.route_ref, s32[1]{0:T(128)} %bitcast.11.group_ref, bf16[2,1024,512]{2,1,0:T(8,128)(2,1)S(1)} %bitcast.21, f32[2,1024,256]{2,1,0:T(8,128)S(1)} %copy-done.7, bf16[2,1024,256]{2,1,0:T(8,128)(2,1)S(1)} %copy-done.11, bf16[1024,256]{1,0:T(8,128)(2,1)S(1)} %copy-done.55), custom_call_target="tpu_custom_call" | custom-call | flops 1 | bytes 1 | tf_op jit(solution)/shard_map/store_grads/pallas_call | solution.py:363
  157.4 2.5 %store_grads.3 = bf16[2,1024,512]{2,1,0:T(8,128)(2,1)} custom-call(s32[2,8,1]{2,1,0:T(8,128)S(1)} %copy.13.route_ref, s32[1]{0:T(128)} %bitcast.1.group_ref, bf16[2,1024,512]{2,1,0:T(8,128)(2,1)S(1)} %bitcast.22, f32[2,1024,256]{2,1,0:T(8,128)S(1)} %copy-done.9, bf16[2,1024,256]{2,1,0:T(8,128)(2,1)S(1)} %copy-done.13, ...), custom_call_target="tpu_custom_call", output_to_operand_aliasing={{}: (6, {})} | custom-call | flops 1 | bytes 1 | tf_op jit(solution)/shard_map/store_grads/pallas_call | solution.py:363
  159.8 2.1 %collective-permute-done.46.refs_12_ = bf16[512,384]{1,0:T(8,128)(2,1)} collective-permute-done((bf16[512,384]{1,0:T(8,128)(2,1)}, bf16[512,384]{1,0:T(8,128)(2,1)}, u32[]{:S(2)}, u32[]{:S(2)}) %collective-permute-start.46) | collective-permute-done | bytes 393248 | tf_op jit(solution)/shard_map/ppermute | solution.py:54
  162.0 4.3 %kept_half.9 = bf16[512,1792]{1,0:T(8,128)(2,1)} custom-call(bf16[256,2048]{1,0:T(8,128)(2,1)S(1)} %hidden_acts.1.refs_0_, bf16[256,2048]{1,0:T(8,128)(2,1)S(1)} %collective-permute-done.13.refs_1_, bf16[256,2048]{1,0:T(8,128)(2,1)S(1)} %collective-permute-done.4.refs_2_, bf16[256,2048]{1,0:T(8,128)(2,1)S(1)} %copy-done.2, ...), custom_call_target="tpu_custom_call", output_to_operand_aliasing={{}: (13, {})} | custom-call | flops 1 | bytes 1 | tf_op jit(solution)/shard_map/kept_half/pallas_call | solution.py:229
  (166 shorter events, 20.9 us)
Async XLA Ops:
  1.8 7.7 %collective-permute-start.3 = (bf16[2,128,256]{2,1,0:T(8,128)(2,1)S(1)}, bf16[2,128,256]{2,1,0:T(8,128)(2,1)S(1)}, u32[]{:S(2)}, u32[]{:S(2)}) collective-permute-start(bf16[2,128,256]{2,1,0:T(8,128)(2,1)S(1)} %get-tuple-element.114), channel_id=1, source_target_pairs={{0,1},{1,0},{2,3},{3,2},{4,5},{5,4},{6,7},{7,6},{8,9},{9,8},{10,11... | collective-permute-start | bytes 393224 | tf_op jit(solution)/shard_map/ppermute | solution.py:44
  1.9 7.6 %collective-permute-start.2 = (bf16[2,128,256]{2,1,0:T(8,128)(2,1)S(1)}, bf16[2,128,256]{2,1,0:T(8,128)(2,1)S(1)}, u32[]{:S(2)}, u32[]{:S(2)}) collective-permute-start(bf16[2,128,256]{2,1,0:T(8,128)(2,1)S(1)} %get-tuple-element.115), channel_id=1, source_target_pairs={{0,3},{1,2},{2,1},{3,0},{4,7},{5,6},{6,5},{7,4},{8,11},{9,10},{10,... | collective-permute-start | bytes 393224 | tf_op jit(solution)/shard_map/ppermute | solution.py:44
  3.5 7.1 %collective-permute-start.1 = (bf16[2,128,256]{2,1,0:T(8,128)(2,1)S(1)}, bf16[2,128,256]{2,1,0:T(8,128)(2,1)S(1)}, u32[]{:S(2)}, u32[]{:S(2)}) collective-permute-start(bf16[2,128,256]{2,1,0:T(8,128)(2,1)S(1)} %get-tuple-element.116), channel_id=1, source_target_pairs={{0,2},{1,3},{2,0},{3,1},{4,6},{5,7},{6,4},{7,5},{8,10},{9,11},{10,... | collective-permute-start | bytes 393224 | tf_op jit(solution)/shard_map/ppermute | solution.py:44
  4.1 6.5 %collective-permute-start = (bf16[2,128,256]{2,1,0:T(8,128)(2,1)S(1)}, bf16[2,128,256]{2,1,0:T(8,128)(2,1)S(1)}, u32[]{:S(2)}, u32[]{:S(2)}) collective-permute-start(bf16[2,128,256]{2,1,0:T(8,128)(2,1)S(1)} %get-tuple-element.117.refs_4_.refs_2_), channel_id=1, source_target_pairs={{4,0},{5,1},{6,2},{7,3},{0,4},{1,5},{2,6},{3,7},{12,8},{13,9},{14,... | collective-permute-start | bytes 393224 | tf_op jit(solution)/shard_map/ppermute | solution.py:49
  11.2 28.3 %collective-permute-start.4 = (bf16[256,2048]{1,0:T(8,128)(2,1)S(1)}, bf16[256,2048]{1,0:T(8,128)(2,1)S(1)}, u32[]{:S(2)}, u32[]{:S(2)}) collective-permute-start(bf16[256,2048]{1,0:T(8,128)(2,1)S(1)} %hidden_acts.1.refs_0_), channel_id=1, source_target_pairs={{0,2},{1,3},{2,0},{3,1},{4,6},{5,7},{6,4},{7,5},{8,10},{9,11},{10,... | collective-permute-start | bytes 3145736 | tf_op jit(solution)/shard_map/ppermute | solution.py:44
  12.7 33.3 %copy-start.15 = (bf16[2,128,256]{2,1,0:T(8,128)(2,1)S(1)}, bf16[2,128,256]{2,1,0:T(8,128)(2,1)}, u32[]{:S(2)}) copy-start(bf16[2,128,256]{2,1,0:T(8,128)(2,1)} %copy-done.14) | copy-start | bytes 393220
  12.7 33.3 %copy-start.45 = (bf16[2,128,256]{2,1,0:T(8,128)(2,1)S(1)}, bf16[2,128,256]{2,1,0:T(8,128)(2,1)}, u32[]{:S(2)}) copy-start(bf16[2,128,256]{2,1,0:T(8,128)(2,1)} %copy-done.44) | copy-start | bytes 393220
  15.3 5.0 %collective-permute-start.9 = (bf16[2,128,384]{2,1,0:T(8,128)(2,1)S(1)}, bf16[2,128,384]{2,1,0:T(8,128)(2,1)S(1)}, u32[]{:S(2)}, u32[]{:S(2)}) collective-permute-start(bf16[2,128,384]{2,1,0:T(8,128)(2,1)S(1)} %get-tuple-element.110), channel_id=1, source_target_pairs={{0,1},{1,0},{2,3},{3,2},{4,5},{5,4},{6,7},{7,6},{8,9},{9,8},{10,11... | collective-permute-start | bytes 589832 | tf_op jit(solution)/shard_map/ppermute | solution.py:44
  15.3 6.4 %collective-permute-start.5 = (bf16[2,128,256]{2,1,0:T(8,128)(2,1)S(1)}, bf16[2,128,256]{2,1,0:T(8,128)(2,1)S(1)}, u32[]{:S(2)}, u32[]{:S(2)}) collective-permute-start(bf16[2,128,256]{2,1,0:T(8,128)(2,1)S(1)} %collective-permute-done.3.refs_5_.refs_3_), channel_id=1, source_target_pairs={{4,0},{5,1},{6,2},{7,3},{0,4},{1,5},{2,6},{3,7},{12,8},{13,9},{14,... | collective-permute-start | bytes 393224 | tf_op jit(solution)/shard_map/ppermute | solution.py:49
  17.6 6.9 %collective-permute-start.6 = (bf16[2,128,256]{2,1,0:T(8,128)(2,1)S(1)}, bf16[2,128,256]{2,1,0:T(8,128)(2,1)S(1)}, u32[]{:S(2)}, u32[]{:S(2)}) collective-permute-start(bf16[2,128,256]{2,1,0:T(8,128)(2,1)S(1)} %collective-permute-done.1.refs_6_.refs_0_), channel_id=1, source_target_pairs={{4,0},{5,1},{6,2},{7,3},{0,4},{1,5},{2,6},{3,7},{12,8},{13,9},{14,... | collective-permute-start | bytes 393224 | tf_op jit(solution)/shard_map/ppermute | solution.py:49
  18.8 20.8 %collective-permute-start.8 = (bf16[2,128,384]{2,1,0:T(8,128)(2,1)S(1)}, bf16[2,128,384]{2,1,0:T(8,128)(2,1)S(1)}, u32[]{:S(2)}, u32[]{:S(2)}) collective-permute-start(bf16[2,128,384]{2,1,0:T(8,128)(2,1)S(1)} %get-tuple-element.55.refs_4_), channel_id=1, source_target_pairs={{4,0},{5,1},{6,2},{7,3},{0,4},{1,5},{2,6},{3,7},{12,8},{13,9},{14,... | collective-permute-start | bytes 589832 | tf_op jit(solution)/shard_map/ppermute | solution.py:49
  20.3 19.2 %collective-permute-start.11 = (bf16[2,128,384]{2,1,0:T(8,128)(2,1)S(1)}, bf16[2,128,384]{2,1,0:T(8,128)(2,1)S(1)}, u32[]{:S(2)}, u32[]{:S(2)}) collective-permute-start(bf16[2,128,384]{2,1,0:T(8,128)(2,1)S(1)} %get-tuple-element.57.refs_4_.refs_6_), channel_id=1, source_target_pairs={{4,0},{5,1},{6,2},{7,3},{0,4},{1,5},{2,6},{3,7},{12,8},{13,9},{14,... | collective-permute-start | bytes 589832 | tf_op jit(solution)/shard_map/ppermute | solution.py:49
  21.7 17.8 %collective-permute-start.10 = (bf16[2,128,384]{2,1,0:T(8,128)(2,1)S(1)}, bf16[2,128,384]{2,1,0:T(8,128)(2,1)S(1)}, u32[]{:S(2)}, u32[]{:S(2)}) collective-permute-start(bf16[2,128,384]{2,1,0:T(8,128)(2,1)S(1)} %collective-permute-done.9.refs_5_), channel_id=1, source_target_pairs={{4,0},{5,1},{6,2},{7,3},{0,4},{1,5},{2,6},{3,7},{12,8},{13,9},{14,... | collective-permute-start | bytes 589832 | tf_op jit(solution)/shard_map/ppermute | solution.py:49
  24.5 15.0 %collective-permute-start.7 = (bf16[2,128,256]{2,1,0:T(8,128)(2,1)S(1)}, bf16[2,128,256]{2,1,0:T(8,128)(2,1)S(1)}, u32[]{:S(2)}, u32[]{:S(2)}) collective-permute-start(bf16[2,128,256]{2,1,0:T(8,128)(2,1)S(1)} %collective-permute-done.2.refs_7_.refs_1_), channel_id=1, source_target_pairs={{4,0},{5,1},{6,2},{7,3},{0,4},{1,5},{2,6},{3,7},{12,8},{13,9},{14,... | collective-permute-start | bytes 393224 | tf_op jit(solution)/shard_map/ppermute | solution.py:49
  39.5 6.0 %collective-permute-start.13 = (bf16[256,2048]{1,0:T(8,128)(2,1)S(1)}, bf16[256,2048]{1,0:T(8,128)(2,1)S(1)}, u32[]{:S(2)}, u32[]{:S(2)}) collective-permute-start(bf16[256,2048]{1,0:T(8,128)(2,1)S(1)} %hidden_acts.1.refs_0_), channel_id=1, source_target_pairs={{0,1},{1,0},{2,3},{3,2},{4,5},{5,4},{6,7},{7,6},{8,9},{9,8},{10,11... | collective-permute-start | bytes 3145736 | tf_op jit(solution)/shard_map/ppermute | solution.py:44
  39.6 6.5 %collective-permute-start.14 = (bf16[256,2048]{1,0:T(8,128)(2,1)S(1)}, bf16[256,2048]{1,0:T(8,128)(2,1)S(1)}, u32[]{:S(2)}, u32[]{:S(2)}) collective-permute-start(bf16[256,2048]{1,0:T(8,128)(2,1)S(1)} %collective-permute-done.4.refs_2_), channel_id=1, source_target_pairs={{0,1},{1,0},{2,3},{3,2},{4,5},{5,4},{6,7},{7,6},{8,9},{9,8},{10,11... | collective-permute-start | bytes 3145736 | tf_op jit(solution)/shard_map/ppermute | solution.py:44
  40.1 3.9 %collective-permute-start.18 = (bf16[2,128,384]{2,1,0:T(8,128)(2,1)S(1)}, bf16[2,128,384]{2,1,0:T(8,128)(2,1)S(1)}, u32[]{:S(2)}, u32[]{:S(2)}) collective-permute-start(bf16[2,128,384]{2,1,0:T(8,128)(2,1)S(1)} %get-tuple-element.107), channel_id=1, source_target_pairs={{0,1},{1,0},{2,3},{3,2},{4,5},{5,4},{6,7},{7,6},{8,9},{9,8},{10,11... | collective-permute-start | bytes 589832 | tf_op jit(solution)/shard_map/ppermute | solution.py:44
  40.2 10.3 %collective-permute-start.12 = (bf16[2,128,384]{2,1,0:T(8,128)(2,1)S(1)}, bf16[2,128,384]{2,1,0:T(8,128)(2,1)S(1)}, u32[]{:S(2)}, u32[]{:S(2)}) collective-permute-start(bf16[2,128,384]{2,1,0:T(8,128)(2,1)S(1)} %get-tuple-element.59), channel_id=1, source_target_pairs={{0,2},{1,3},{2,0},{3,1},{4,6},{5,7},{6,4},{7,5},{8,10},{9,11},{10,... | collective-permute-start | bytes 589832 | tf_op jit(solution)/shard_map/ppermute | solution.py:44
  40.7 12.9 %collective-permute-start.16 = (bf16[2,128,384]{2,1,0:T(8,128)(2,1)S(1)}, bf16[2,128,384]{2,1,0:T(8,128)(2,1)S(1)}, u32[]{:S(2)}, u32[]{:S(2)}) collective-permute-start(bf16[2,128,384]{2,1,0:T(8,128)(2,1)S(1)} %get-tuple-element.63), channel_id=1, source_target_pairs={{0,3},{1,2},{2,1},{3,0},{4,7},{5,6},{6,5},{7,4},{8,11},{9,10},{10,... | collective-permute-start | bytes 589832 | tf_op jit(solution)/shard_map/ppermute | solution.py:44
  44.0 10.1 %collective-permute-start.19 = (bf16[2,128,384]{2,1,0:T(8,128)(2,1)S(1)}, bf16[2,128,384]{2,1,0:T(8,128)(2,1)S(1)}, u32[]{:S(2)}, u32[]{:S(2)}) collective-permute-start(bf16[2,128,384]{2,1,0:T(8,128)(2,1)S(1)} %collective-permute-done.18.refs_5_.refs_7_), channel_id=1, source_target_pairs={{4,0},{5,1},{6,2},{7,3},{0,4},{1,5},{2,6},{3,7},{12,8},{13,9},{14,... | collective-permute-start | bytes 589832 | tf_op jit(solution)/shard_map/ppermute | solution.py:49
  45.6 10.4 %collective-permute-start.20 = (bf16[2,128,384]{2,1,0:T(8,128)(2,1)S(1)}, bf16[2,128,384]{2,1,0:T(8,128)(2,1)S(1)}, u32[]{:S(2)}, u32[]{:S(2)}) collective-permute-start(bf16[2,128,384]{2,1,0:T(8,128)(2,1)S(1)} %get-tuple-element.66.refs_4_.refs_8_), channel_id=1, source_target_pairs={{4,0},{5,1},{6,2},{7,3},{0,4},{1,5},{2,6},{3,7},{12,8},{13,9},{14,... | collective-permute-start | bytes 589832 | tf_op jit(solution)/shard_map/ppermute | solution.py:49
  48.8 78.8 %copy-start = (bf16[256,2048]{1,0:T(8,128)(2,1)}, bf16[256,2048]{1,0:T(8,128)(2,1)S(1)}, u32[]{:S(2)}) copy-start(bf16[256,2048]{1,0:T(8,128)(2,1)S(1)} %collective-permute-done.14.refs_3_) | copy-start | bytes 3145732
  50.5 9.7 %collective-permute-start.15 = (bf16[2,128,384]{2,1,0:T(8,128)(2,1)S(1)}, bf16[2,128,384]{2,1,0:T(8,128)(2,1)S(1)}, u32[]{:S(2)}, u32[]{:S(2)}) collective-permute-start(bf16[2,128,384]{2,1,0:T(8,128)(2,1)S(1)} %collective-permute-done.12.refs_6_.refs_12_), channel_id=1, source_target_pairs={{4,0},{5,1},{6,2},{7,3},{0,4},{1,5},{2,6},{3,7},{12,8},{13,9},{14,... | collective-permute-start | bytes 589832 | tf_op jit(solution)/shard_map/ppermute | solution.py:49
  52.1 14.1 %collective-permute-start.21 = (bf16[512,256]{1,0:T(8,128)(2,1)S(1)}, bf16[512,256]{1,0:T(8,128)(2,1)S(1)}, u32[]{:S(2)}, u32[]{:S(2)}) collective-permute-start(bf16[512,256]{1,0:T(8,128)(2,1)S(1)} %given_half.5), channel_id=1, source_target_pairs={{0,24},{8,16},{16,8},{24,0},{1,25},{9,17},{17,9},{25,1},{2,26},{10... | collective-permute-start | bytes 786440 | tf_op jit(solution)/shard_map/ppermute | solution.py:54
  53.7 10.0 %collective-permute-start.17 = (bf16[2,128,384]{2,1,0:T(8,128)(2,1)S(1)}, bf16[2,128,384]{2,1,0:T(8,128)(2,1)S(1)}, u32[]{:S(2)}, u32[]{:S(2)}) collective-permute-start(bf16[2,128,384]{2,1,0:T(8,128)(2,1)S(1)} %collective-permute-done.16.refs_7_.refs_13_), channel_id=1, source_target_pairs={{4,0},{5,1},{6,2},{7,3},{0,4},{1,5},{2,6},{3,7},{12,8},{13,9},{14,... | collective-permute-start | bytes 589832 | tf_op jit(solution)/shard_map/ppermute | solution.py:49
  54.2 12.0 %collective-permute-start.22 = (bf16[2,128,384]{2,1,0:T(8,128)(2,1)S(1)}, bf16[2,128,384]{2,1,0:T(8,128)(2,1)S(1)}, u32[]{:S(2)}, u32[]{:S(2)}) collective-permute-start(bf16[2,128,384]{2,1,0:T(8,128)(2,1)S(1)} %get-tuple-element.68), channel_id=1, source_target_pairs={{0,2},{1,3},{2,0},{3,1},{4,6},{5,7},{6,4},{7,5},{8,10},{9,11},{10,... | collective-permute-start | bytes 589832 | tf_op jit(solution)/shard_map/ppermute | solution.py:44
  56.0 75.0 %copy-start.16 = (bf16[2,128,384]{2,1,0:T(8,128)(2,1)}, bf16[2,128,384]{2,1,0:T(8,128)(2,1)S(1)}, u32[]{:S(2)}) copy-start(bf16[2,128,384]{2,1,0:T(8,128)(2,1)S(1)} %collective-permute-done.20.refs_8_) | copy-start | bytes 589828
  56.0 10.2 %collective-permute-start.23 = (bf16[2,128,384]{2,1,0:T(8,128)(2,1)S(1)}, bf16[2,128,384]{2,1,0:T(8,128)(2,1)S(1)}, u32[]{:S(2)}, u32[]{:S(2)}) collective-permute-start(bf16[2,128,384]{2,1,0:T(8,128)(2,1)S(1)} %get-tuple-element.69), channel_id=1, source_target_pairs={{0,3},{1,2},{2,1},{3,0},{4,7},{5,6},{6,5},{7,4},{8,11},{9,10},{10,... | collective-permute-start | bytes 589832 | tf_op jit(solution)/shard_map/ppermute | solution.py:44
  60.2 20.9 %copy-start.50 = (bf16[2,128,256]{2,1,0:T(8,128)(2,1)S(1)}, bf16[2,128,256]{2,1,0:T(8,128)(2,1)}, u32[]{:S(2)}) copy-start(bf16[2,128,256]{2,1,0:T(8,128)(2,1)} %copy-done.48) | copy-start | bytes 393220
  60.2 20.9 %copy-start.53 = (bf16[2,128,256]{2,1,0:T(8,128)(2,1)S(1)}, bf16[2,128,256]{2,1,0:T(8,128)(2,1)}, u32[]{:S(2)}) copy-start(bf16[2,128,256]{2,1,0:T(8,128)(2,1)} %copy-done.51) | copy-start | bytes 393220
  60.2 10.2 %collective-permute-start.28 = (bf16[2,128,384]{2,1,0:T(8,128)(2,1)S(1)}, bf16[2,128,384]{2,1,0:T(8,128)(2,1)S(1)}, u32[]{:S(2)}, u32[]{:S(2)}) collective-permute-start(bf16[2,128,384]{2,1,0:T(8,128)(2,1)S(1)} %get-tuple-element.102), channel_id=1, source_target_pairs={{0,1},{1,0},{2,3},{3,2},{4,5},{5,4},{6,7},{7,6},{8,9},{9,8},{10,11... | collective-permute-start | bytes 589832 | tf_op jit(solution)/shard_map/ppermute | solution.py:44
  66.2 6.2 %collective-permute-start.24 = (bf16[2,128,384]{2,1,0:T(8,128)(2,1)S(1)}, bf16[2,128,384]{2,1,0:T(8,128)(2,1)S(1)}, u32[]{:S(2)}, u32[]{:S(2)}) collective-permute-start(bf16[2,128,384]{2,1,0:T(8,128)(2,1)S(1)} %get-tuple-element.71), channel_id=1, source_target_pairs={{0,2},{1,3},{2,0},{3,1},{4,6},{5,7},{6,4},{7,5},{8,10},{9,11},{10,... | collective-permute-start | bytes 589832 | tf_op jit(solution)/shard_map/ppermute | solution.py:44
  66.8 7.8 %collective-permute-start.26 = (bf16[2,128,384]{2,1,0:T(8,128)(2,1)S(1)}, bf16[2,128,384]{2,1,0:T(8,128)(2,1)S(1)}, u32[]{:S(2)}, u32[]{:S(2)}) collective-permute-start(bf16[2,128,384]{2,1,0:T(8,128)(2,1)S(1)} %collective-permute-done.22.refs_6_.refs_14_), channel_id=1, source_target_pairs={{4,0},{5,1},{6,2},{7,3},{0,4},{1,5},{2,6},{3,7},{12,8},{13,9},{14,... | collective-permute-start | bytes 589832 | tf_op jit(solution)/shard_map/ppermute | solution.py:49
  68.3 10.5 %collective-permute-start.27 = (bf16[2,128,384]{2,1,0:T(8,128)(2,1)S(1)}, bf16[2,128,384]{2,1,0:T(8,128)(2,1)S(1)}, u32[]{:S(2)}, u32[]{:S(2)}) collective-permute-start(bf16[2,128,384]{2,1,0:T(8,128)(2,1)S(1)} %collective-permute-done.23.refs_7_.refs_15_), channel_id=1, source_target_pairs={{4,0},{5,1},{6,2},{7,3},{0,4},{1,5},{2,6},{3,7},{12,8},{13,9},{14,... | collective-permute-start | bytes 589832 | tf_op jit(solution)/shard_map/ppermute | solution.py:49
  68.8 17.9 %collective-permute-start.30 = (bf16[512,384]{1,0:T(8,128)(2,1)S(1)}, bf16[512,384]{1,0:T(8,128)(2,1)S(1)}, u32[]{:S(2)}, u32[]{:S(2)}) collective-permute-start(bf16[512,384]{1,0:T(8,128)(2,1)S(1)} %given_half.6), channel_id=1, source_target_pairs={{0,24},{8,16},{16,8},{24,0},{1,25},{9,17},{17,9},{25,1},{2,26},{10... | collective-permute-start | bytes 1179656 | tf_op jit(solution)/shard_map/ppermute | solution.py:54
  70.4 38.1 %copy-start.20 = (bf16[2,128,384]{2,1,0:T(8,128)(2,1)}, bf16[2,128,384]{2,1,0:T(8,128)(2,1)S(1)}, u32[]{:S(2)}) copy-start(bf16[2,128,384]{2,1,0:T(8,128)(2,1)S(1)} %collective-permute-done.28.refs_5_.refs_9_) | copy-start | bytes 589828
  70.4 10.7 %collective-permute-start.29 = (bf16[2,128,384]{2,1,0:T(8,128)(2,1)S(1)}, bf16[2,128,384]{2,1,0:T(8,128)(2,1)S(1)}, u32[]{:S(2)}, u32[]{:S(2)}) collective-permute-start(bf16[2,128,384]{2,1,0:T(8,128)(2,1)S(1)} %collective-permute-done.28.refs_5_.refs_9_), channel_id=1, source_target_pairs={{4,0},{5,1},{6,2},{7,3},{0,4},{1,5},{2,6},{3,7},{12,8},{13,9},{14,... | collective-permute-start | bytes 589832 | tf_op jit(solution)/shard_map/ppermute | solution.py:49
  72.4 55.2 %copy-start.18 = (bf16[2,128,384]{2,1,0:T(8,128)(2,1)}, bf16[2,128,384]{2,1,0:T(8,128)(2,1)S(1)}, u32[]{:S(2)}) copy-start(bf16[2,128,384]{2,1,0:T(8,128)(2,1)S(1)} %collective-permute-done.24.refs_6_.refs_18_) | copy-start | bytes 589828
  72.4 13.7 %collective-permute-start.25 = (bf16[2,128,384]{2,1,0:T(8,128)(2,1)S(1)}, bf16[2,128,384]{2,1,0:T(8,128)(2,1)S(1)}, u32[]{:S(2)}, u32[]{:S(2)}) collective-permute-start(bf16[2,128,384]{2,1,0:T(8,128)(2,1)S(1)} %get-tuple-element.72), channel_id=1, source_target_pairs={{0,2},{1,3},{2,0},{3,1},{4,6},{5,7},{6,4},{7,5},{8,10},{9,11},{10,... | collective-permute-start | bytes 589832 | tf_op jit(solution)/shard_map/ppermute | solution.py:44
  74.6 11.5 %collective-permute-start.31 = (bf16[2,128,384]{2,1,0:T(8,128)(2,1)S(1)}, bf16[2,128,384]{2,1,0:T(8,128)(2,1)S(1)}, u32[]{:S(2)}, u32[]{:S(2)}) collective-permute-start(bf16[2,128,384]{2,1,0:T(8,128)(2,1)S(1)} %get-tuple-element.77), channel_id=1, source_target_pairs={{0,3},{1,2},{2,1},{3,0},{4,7},{5,6},{6,5},{7,4},{8,11},{9,10},{10,... | collective-permute-start | bytes 589832 | tf_op jit(solution)/shard_map/ppermute | solution.py:44
  78.9 7.3 %collective-permute-start.32 = (bf16[2,128,384]{2,1,0:T(8,128)(2,1)S(1)}, bf16[2,128,384]{2,1,0:T(8,128)(2,1)S(1)}, u32[]{:S(2)}, u32[]{:S(2)}) collective-permute-start(bf16[2,128,384]{2,1,0:T(8,128)(2,1)S(1)} %get-tuple-element.78), channel_id=1, source_target_pairs={{0,3},{1,2},{2,1},{3,0},{4,7},{5,6},{6,5},{7,4},{8,11},{9,10},{10,... | collective-permute-start | bytes 589832 | tf_op jit(solution)/shard_map/ppermute | solution.py:44
  81.1 49.9 %copy-start.26 = (bf16[2,128,384]{2,1,0:T(8,128)(2,1)}, bf16[2,128,384]{2,1,0:T(8,128)(2,1)S(1)}, u32[]{:S(2)}) copy-start(bf16[2,128,384]{2,1,0:T(8,128)(2,1)S(1)} %collective-permute-done.29.refs_9_.refs_13_) | copy-start | bytes 589828
  81.1 5.7 %collective-permute-start.39 = (bf16[2,128,384]{2,1,0:T(8,128)(2,1)S(1)}, bf16[2,128,384]{2,1,0:T(8,128)(2,1)S(1)}, u32[]{:S(2)}, u32[]{:S(2)}) collective-permute-start(bf16[2,128,384]{2,1,0:T(8,128)(2,1)S(1)} %get-tuple-element.98), channel_id=1, source_target_pairs={{0,1},{1,0},{2,3},{3,2},{4,5},{5,4},{6,7},{7,6},{8,9},{9,8},{10,11... | collective-permute-start | bytes 589832 | tf_op jit(solution)/shard_map/ppermute | solution.py:44
  86.1 22.4 %copy-start.28 = (bf16[2,128,384]{2,1,0:T(8,128)(2,1)}, bf16[2,128,384]{2,1,0:T(8,128)(2,1)S(1)}, u32[]{:S(2)}) copy-start(bf16[2,128,384]{2,1,0:T(8,128)(2,1)S(1)} %collective-permute-done.25.refs_6_.refs_16_) | copy-start | bytes 589828
  86.1 22.4 %copy-start.30 = (bf16[2,128,384]{2,1,0:T(8,128)(2,1)}, bf16[2,128,384]{2,1,0:T(8,128)(2,1)S(1)}, u32[]{:S(2)}) copy-start(bf16[2,128,384]{2,1,0:T(8,128)(2,1)S(1)} %collective-permute-done.31.refs_7_.refs_17_) | copy-start | bytes 589828
  86.1 41.5 %copy-start.22 = (bf16[2,128,384]{2,1,0:T(8,128)(2,1)}, bf16[2,128,384]{2,1,0:T(8,128)(2,1)S(1)}, u32[]{:S(2)}) copy-start(bf16[2,128,384]{2,1,0:T(8,128)(2,1)S(1)} %collective-permute-done.32.refs_7_.refs_19_) | copy-start | bytes 589828
  86.7 40.9 %copy-start.24 = (bf16[2,128,384]{2,1,0:T(8,128)(2,1)}, bf16[2,128,384]{2,1,0:T(8,128)(2,1)S(1)}, u32[]{:S(2)}) copy-start(bf16[2,128,384]{2,1,0:T(8,128)(2,1)S(1)} %collective-permute-done.39.refs_5_.refs_11_) | copy-start | bytes 589828
  91.4 10.5 %copy-start.6 = (f32[2,1024,256]{2,1,0:T(8,128)}, f32[2,1024,256]{2,1,0:T(8,128)S(1)}, u32[]{:S(2)}) copy-start(f32[2,1024,256]{2,1,0:T(8,128)S(1)} %get-tuple-element.93.keep_ref) | copy-start | bytes 6291460
  91.4 5.2 %collective-permute-start.42 = (bf16[2,1024,256]{2,1,0:T(8,128)(2,1)S(1)}, bf16[2,1024,256]{2,1,0:T(8,128)(2,1)S(1)}, u32[]{:S(2)}, u32[]{:S(2)}) collective-permute-start(bf16[2,1024,256]{2,1,0:T(8,128)(2,1)S(1)} %get-tuple-element.94), channel_id=1, source_target_pairs={{0,1},{1,0},{2,3},{3,2},{4,5},{5,4},{6,7},{7,6},{8,9},{9,8},{10,11... | collective-permute-start | bytes 3145736 | tf_op jit(solution)/shard_map/ppermute | solution.py:44
  91.4 20.0 %collective-permute-start.36 = (bf16[512,384]{1,0:T(8,128)(2,1)S(1)}, bf16[512,384]{1,0:T(8,128)(2,1)S(1)}, u32[]{:S(2)}, u32[]{:S(2)}) collective-permute-start(bf16[512,384]{1,0:T(8,128)(2,1)S(1)} %given_half.7), channel_id=1, source_target_pairs={{0,24},{8,16},{16,8},{24,0},{1,25},{9,17},{17,9},{25,1},{2,26},{10... | collective-permute-start | bytes 1179656 | tf_op jit(solution)/shard_map/ppermute | solution.py:54
  93.1 8.8 %collective-permute-start.33 = (bf16[2,128,384]{2,1,0:T(8,128)(2,1)S(1)}, bf16[2,128,384]{2,1,0:T(8,128)(2,1)S(1)}, u32[]{:S(2)}, u32[]{:S(2)}) collective-permute-start(bf16[2,128,384]{2,1,0:T(8,128)(2,1)S(1)} %collective-permute-done.25.refs_6_.refs_16_), channel_id=1, source_target_pairs={{4,0},{5,1},{6,2},{7,3},{0,4},{1,5},{2,6},{3,7},{12,8},{13,9},{14,... | collective-permute-start | bytes 589832 | tf_op jit(solution)/shard_map/ppermute | solution.py:49
  94.6 10.5 %collective-permute-start.34 = (bf16[2,128,384]{2,1,0:T(8,128)(2,1)S(1)}, bf16[2,128,384]{2,1,0:T(8,128)(2,1)S(1)}, u32[]{:S(2)}, u32[]{:S(2)}) collective-permute-start(bf16[2,128,384]{2,1,0:T(8,128)(2,1)S(1)} %collective-permute-done.31.refs_7_.refs_17_), channel_id=1, source_target_pairs={{4,0},{5,1},{6,2},{7,3},{0,4},{1,5},{2,6},{3,7},{12,8},{13,9},{14,... | collective-permute-start | bytes 589832 | tf_op jit(solution)/shard_map/ppermute | solution.py:49
  95.1 13.4 %collective-permute-start.35 = (bf16[2,128,384]{2,1,0:T(8,128)(2,1)S(1)}, bf16[2,128,384]{2,1,0:T(8,128)(2,1)S(1)}, u32[]{:S(2)}, u32[]{:S(2)}) collective-permute-start(bf16[2,128,384]{2,1,0:T(8,128)(2,1)S(1)} %get-tuple-element.82.refs_4_.refs_10_), channel_id=1, source_target_pairs={{4,0},{5,1},{6,2},{7,3},{0,4},{1,5},{2,6},{3,7},{12,8},{13,9},{14,... | collective-permute-start | bytes 589832 | tf_op jit(solution)/shard_map/ppermute | solution.py:49
  96.8 38.9 %collective-permute-start.43 = (bf16[1024,256]{1,0:T(8,128)(2,1)S(1)}, bf16[1024,256]{1,0:T(8,128)(2,1)S(1)}, u32[]{:S(2)}, u32[]{:S(2)}) collective-permute-start(bf16[1024,256]{1,0:T(8,128)(2,1)S(1)} %fusion), channel_id=1, source_target_pairs={{0,2},{1,3},{2,0},{3,1},{4,6},{5,7},{6,4},{7,5},{8,10},{9,11},{10,... | collective-permute-start | bytes 1572872 | tf_op jit(solution)/shard_map/ppermute | solution.py:44
  101.8 29.1 %copy-start.34 = (bf16[2,128,384]{2,1,0:T(8,128)(2,1)}, bf16[2,128,384]{2,1,0:T(8,128)(2,1)S(1)}, u32[]{:S(2)}) copy-start(bf16[2,128,384]{2,1,0:T(8,128)(2,1)S(1)} %collective-permute-done.33.refs_10_.refs_14_) | copy-start | bytes 589828
  105.0 26.0 %copy-start.36 = (bf16[2,128,384]{2,1,0:T(8,128)(2,1)}, bf16[2,128,384]{2,1,0:T(8,128)(2,1)S(1)}, u32[]{:S(2)}) copy-start(bf16[2,128,384]{2,1,0:T(8,128)(2,1)S(1)} %collective-permute-done.34.refs_11_.refs_15_) | copy-start | bytes 589828
  108.5 22.5 %copy-start.32 = (bf16[2,128,384]{2,1,0:T(8,128)(2,1)}, bf16[2,128,384]{2,1,0:T(8,128)(2,1)S(1)}, u32[]{:S(2)}) copy-start(bf16[2,128,384]{2,1,0:T(8,128)(2,1)S(1)} %collective-permute-done.35.refs_8_.refs_16_) | copy-start | bytes 589828
  111.4 24.2 %collective-permute-start.41 = (bf16[512,384]{1,0:T(8,128)(2,1)S(1)}, bf16[512,384]{1,0:T(8,128)(2,1)S(1)}, u32[]{:S(2)}, u32[]{:S(2)}) collective-permute-start(bf16[512,384]{1,0:T(8,128)(2,1)S(1)} %given_half.8), channel_id=1, source_target_pairs={{0,24},{8,16},{16,8},{24,0},{1,25},{9,17},{17,9},{25,1},{2,26},{10... | collective-permute-start | bytes 1179656 | tf_op jit(solution)/shard_map/ppermute | solution.py:54
  113.0 7.8 %collective-permute-start.37 = (bf16[2,128,384]{2,1,0:T(8,128)(2,1)S(1)}, bf16[2,128,384]{2,1,0:T(8,128)(2,1)S(1)}, u32[]{:S(2)}, u32[]{:S(2)}) collective-permute-start(bf16[2,128,384]{2,1,0:T(8,128)(2,1)S(1)} %collective-permute-done.24.refs_6_.refs_18_), channel_id=1, source_target_pairs={{4,0},{5,1},{6,2},{7,3},{0,4},{1,5},{2,6},{3,7},{12,8},{13,9},{14,... | collective-permute-start | bytes 589832 | tf_op jit(solution)/shard_map/ppermute | solution.py:49
  114.5 10.6 %collective-permute-start.38 = (bf16[2,128,384]{2,1,0:T(8,128)(2,1)S(1)}, bf16[2,128,384]{2,1,0:T(8,128)(2,1)S(1)}, u32[]{:S(2)}, u32[]{:S(2)}) collective-permute-start(bf16[2,128,384]{2,1,0:T(8,128)(2,1)S(1)} %collective-permute-done.32.refs_7_.refs_19_), channel_id=1, source_target_pairs={{4,0},{5,1},{6,2},{7,3},{0,4},{1,5},{2,6},{3,7},{12,8},{13,9},{14,... | collective-permute-start | bytes 589832 | tf_op jit(solution)/shard_map/ppermute | solution.py:49
  115.0 12.6 %collective-permute-start.40 = (bf16[2,128,384]{2,1,0:T(8,128)(2,1)S(1)}, bf16[2,128,384]{2,1,0:T(8,128)(2,1)S(1)}, u32[]{:S(2)}, u32[]{:S(2)}) collective-permute-start(bf16[2,128,384]{2,1,0:T(8,128)(2,1)S(1)} %collective-permute-done.39.refs_5_.refs_11_), channel_id=1, source_target_pairs={{4,0},{5,1},{6,2},{7,3},{0,4},{1,5},{2,6},{3,7},{12,8},{13,9},{14,... | collective-permute-start | bytes 589832 | tf_op jit(solution)/shard_map/ppermute | solution.py:49
  135.7 2.7 %collective-permute-start.44 = (bf16[2,1024,256]{2,1,0:T(8,128)(2,1)S(1)}, bf16[2,1024,256]{2,1,0:T(8,128)(2,1)S(1)}, u32[]{:S(2)}, u32[]{:S(2)}) collective-permute-start(bf16[2,1024,256]{2,1,0:T(8,128)(2,1)S(1)} %get-tuple-element.96), channel_id=1, source_target_pairs={{0,1},{1,0},{2,3},{3,2},{4,5},{5,4},{6,7},{7,6},{8,9},{9,8},{10,11... | collective-permute-start | bytes 3145736 | tf_op jit(solution)/shard_map/ppermute | solution.py:44
  140.9 16.2 %collective-permute-start.45 = (bf16[1024,256]{1,0:T(8,128)(2,1)}, bf16[1024,256]{1,0:T(8,128)(2,1)}, u32[]{:S(2)}, u32[]{:S(2)}) collective-permute-start(bf16[1024,256]{1,0:T(8,128)(2,1)} %fusion.1), channel_id=1, source_target_pairs={{0,2},{1,3},{2,0},{3,1},{4,6},{5,7},{6,4},{7,5},{8,10},{9,11},{10,... | collective-permute-start | bytes 1572872 | tf_op jit(solution)/shard_map/ppermute | solution.py:44
  142.4 19.6 %collective-permute-start.46 = (bf16[512,384]{1,0:T(8,128)(2,1)}, bf16[512,384]{1,0:T(8,128)(2,1)}, u32[]{:S(2)}, u32[]{:S(2)}) collective-permute-start(bf16[512,384]{1,0:T(8,128)(2,1)} %given_half.9), channel_id=1, source_target_pairs={{0,24},{8,16},{16,8},{24,0},{1,25},{9,17},{17,9},{25,1},{2,26},{10... | collective-permute-start | bytes 1179656 | tf_op jit(solution)/shard_map/ppermute | solution.py:54
  (41 other events, 123.9 us)

commit v3 on v2

--- a/solution.py
+++ b/solution.py
@@ -9,14 +9,15 @@
 
 TILE = 128
 GROUP = 4
-VMEM_BYTES = 40 * 1024 * 1024
+VMEM_BYTES = 17 * 1024 * 1024
+LARGE_VMEM_BYTES = 60 * 1024 * 1024
 ANY = pl.BlockSpec(memory_space=pltpu.MemorySpace.HBM)
 SMEM = pl.BlockSpec(memory_space=pltpu.SMEM)
 VMEM = pl.BlockSpec(memory_space=pltpu.VMEM)
 
 
-def params():
-    return pltpu.CompilerParams(vmem_limit_bytes=VMEM_BYTES)
+def params(limit=VMEM_BYTES):
+    return pltpu.CompilerParams(vmem_limit_bytes=limit)
 
 
 def cost(flops, nbytes):
@@ -215,6 +216,54 @@
     copy.wait()
 
 
+def dot_kernel(offsets, *refs):
+    after_pieces = GROUP + len(offsets) + 1
+    out_ref = refs[after_pieces]
+    out_ref[...] = half_grad(False, refs, offsets, *refs[after_pieces + 1 :])
+
+
+def kept_dot(hidden_all, placed, width, gate):
+    units = hidden_all[0].shape[0]
+    pieces, offsets = zip(*placed)
+    return pl.pallas_call(
+        functools.partial(dot_kernel, offsets),
+        out_shape=jax.ShapeDtypeStruct((2 * units, width), jnp.float32),
+        in_specs=[ANY] * (GROUP + len(pieces) + 1),
+        out_specs=VMEM,
+        scratch_shapes=scratches(hidden_all, pieces, width),
+        compiler_params=params(),
+        cost_estimate=grad_cost(hidden_all, width),
+        name="kept_dot",
+    )(*hidden_all, *pieces, gate)
+
+
+def add_kernel(offset, parts, dot_ref, *refs):
+    out_ref, scratch, sem = refs[parts + 1 :]
+    rows = scratch.shape[0] // parts
+    for i in range(parts):
+        part = pl.ds(i * rows, rows)
+        total = dot_ref[part, :] + refs[i][...].astype(jnp.float32)
+        scratch[part, :] = total.astype(scratch.dtype)
+    width = scratch.shape[1]
+    copy = pltpu.make_async_copy(scratch, out_ref.at[:, pl.ds(offset, width)], sem)
+    copy.start()
+    copy.wait()
+
+
+def kept_add(dot, partners, total, offset):
+    return pl.pallas_call(
+        functools.partial(add_kernel, offset, len(partners)),
+        out_shape=jax.ShapeDtypeStruct(total.shape, total.dtype),
+        in_specs=[VMEM] * (1 + len(partners)) + [ANY],
+        out_specs=ANY,
+        scratch_shapes=[pltpu.VMEM(dot.shape, total.dtype), pltpu.SemaphoreType.DMA],
+        input_output_aliases={1 + len(partners): 0},
+        compiler_params=params(),
+        cost_estimate=cost(dot.size, dot.size * 8),
+        name="kept_add",
+    )(dot, *partners, total)
+
+
 def kept_half(hidden_all, placed, partner, total, offset, full_width):
     units = hidden_all[0].shape[0]
     width = partner.shape[1]
@@ -243,7 +292,7 @@
 def partial_kernel(places, *refs):
     pieces = len(places)
     piece_refs, weight_ref = refs[:pieces], refs[pieces]
-    keep_ref, send_ref, token_scratch, sems = refs[pieces + 1 :]
+    keep_ref, self_ref, *other_refs, token_scratch, sems = refs[pieces + 1 :]
     _, quarter = place()
     copies = []
     for i, (mask, offset) in enumerate(places):
@@ -257,14 +306,22 @@
     rows = keep_ref.shape[1]
     units = keep_ref.shape[2]
     tokens = token_scratch[...].reshape(rows, token_scratch.shape[3])
-    for mask, out_ref, place_in in ((3, send_ref, 1), (2, keep_ref, 1), (1, send_ref, 0), (0, keep_ref, 0)):
+    for mask in (3, 2, 1, 0):
         start = pl.multiple_of((quarter ^ mask) * units, units)
-        out_ref[place_in] = lax.dot_general(
+        total = lax.dot_general(
             tokens,
             weight_ref[pl.ds(start, units), :],
             (((1,), (1,)), ((), ())),
             preferred_element_type=jnp.float32,
-        ).astype(out_ref.dtype)
+        )
+        if mask == 3:
+            for i, other_ref in enumerate(other_refs):
+                part = other_ref.shape[0]
+                other_ref[...] = total[i * part : (i + 1) * part].astype(other_ref.dtype)
+        elif mask == 1:
+            self_ref[...] = total.astype(self_ref.dtype)
+        else:
+            keep_ref[mask // 2] = total
 
 
 def partial_grads(pieces, places, weight):
@@ -276,10 +333,11 @@
         functools.partial(partial_kernel, places),
         out_shape=(
             jax.ShapeDtypeStruct((2, rows, units), jnp.float32),
-            jax.ShapeDtypeStruct((2, rows, units), jnp.bfloat16),
+            jax.ShapeDtypeStruct((rows, units), jnp.bfloat16),
+            *[jax.ShapeDtypeStruct((rows // micros, units), jnp.bfloat16)] * micros,
         ),
         in_specs=[ANY] * len(pieces) + [VMEM],
-        out_specs=(VMEM, VMEM),
+        out_specs=(VMEM,) * (2 + micros),
         scratch_shapes=[
             pltpu.VMEM((micros, GROUP, block_rows, width), jnp.bfloat16),
             pltpu.SemaphoreType.DMA((len(pieces),)),
@@ -290,9 +348,10 @@
     )(*pieces, weight)
 
 
-def store_kernel(first, route_ref, group_ref, stored_ref, keep_ref, core_ref, across_ref, *refs):
+def store_kernel(first, route_ref, group_ref, stored_ref, keep_ref, core_ref, *refs):
     out_ref, scratch, zeros, sems, zero_sems = refs[-5:]
     micros, ranks = route_ref.shape[0], route_ref.shape[1]
+    across_refs = refs[:micros]
     expert, _ = place()
     source = group_ref[0]
     block_rows = scratch.shape[2]
@@ -327,8 +386,8 @@
                 rows = pl.ds((micro * GROUP + member) * block_rows, block_rows)
                 grad = (
                     keep_ref[0, rows, :]
-                    + core_ref[0, rows, :].astype(jnp.float32)
-                    + across_ref[rows, :].astype(jnp.float32)
+                    + core_ref[rows, :].astype(jnp.float32)
+                    + across_refs[micro][member * block_rows : (member + 1) * block_rows, :].astype(jnp.float32)
                 )
                 pre = stored_ref[micro, pl.ds(pl.multiple_of(slot * block_rows, block_rows), block_rows), :]
                 gate = pre[:, :hidden].astype(jnp.float32)
@@ -348,13 +407,13 @@
 
 def store_grads(route, group, stored, keep, core, across, total):
     micros = stored.shape[0]
-    rows, units = across.shape
+    rows, units = core.shape
     block_rows = rows // (micros * GROUP)
     slots = stored.shape[1] // block_rows
     half = pl.BlockSpec((1, rows, units), lambda i: (0, 0, 0))
-    operands = [route, group.reshape(1), stored, keep, core, across]
-    whole = [pl.BlockSpec(v.shape, lambda i, n=v.ndim: (0,) * n) for v in (stored, across)]
-    specs = [SMEM, SMEM, whole[0], half, half, whole[1]]
+    operands = [route, group.reshape(1), stored, keep, core, *across]
+    whole = [pl.BlockSpec(v.shape, lambda i, n=v.ndim: (0,) * n) for v in (stored, core, *across)]
+    specs = [SMEM, SMEM, whole[0], half, *whole[1:]]
     aliases = {}
     if total is not None:
         aliases = {len(operands): 0}
@@ -432,10 +491,17 @@
         places, pieces = zip(*found)
         return partial_grads((after(pieces[0], gate), *pieces[1:]), places, weight)
 
-    def group_sum(keep, send):
-        core = swap(send, 1)
-        across = swap((keep[1] + core[1].astype(jnp.float32)).astype(jnp.bfloat16), 2)
-        return keep, core, across
+    def core_sum(keep, _, *others):
+        sums = []
+        for i, other in enumerate(others):
+            size = other.shape[0]
+            mine = lax.slice_in_dim(keep[1], i * size, (i + 1) * size)
+            sums.append((mine + swap(other, 1).astype(jnp.float32)).astype(jnp.bfloat16))
+        return sums
+
+    def chip_sum(parts, sums, gate):
+        own = swap(after(parts[1], gate), 1)
+        return parts[0], own, [swap(after(value, gate), 2) for value in sums]
 
     def store(step, sums, total):
         source = lax.rem(group + step, groups).astype(jnp.int32)
@@ -448,16 +514,17 @@
         return kept_half(hidden_all, placed(i), partners[i], total, chunks[i][0], quarter_width)
 
     narrow = chunks[0]
-    ready = exchange(narrow, (2, 3, 0, 1)) + cross(narrow, (0,))
+    ready = exchange(narrow, (2, 3, 1, 0)) + cross(narrow, (0, 1))
     hidden = hidden_acts(routes, saved_pre, block_rows)
     late_rows = after(grad_rows, inside[1, 0])
+    early = []
     for part in chunks[1:]:
-        exchange(part, (0, 1))
+        early += exchange(part, (0, 1))
     hidden = after(hidden, *ready)
     crossed = swap(hidden, 2)
-    ready = cross(narrow, (1, 2, 3), hidden) + cross(chunks[1], (0, 1), hidden)
+    ready = cross(narrow, (2, 3), hidden) + cross(chunks[1], (0, 1), hidden)
     ready += cross(chunks[2], (0,), hidden)
-    crossed = after(crossed, *ready)
+    crossed = after(crossed, *ready, *early)
     hidden_all = [hidden, swap(after(hidden, crossed), 1), crossed, swap(crossed, 1)]
     exchange(chunks[1], (2, 3), crossed)
     far = cross(chunks[2], (1,), crossed) + cross(chunks[3], (0,), crossed)
@@ -466,16 +533,18 @@
     weight_grad = None
     store_grad = None
     ready = []
-    later = []
-    own_sums = None
-    extra = {1: (3, 1), 2: (4, 0), 3: (4, 1)}
+    extra = {1: [(3, 1), (4, 0)], 2: [(4, 1)]}
+    rounds = [[1], [2], [3], [4]]
     for i in range(last):
         payload = after(halves[i], *ready)
         partners.append(mirror(payload))
-        arrived = cross(chunks[i + 1], (2, 3), payload)
-        if i in extra:
-            arrived += cross(chunks[extra[i][0]], (extra[i][1],), payload)
-        ready = arrived + [partners[i]]
+        arrived = []
+        for chunk in rounds[i]:
+            arrived += cross(chunks[chunk], (2, 3), payload)
+        more = []
+        for chunk, mask in extra.get(i, []):
+            more += cross(chunks[chunk], (mask,), payload)
+        ready = arrived + more + [partners[i]]
         if i == 0:
             arrived = arrived + far
             ready += exchange(chunks[2], (2, 3), payload)
@@ -486,20 +555,28 @@
             for part in chunks[3:]:
                 ready += exchange(part, (2, 3), payload)
         if i == last - 2:
-            own_sums = group_sum(*partial(0, payload))
+            own_parts = partial(0, payload)
+            ready += own_parts[2:]
+        if i + 1 == last:
+            arrived = arrived + more + [payload]
         halves.append(given(i + 1, after(hidden_all[0], *arrived)))
         if i == last - 1:
-            ready.append(own_sums[2])
-            later = [partial(step, halves[last]) for step in range(1, groups)]
-            ready += [sums[1] for sums in later]
+            own_sums = core_sum(*own_parts[:2], *[after(part, payload) for part in own_parts[2:]])
+            own_sums = chip_sum(own_parts, own_sums, own_sums[0])
+            ready += own_sums[2]
+            other_parts = [partial(step, halves[last]) for step in range(1, groups)]
+            ready += [part for parts in other_parts for part in parts[2:]]
     payload = after(halves[last], *ready)
-    partners.append(mirror(payload))
+    upper = mirror(payload[: payload.shape[0] // 2])
     weight_grad = kept(last - 1, weight_grad)
+    last_total = kept_dot(hidden_all, placed(last), chunks[last][1], payload)
+    lower = mirror(after(payload[payload.shape[0] // 2 :], upper, weight_grad, last_total))
     store_grad = store(0, own_sums, None)
-    for step, (keep, send) in enumerate(later, 1):
-        store_grad = store(step, group_sum(keep, after(send, payload)), store_grad)
-    partners[last] = after(partners[last], store_grad, weight_grad)
-    weight_grad = kept(last, weight_grad)
+    for step, parts in enumerate(other_parts, 1):
+        sums = core_sum(*parts[:2], *[after(part, payload) for part in parts[2:]])
+        store_grad = store(step, chip_sum(parts, sums, payload), store_grad)
+    upper = after(upper, store_grad)
+    weight_grad = kept_add(last_total, (upper, lower), weight_grad, chunks[last][0])
     return store_grad[None], weight_grad[None]
 
 

time: 169 us -> 155 us (0.917)
  local copies, waits for them, and re-layouts: 21.8 us -> 12.6 us
  waiting for transfers between devices: 55.3 us -> 47.4 us
  starting transfers between devices: 41.8 us -> 46.2 us
    ppermute x20, waiting for transfers between devices: 46 us -> 34.3 us  [from_group(): lax.ppermute(value, 'expert', [((i + step * GROUP) % size, i) for i in ra...]
    unnamed x116 -> x28, local copies, waits for them, and re-layouts: 17.4 us -> 7.47 us
    pallas_call x5 -> x4, Pallas kernels: 16.8 us -> 12.3 us  [kept_half(): pl.pallas_call(functools.partial(kept_kernel, offsets, offset, total is n...]
    ppermute x22 -> x28, starting transfers between devices: 11.6 us -> 15.5 us  [swap(): return lax.ppermute(value, 'expert', [(i, i ^ mask) for i in range(size)])]
    ppermute x22 -> x28, waiting for transfers between devices: 6.23 us -> 9.93 us  [swap(): return lax.ppermute(value, 'expert', [(i, i ^ mask) for i in range(size)])]
    pallas_call x0 -> x2, Pallas kernels: none -> 3.37 us  [the longest x1 2.53 us: kept_dot(): pl.pallas_call(functools.partial(dot_kernel, offsets), out_shape=jax.Shap...]
    ppermute x5 -> x6, starting transfers between devices: 6.8 us -> 9.05 us  [mirror(): return lax.ppermute(value, 'pipe', [(i, size - 1 - i) for i in range(size)])]
    ppermute x20, starting transfers between devices: 23.4 us -> 21.6 us  [from_group(): lax.ppermute(value, 'expert', [((i + step * GROUP) % size, i) for i in ra...]
  transfers between devices with their start and end apart: 47 -> 54, of which waited for: 21 -> 18; matrix products, arithmetic and copies ran while one was open for 2% -> 3% of each run, Pallas kernels for 22% -> 29%
where the time goes in v3:
time: 155 us; the launch traced here: 154 us
  waiting for transfers between devices  47.4 us (31%)
  starting transfers between devices  46.2 us (30%)
  Pallas kernels  45.4 us (29%)
  local copies, waits for them, and re-layouts  12.6 us (8%)
    ppermute x20, waiting for transfers between devices, from_group(): lax.ppermute(value, 'expert', [((i + step * GROUP) % size, i) for i in ra...  34.3 us
    ppermute x20, starting transfers between devices, from_group(): lax.ppermute(value, 'expert', [((i + step * GROUP) % size, i) for i in ra...  21.6 us
    ppermute x28, starting transfers between devices, swap(): return lax.ppermute(value, 'expert', [(i, i ^ mask) for i in range(size)])  15.5 us
    pallas_call x4, Pallas kernels, kept_half(): pl.pallas_call(functools.partial(kept_kernel, offsets, offset, total is n...  12.3 us
    pallas_call x5, Pallas kernels, given_half(): pl.pallas_call(functools.partial(given_kernel, offsets), out_shape=jax.Sh...  11.8 us
    pallas_call x2, Pallas kernels, partial_grads(): pl.pallas_call(functools.partial(partial_kernel, places), out_shape=(jax....  10.8 us
    ppermute x28, waiting for transfers between devices, swap(): return lax.ppermute(value, 'expert', [(i, i ^ mask) for i in range(size)])  9.93 us
    ppermute x6, starting transfers between devices, mirror(): return lax.ppermute(value, 'pipe', [(i, size - 1 - i) for i in range(size)])  9.05 us
  transfers between devices with their start and end apart: 54, of which 18 were waited for; matrix products, arithmetic and copies ran while one was open for 3% of the time, Pallas kernels for 29%

profile of v3, /device:TPU:8, one launch (start us, length us, event | category | flops | bytes accessed | tf_op | source)
XLA Modules:
  0.0 154.0 jit_solution(5931799414816375689)
XLA Ops:
  0.7 1.1 dynamic-slice_bitcast_fusion
  1.9 1.6 %collective-permute-start.2 = (bf16[2,128,256]{2,1,0:T(8,128)(2,1)S(1)}, bf16[2,128,256]{2,1,0:T(8,128)(2,1)S(1)}, u32[]{:S(2)}, u32[]{:S(2)}) collective-permute-start(bf16[2,128,256]{2,1,0:T(8,128)(2,1)S(1)} %get-tuple-element.141), channel_id=1, source_target_pairs={{0,3},{1,2},{2,1},{3,0},{4,7},{5,6},{6,5},{7,4},{8,11},{9,10},{10,... | collective-permute-start | bytes 393224 | tf_op jit(solution)/shard_map/ppermute | solution.py:45
  4.0 1.5 collective-permute-start
  6.1 0.8 copy.13.route_ref
  6.8 1.6 %copy-done = bf16[1,2,1024,512]{3,2,1,0:T(8,128)(2,1)S(1)} copy-done((bf16[1,2,1024,512]{3,2,1,0:T(8,128)(2,1)S(1)}, bf16[1,2,1024,512]{3,2,1,0:T(8,128)(2,1)}, u32[]{:S(2)}) %copy-start) | copy-done | bytes 2097176
  8.4 2.0 %hidden_acts.1.refs_0_ = bf16[256,2048]{1,0:T(8,128)(2,1)S(1)} custom-call(s32[2,8,1]{2,1,0:T(8,128)S(1)} %copy.13.route_ref, bf16[2,1024,512]{2,1,0:T(8,128)(2,1)S(1)} %bitcast.32), custom_call_target="tpu_custom_call" | custom-call | flops 1 | bytes 1 | tf_op jit(solution)/shard_map/hidden_acts/pallas_call | solution.py:105
  10.6 1.5 collective-permute-done.4.refs_9_.refs_1_
  12.0 1.5 collective-permute-start.5
  13.5 2.4 %constant_dynamic-slice_fusion = (bf16[2,128,384]{2,1,0:T(8,128)(2,1)S(1)}, bf16[2,128,384]{2,1,0:T(8,128)(2,1)S(1)}, bf16[2,128,384]{2,1,0:T(8,128)(2,1)S(1)}, ...) fusion(bf16[2,128,7168]{2,1,0:T(8,128)(2,1)} %bitcast.39, ...), kind=kLoop, calls=%fused_computation.12 | loop fusion | bytes 6291520 | tf_op jit(solution)/shard_map/dynamic_slice | solution.py:455
  17.5 1.5 collective-permute-start.6
  19.5 1.5 collective-permute-start.11
  21.5 2.3 %collective-permute-done.6.refs_10_.refs_2_ = bf16[2,128,256]{2,1,0:T(8,128)(2,1)S(1)} collective-permute-done((bf16[2,128,256]{2,1,0:T(8,128)(2,1)S(1)}, bf16[2,128,256]{2,1,0:T(8,128)(2,1)S(1)}, u32[]{:S(2)}, u32[]{:S(2)}) %collective-permute-start.6) | collective-permute-done | bytes 131104 | tf_op jit(solution)/shard_map/ppermute | solution.py:50
  23.8 1.5 collective-permute-start.7
  25.3 13.1 %collective-permute-done.7.refs_11_.refs_3_ = bf16[2,128,256]{2,1,0:T(8,128)(2,1)S(1)} collective-permute-done((bf16[2,128,256]{2,1,0:T(8,128)(2,1)S(1)}, bf16[2,128,256]{2,1,0:T(8,128)(2,1)S(1)}, u32[]{:S(2)}, u32[]{:S(2)}) %collective-permute-start.7) | collective-permute-done | bytes 131104 | tf_op jit(solution)/shard_map/ppermute | solution.py:50
  39.3 1.5 collective-permute-start.15
  40.8 1.5 collective-permute-start.21
  42.8 1.7 %given_half.5 = bf16[512,256]{1,0:T(8,128)(2,1)S(1)} custom-call(bf16[256,2048]{1,0:T(8,128)(2,1)S(1)} %hidden_acts.1.refs_0_, bf16[256,2048]{1,0:T(8,128)(2,1)S(1)} %collective-permute-done.16.refs_1_, bf16[256,2048]{1,0:T(8,128)(2,1)S(1)} %collective-permute-done.5.refs_2_, bf16[256,2048]{1,0:T(8,128)(2,1)S(1)} %collective-permute-done.17.refs_3_, ...), custom_call_target="tpu_custom_call" | custom-call | flops 1 | bytes 1 | tf_op jit(solution)/shard_map/given_half/pallas_call | solution.py:194
  44.5 1.6 %collective-permute-start.23 = (bf16[512,256]{1,0:T(8,128)(2,1)S(1)}, bf16[512,256]{1,0:T(8,128)(2,1)S(1)}, u32[]{:S(2)}, u32[]{:S(2)}) collective-permute-start(bf16[512,256]{1,0:T(8,128)(2,1)S(1)} %given_half.5), channel_id=1, source_target_pairs={{0,24},{8,16},{16,8},{24,0},{1,25},{9,17},{17,9},{25,1},{2,26},{10... | collective-permute-start | bytes 786440 | tf_op jit(solution)/shard_map/ppermute | solution.py:55
  46.1 4.4 %collective-permute-done.15.refs_6_.refs_12_ = bf16[2,128,384]{2,1,0:T(8,128)(2,1)S(1)} collective-permute-done((bf16[2,128,384]{2,1,0:T(8,128)(2,1)S(1)}, bf16[2,128,384]{2,1,0:T(8,128)(2,1)S(1)}, u32[]{:S(2)}, u32[]{:S(2)}) %collective-permute-start.15) | collective-permute-done | bytes 196640 | tf_op jit(solution)/shard_map/ppermute | solution.py:45
  50.5 1.5 collective-permute-start.18
  53.2 5.1 %collective-permute-done.18.refs_10_.refs_9_ = bf16[2,128,384]{2,1,0:T(8,128)(2,1)S(1)} collective-permute-done((bf16[2,128,384]{2,1,0:T(8,128)(2,1)S(1)}, bf16[2,128,384]{2,1,0:T(8,128)(2,1)S(1)}, u32[]{:S(2)}, u32[]{:S(2)}) %collective-permute-start.18) | collective-permute-done | bytes 196640 | tf_op jit(solution)/shard_map/ppermute | solution.py:50
  58.3 3.1 %collective-permute-done.20.refs_11_.refs_10_ = bf16[2,128,384]{2,1,0:T(8,128)(2,1)S(1)} collective-permute-done((bf16[2,128,384]{2,1,0:T(8,128)(2,1)S(1)}, bf16[2,128,384]{2,1,0:T(8,128)(2,1)S(1)}, u32[]{:S(2)}, u32[]{:S(2)}) %collective-permute-start.20) | collective-permute-done | bytes 196640 | tf_op jit(solution)/shard_map/ppermute | solution.py:50
  61.4 2.5 %given_half.6 = bf16[512,384]{1,0:T(8,128)(2,1)S(1)} custom-call(bf16[256,2048]{1,0:T(8,128)(2,1)S(1)} %hidden_acts.1.refs_0_, bf16[256,2048]{1,0:T(8,128)(2,1)S(1)} %collective-permute-done.16.refs_1_, bf16[256,2048]{1,0:T(8,128)(2,1)S(1)} %collective-permute-done.5.refs_2_, bf16[256,2048]{1,0:T(8,128)(2,1)S(1)} %collective-permute-done.17.refs_3_, ...), custom_call_target="tpu_custom_call" | custom-call | flops 1 | bytes 1 | tf_op jit(solution)/shard_map/given_half/pallas_call | solution.py:194
  64.5 1.5 collective-permute-start.27
  66.0 1.5 collective-permute-start.28
  68.0 1.6 %collective-permute-start.32 = (bf16[512,384]{1,0:T(8,128)(2,1)S(1)}, bf16[512,384]{1,0:T(8,128)(2,1)S(1)}, u32[]{:S(2)}, u32[]{:S(2)}) collective-permute-start(bf16[512,384]{1,0:T(8,128)(2,1)S(1)} %given_half.6), channel_id=1, source_target_pairs={{0,24},{8,16},{16,8},{24,0},{1,25},{9,17},{17,9},{25,1},{2,26},{10... | collective-permute-start | bytes 1179656 | tf_op jit(solution)/shard_map/ppermute | solution.py:55
  69.6 2.2 %collective-permute-done.26.refs_18_.refs_6_ = bf16[2,128,384]{2,1,0:T(8,128)(2,1)S(1)} collective-permute-done((bf16[2,128,384]{2,1,0:T(8,128)(2,1)S(1)}, bf16[2,128,384]{2,1,0:T(8,128)(2,1)S(1)}, u32[]{:S(2)}, u32[]{:S(2)}) %collective-permute-start.26) | collective-permute-done | bytes 196640 | tf_op jit(solution)/shard_map/ppermute | solution.py:45
  71.8 1.5 collective-permute-start.30
  74.0 1.5 collective-permute-start.31
  75.5 2.6 %collective-permute-done.29.refs_11_.refs_12_ = bf16[2,128,384]{2,1,0:T(8,128)(2,1)S(1)} collective-permute-done((bf16[2,128,384]{2,1,0:T(8,128)(2,1)S(1)}, bf16[2,128,384]{2,1,0:T(8,128)(2,1)S(1)}, u32[]{:S(2)}, u32[]{:S(2)}) %collective-permute-start.29) | collective-permute-done | bytes 196640 | tf_op jit(solution)/shard_map/ppermute | solution.py:50
  78.1 2.4 %kept_half.4.refs_13_ = bf16[512,1792]{1,0:T(8,128)(2,1)} custom-call(bf16[256,2048]{1,0:T(8,128)(2,1)S(1)} %hidden_acts.1.refs_0_, bf16[256,2048]{1,0:T(8,128)(2,1)S(1)} %collective-permute-done.16.refs_1_, bf16[256,2048]{1,0:T(8,128)(2,1)S(1)} %collective-permute-done.5.refs_2_, bf16[256,2048]{1,0:T(8,128)(2,1)S(1)} %collective-permute-done.17.refs_3_, ...), custom_call_target="tpu_custom_call" | custom-call | flops 1 | bytes 1 | tf_op jit(solution)/shard_map/kept_half/pallas_call | solution.py:278
  80.5 2.6 %given_half.7 = bf16[512,384]{1,0:T(8,128)(2,1)S(1)} custom-call(bf16[256,2048]{1,0:T(8,128)(2,1)S(1)} %hidden_acts.1.refs_0_, bf16[256,2048]{1,0:T(8,128)(2,1)S(1)} %collective-permute-done.16.refs_1_, bf16[256,2048]{1,0:T(8,128)(2,1)S(1)} %collective-permute-done.5.refs_2_, bf16[256,2048]{1,0:T(8,128)(2,1)S(1)} %collective-permute-done.17.refs_3_, ...), custom_call_target="tpu_custom_call" | custom-call | flops 1 | bytes 1 | tf_op jit(solution)/shard_map/given_half/pallas_call | solution.py:194
  83.0 0.9 collective-permute-done.31.refs_8_.refs_14_
  83.9 2.1 %collective-permute-done.34.refs_19_.refs_7_ = bf16[2,128,384]{2,1,0:T(8,128)(2,1)S(1)} collective-permute-done((bf16[2,128,384]{2,1,0:T(8,128)(2,1)S(1)}, bf16[2,128,384]{2,1,0:T(8,128)(2,1)S(1)}, u32[]{:S(2)}, u32[]{:S(2)}) %collective-permute-start.34) | collective-permute-done | bytes 196640 | tf_op jit(solution)/shard_map/ppermute | solution.py:45
  86.0 1.6 %collective-permute-start.38 = (bf16[512,384]{1,0:T(8,128)(2,1)S(1)}, bf16[512,384]{1,0:T(8,128)(2,1)S(1)}, u32[]{:S(2)}, u32[]{:S(2)}) collective-permute-start(bf16[512,384]{1,0:T(8,128)(2,1)S(1)} %given_half.7), channel_id=1, source_target_pairs={{0,24},{8,16},{16,8},{24,0},{1,25},{9,17},{17,9},{25,1},{2,26},{10... | collective-permute-start | bytes 1179656 | tf_op jit(solution)/shard_map/ppermute | solution.py:55
  87.6 0.9 collective-permute-start.35
  88.5 1.2 collective-permute-start.36
  89.7 0.8 collective-permute-start.37
  90.5 3.3 %kept_half.5.refs_13_ = bf16[512,1792]{1,0:T(8,128)(2,1)} custom-call(bf16[256,2048]{1,0:T(8,128)(2,1)S(1)} %hidden_acts.1.refs_0_, bf16[256,2048]{1,0:T(8,128)(2,1)S(1)} %collective-permute-done.16.refs_1_, bf16[256,2048]{1,0:T(8,128)(2,1)S(1)} %collective-permute-done.5.refs_2_, ...), custom_call_target="tpu_custom_call", output_to_operand_aliasing={{}: (13, {})} | custom-call | flops 1 | bytes 1 | tf_op jit(solution)/shard_map/kept_half/pallas_call | solution.py:278
  93.8 5.4 %partial_grads.2 = (f32[2,1024,256]{2,1,0:T(8,128)S(1)}, bf16[1024,256]{1,0:T(8,128)(2,1)}, bf16[512,256]{1,0:T(8,128)(2,1)S(1)}, bf16[512,256]{1,0:T(8,128)(2,1)S(1)}) custom-call(bf16[2,128,256]{2,1,0:T(8,128)(2,1)S(1)} %collective-permute-done.1.refs_6_.refs_0_, bf16[2,128,256]{2,1,0:T(8,128)(2,1)S(1)} %collective-permute-done.2.refs_7_.refs_1_, ...), custom_call_target="tpu_custom_call" | custom-call | flops 1 | bytes 1 | tf_op jit(solution)/shard_map/partial_grads/pallas_call | solution.py:332
  99.7 2.5 %given_half.8 = bf16[512,384]{1,0:T(8,128)(2,1)S(1)} custom-call(bf16[256,2048]{1,0:T(8,128)(2,1)S(1)} %hidden_acts.1.refs_0_, bf16[256,2048]{1,0:T(8,128)(2,1)S(1)} %collective-permute-done.16.refs_1_, bf16[256,2048]{1,0:T(8,128)(2,1)S(1)} %collective-permute-done.5.refs_2_, bf16[256,2048]{1,0:T(8,128)(2,1)S(1)} %collective-permute-done.17.refs_3_, ...), custom_call_target="tpu_custom_call" | custom-call | flops 1 | bytes 1 | tf_op jit(solution)/shard_map/given_half/pallas_call | solution.py:194
  102.2 2.5 %collective-permute-done.38.refs_12_ = bf16[512,384]{1,0:T(8,128)(2,1)S(1)} collective-permute-done((bf16[512,384]{1,0:T(8,128)(2,1)S(1)}, bf16[512,384]{1,0:T(8,128)(2,1)S(1)}, u32[]{:S(2)}, u32[]{:S(2)}) %collective-permute-start.38) | collective-permute-done | bytes 393248 | tf_op jit(solution)/shard_map/ppermute | solution.py:55
  105.2 1.6 %collective-permute-start.41 = (bf16[512,384]{1,0:T(8,128)(2,1)S(1)}, bf16[512,384]{1,0:T(8,128)(2,1)S(1)}, u32[]{:S(2)}, u32[]{:S(2)}) collective-permute-start(bf16[512,384]{1,0:T(8,128)(2,1)S(1)} %given_half.8), channel_id=1, source_target_pairs={{0,24},{8,16},{16,8},{24,0},{1,25},{9,17},{17,9},{25,1},{2,26},{10... | collective-permute-start | bytes 1179656 | tf_op jit(solution)/shard_map/ppermute | solution.py:55
  106.9 2.4 %collective-permute-start.43 = (bf16[512,256]{1,0:T(8,128)(2,1)S(1)}, bf16[512,256]{1,0:T(8,128)(2,1)S(1)}, u32[]{:S(2)}, u32[]{:S(2)}) collective-permute-start(bf16[512,256]{1,0:T(8,128)(2,1)S(1)} %get-tuple-element.109), channel_id=1, source_target_pairs={{0,2},{1,3},{2,0},{3,1},{4,6},{5,7},{6,4},{7,5},{8,10},{9,11},{10,... | collective-permute-start | bytes 786440 | tf_op jit(solution)/shard_map/ppermute | solution.py:45
  109.9 1.5 collective-permute-start.40
  111.4 3.3 %kept_half.6.refs_13_ = bf16[512,1792]{1,0:T(8,128)(2,1)} custom-call(bf16[256,2048]{1,0:T(8,128)(2,1)S(1)} %hidden_acts.1.refs_0_, bf16[256,2048]{1,0:T(8,128)(2,1)S(1)} %collective-permute-done.16.refs_1_, bf16[256,2048]{1,0:T(8,128)(2,1)S(1)} %collective-permute-done.5.refs_2_, ...), custom_call_target="tpu_custom_call", output_to_operand_aliasing={{}: (13, {})} | custom-call | flops 1 | bytes 1 | tf_op jit(solution)/shard_map/kept_half/pallas_call | solution.py:278
  114.7 2.5 %collective-permute-done.39.refs_10_.refs_18_ = bf16[2,128,384]{2,1,0:T(8,128)(2,1)S(1)} collective-permute-done((bf16[2,128,384]{2,1,0:T(8,128)(2,1)S(1)}, bf16[2,128,384]{2,1,0:T(8,128)(2,1)S(1)}, u32[]{:S(2)}, u32[]{:S(2)}) %collective-permute-start.39) | collective-permute-done | bytes 196640 | tf_op jit(solution)/shard_map/ppermute | solution.py:50
  117.2 2.9 %collective-permute-done.40.refs_11_.refs_19_ = bf16[2,128,384]{2,1,0:T(8,128)(2,1)S(1)} collective-permute-done((bf16[2,128,384]{2,1,0:T(8,128)(2,1)S(1)}, bf16[2,128,384]{2,1,0:T(8,128)(2,1)S(1)}, u32[]{:S(2)}, u32[]{:S(2)}) %collective-permute-start.40) | collective-permute-done | bytes 196640 | tf_op jit(solution)/shard_map/ppermute | solution.py:50
  120.1 2.5 %given_half.9.refs_12_ = bf16[512,384]{1,0:T(8,128)(2,1)S(1)} custom-call(bf16[256,2048]{1,0:T(8,128)(2,1)S(1)} %hidden_acts.1.refs_0_, bf16[256,2048]{1,0:T(8,128)(2,1)S(1)} %collective-permute-done.16.refs_1_, bf16[256,2048]{1,0:T(8,128)(2,1)S(1)} %collective-permute-done.5.refs_2_, bf16[256,2048]{1,0:T(8,128)(2,1)S(1)} %collective-permute-done.17.refs_3_, ...), custom_call_target="tpu_custom_call" | custom-call | flops 1 | bytes 1 | tf_op jit(solution)/shard_map/given_half/pallas_call | solution.py:194
  122.6 5.4 %partial_grads.3 = (f32[2,1024,256]{2,1,0:T(8,128)S(1)}, bf16[1024,256]{1,0:T(8,128)(2,1)}, bf16[512,256]{1,0:T(8,128)(2,1)S(1)}, bf16[512,256]{1,0:T(8,128)(2,1)S(1)}) custom-call(bf16[2,128,256]{2,1,0:T(8,128)(2,1)S(1)} %collective-permute-done.refs_8_.refs_0_, bf16[2,128,256]{2,1,0:T(8,128)(2,1)S(1)} %collective-permute-done.4.refs_9_.refs_1_, ...), custom_call_target="tpu_custom_call" | custom-call | flops 1 | bytes 1 | tf_op jit(solution)/shard_map/partial_grads/pallas_call | solution.py:332
  128.7 0.8 fusion.4
  129.5 1.6 %collective-permute-start.52 = (bf16[256,384]{1,0:T(8,128)(2,1)S(1)}, bf16[256,384]{1,0:T(8,128)(2,1)S(1)}, u32[]{:S(2)}, u32[]{:S(2)}) collective-permute-start(bf16[256,384]{1,0:T(8,128)(2,1)S(1)} %get-tuple-element.149), channel_id=1, source_target_pairs={{0,24},{8,16},{16,8},{24,0},{1,25},{9,17},{17,9},{25,1},{2,26},{10... | collective-permute-start | bytes 589832 | tf_op jit(solution)/shard_map/ppermute | solution.py:55
  131.2 1.0 fusion
  132.1 1.7 %collective-permute-start.48 = (bf16[512,256]{1,0:T(8,128)(2,1)}, bf16[512,256]{1,0:T(8,128)(2,1)}, u32[]{:S(2)}, u32[]{:S(2)}) collective-permute-start(bf16[512,256]{1,0:T(8,128)(2,1)} %get-tuple-element.117), channel_id=1, source_target_pairs={{0,2},{1,3},{2,0},{3,1},{4,6},{5,7},{6,4},{7,5},{8,10},{9,11},{10,... | collective-permute-start | bytes 786440 | tf_op jit(solution)/shard_map/ppermute | solution.py:45
  134.1 2.5 %kept_dot.1.dot_ref = f32[512,384]{1,0:T(8,128)S(1)} custom-call(bf16[256,2048]{1,0:T(8,128)(2,1)S(1)} %hidden_acts.1.refs_0_, bf16[256,2048]{1,0:T(8,128)(2,1)S(1)} %collective-permute-done.16.refs_1_, bf16[256,2048]{1,0:T(8,128)(2,1)S(1)} %collective-permute-done.5.refs_2_, bf16[256,2048]{1,0:T(8,128)(2,1)S(1)} %collective-permute-done.17.refs_3_, ...), custom_call_target="tpu_custom_call" | custom-call | flops 1 | bytes 1 | tf_op jit(solution)/shard_map/kept_dot/pallas_call | solution.py:228
  136.7 3.3 %kept_half.7.refs_2_ = bf16[512,1792]{1,0:T(8,128)(2,1)} custom-call(bf16[256,2048]{1,0:T(8,128)(2,1)S(1)} %hidden_acts.1.refs_0_, bf16[256,2048]{1,0:T(8,128)(2,1)S(1)} %collective-permute-done.16.refs_1_, bf16[256,2048]{1,0:T(8,128)(2,1)S(1)} %collective-permute-done.5.refs_2_, ...), custom_call_target="tpu_custom_call", output_to_operand_aliasing={{}: (13, {})} | custom-call | flops 1 | bytes 1 | tf_op jit(solution)/shard_map/kept_half/pallas_call | solution.py:278
  141.4 1.1 collective-permute-start.53
  142.6 1.6 %copy-done.1 = bf16[1,2,1024,512]{3,2,1,0:T(8,128)(2,1)S(1)} copy-done((bf16[1,2,1024,512]{3,2,1,0:T(8,128)(2,1)S(1)}, bf16[1,2,1024,512]{3,2,1,0:T(8,128)(2,1)}, u32[]{:S(2)}) %copy-start.1) | copy-done | bytes 2097176
  144.2 1.6 %copy-done.5 = f32[2,1024,256]{2,1,0:T(8,128)S(1)} copy-done((f32[2,1024,256]{2,1,0:T(8,128)S(1)}, f32[2,1024,256]{2,1,0:T(8,128)}, u32[]{:S(2)}) %copy-start.5) | copy-done | bytes 2097176
  145.8 0.9 copy-done.9
  146.7 0.9 copy-done.11
  147.7 2.6 %store_grads.2.refs_2_ = bf16[2,1024,512]{2,1,0:T(8,128)(2,1)} custom-call(s32[2,8,1]{2,1,0:T(8,128)S(1)} %copy.13.route_ref, s32[1]{0:T(128)} %bitcast.13.group_ref, bf16[2,1024,512]{2,1,0:T(8,128)(2,1)S(1)} %bitcast.33, f32[2,1024,256]{2,1,0:T(8,128)S(1)} %copy-done.5, bf16[1024,256]{1,0:T(8,128)(2,1)} %collective-permute-done.51.core_ref, ...), custom_call_target="tpu_custom_call" | custom-call | flops 1 | bytes 1 | tf_op jit(solution)/shard_map/store_grads/pallas_call | solution.py:422
  150.5 2.5 %store_grads.3 = bf16[2,1024,512]{2,1,0:T(8,128)(2,1)} custom-call(s32[2,8,1]{2,1,0:T(8,128)S(1)} %copy.13.route_ref, s32[1]{0:T(128)} %bitcast.1.group_ref, bf16[2,1024,512]{2,1,0:T(8,128)(2,1)S(1)} %bitcast.34, f32[2,1024,256]{2,1,0:T(8,128)S(1)} %copy-done.7, ...), custom_call_target="tpu_custom_call", output_to_operand_aliasing={{}: (7, {})} | custom-call | flops 1 | bytes 1 | tf_op jit(solution)/shard_map/store_grads/pallas_call | solution.py:422
  153.0 0.8 kept_add.1
  (94 shorter events, 12.2 us)
Async XLA Ops:
  1.8 3.7 %collective-permute-start.3 = (bf16[2,128,256]{2,1,0:T(8,128)(2,1)S(1)}, bf16[2,128,256]{2,1,0:T(8,128)(2,1)S(1)}, u32[]{:S(2)}, u32[]{:S(2)}) collective-permute-start(bf16[2,128,256]{2,1,0:T(8,128)(2,1)S(1)} %get-tuple-element.140), channel_id=1, source_target_pairs={{0,1},{1,0},{2,3},{3,2},{4,5},{5,4},{6,7},{7,6},{8,9},{9,8},{10,11... | collective-permute-start | bytes 393224 | tf_op jit(solution)/shard_map/ppermute | solution.py:45
  1.9 8.5 %collective-permute-start.2 = (bf16[2,128,256]{2,1,0:T(8,128)(2,1)S(1)}, bf16[2,128,256]{2,1,0:T(8,128)(2,1)S(1)}, u32[]{:S(2)}, u32[]{:S(2)}) collective-permute-start(bf16[2,128,256]{2,1,0:T(8,128)(2,1)S(1)} %get-tuple-element.141), channel_id=1, source_target_pairs={{0,3},{1,2},{2,1},{3,0},{4,7},{5,6},{6,5},{7,4},{8,11},{9,10},{10,... | collective-permute-start | bytes 393224 | tf_op jit(solution)/shard_map/ppermute | solution.py:45
  3.5 7.1 %collective-permute-start.1 = (bf16[2,128,256]{2,1,0:T(8,128)(2,1)S(1)}, bf16[2,128,256]{2,1,0:T(8,128)(2,1)S(1)}, u32[]{:S(2)}, u32[]{:S(2)}) collective-permute-start(bf16[2,128,256]{2,1,0:T(8,128)(2,1)S(1)} %get-tuple-element.142), channel_id=1, source_target_pairs={{0,2},{1,3},{2,0},{3,1},{4,6},{5,7},{6,4},{7,5},{8,10},{9,11},{10,... | collective-permute-start | bytes 393224 | tf_op jit(solution)/shard_map/ppermute | solution.py:45
  4.0 6.5 %collective-permute-start = (bf16[2,128,256]{2,1,0:T(8,128)(2,1)S(1)}, bf16[2,128,256]{2,1,0:T(8,128)(2,1)S(1)}, u32[]{:S(2)}, u32[]{:S(2)}) collective-permute-start(bf16[2,128,256]{2,1,0:T(8,128)(2,1)S(1)} %get-tuple-element.143.refs_4_.refs_3_), channel_id=1, source_target_pairs={{4,0},{5,1},{6,2},{7,3},{0,4},{1,5},{2,6},{3,7},{12,8},{13,9},{14,... | collective-permute-start | bytes 393224 | tf_op jit(solution)/shard_map/ppermute | solution.py:50
  5.6 6.5 %collective-permute-start.4 = (bf16[2,128,256]{2,1,0:T(8,128)(2,1)S(1)}, bf16[2,128,256]{2,1,0:T(8,128)(2,1)S(1)}, u32[]{:S(2)}, u32[]{:S(2)}) collective-permute-start(bf16[2,128,256]{2,1,0:T(8,128)(2,1)S(1)} %collective-permute-done.3.refs_5_.refs_2_), channel_id=1, source_target_pairs={{4,0},{5,1},{6,2},{7,3},{0,4},{1,5},{2,6},{3,7},{12,8},{13,9},{14,... | collective-permute-start | bytes 393224 | tf_op jit(solution)/shard_map/ppermute | solution.py:50
  6.8 1.6 %copy-start = (bf16[1,2,1024,512]{3,2,1,0:T(8,128)(2,1)S(1)}, bf16[1,2,1024,512]{3,2,1,0:T(8,128)(2,1)}, u32[]{:S(2)}) copy-start(bf16[1,2,1024,512]{3,2,1,0:T(8,128)(2,1)} %param.6) | copy-start | bytes 6291460
  12.0 26.5 %collective-permute-start.5 = (bf16[256,2048]{1,0:T(8,128)(2,1)S(1)}, bf16[256,2048]{1,0:T(8,128)(2,1)S(1)}, u32[]{:S(2)}, u32[]{:S(2)}) collective-permute-start(bf16[256,2048]{1,0:T(8,128)(2,1)S(1)} %hidden_acts.1.refs_0_), channel_id=1, source_target_pairs={{0,2},{1,3},{2,0},{3,1},{4,6},{5,7},{6,4},{7,5},{8,10},{9,11},{10,... | collective-permute-start | bytes 3145736 | tf_op jit(solution)/shard_map/ppermute | solution.py:45
  16.0 1.5 collective-permute-start.9
  16.1 3.0 %collective-permute-start.14 = (bf16[2,128,384]{2,1,0:T(8,128)(2,1)S(1)}, bf16[2,128,384]{2,1,0:T(8,128)(2,1)S(1)}, u32[]{:S(2)}, u32[]{:S(2)}) collective-permute-start(bf16[2,128,384]{2,1,0:T(8,128)(2,1)S(1)} %get-tuple-element.130), channel_id=1, source_target_pairs={{0,1},{1,0},{2,3},{3,2},{4,5},{5,4},{6,7},{7,6},{8,9},{9,8},{10,11... | collective-permute-start | bytes 589832 | tf_op jit(solution)/shard_map/ppermute | solution.py:45
  16.6 3.0 %collective-permute-start.13 = (bf16[2,128,384]{2,1,0:T(8,128)(2,1)S(1)}, bf16[2,128,384]{2,1,0:T(8,128)(2,1)S(1)}, u32[]{:S(2)}, u32[]{:S(2)}) collective-permute-start(bf16[2,128,384]{2,1,0:T(8,128)(2,1)S(1)} %get-tuple-element.132), channel_id=1, source_target_pairs={{0,1},{1,0},{2,3},{3,2},{4,5},{5,4},{6,7},{7,6},{8,9},{9,8},{10,11... | collective-permute-start | bytes 589832 | tf_op jit(solution)/shard_map/ppermute | solution.py:45
  16.6 4.4 %collective-permute-start.12 = (bf16[2,128,384]{2,1,0:T(8,128)(2,1)S(1)}, bf16[2,128,384]{2,1,0:T(8,128)(2,1)S(1)}, u32[]{:S(2)}, u32[]{:S(2)}) collective-permute-start(bf16[2,128,384]{2,1,0:T(8,128)(2,1)S(1)} %get-tuple-element.134), channel_id=1, source_target_pairs={{0,1},{1,0},{2,3},{3,2},{4,5},{5,4},{6,7},{7,6},{8,9},{9,8},{10,11... | collective-permute-start | bytes 589832 | tf_op jit(solution)/shard_map/ppermute | solution.py:45
  17.5 6.3 %collective-permute-start.6 = (bf16[2,128,256]{2,1,0:T(8,128)(2,1)S(1)}, bf16[2,128,256]{2,1,0:T(8,128)(2,1)S(1)}, u32[]{:S(2)}, u32[]{:S(2)}) collective-permute-start(bf16[2,128,256]{2,1,0:T(8,128)(2,1)S(1)} %collective-permute-done.1.refs_6_.refs_0_), channel_id=1, source_target_pairs={{4,0},{5,1},{6,2},{7,3},{0,4},{1,5},{2,6},{3,7},{12,8},{13,9},{14,... | collective-permute-start | bytes 393224 | tf_op jit(solution)/shard_map/ppermute | solution.py:50
  19.0 19.5 %collective-permute-start.8 = (bf16[2,128,384]{2,1,0:T(8,128)(2,1)S(1)}, bf16[2,128,384]{2,1,0:T(8,128)(2,1)S(1)}, u32[]{:S(2)}, u32[]{:S(2)}) collective-permute-start(bf16[2,128,384]{2,1,0:T(8,128)(2,1)S(1)} %get-tuple-element.67.refs_4_), channel_id=1, source_target_pairs={{4,0},{5,1},{6,2},{7,3},{0,4},{1,5},{2,6},{3,7},{12,8},{13,9},{14,... | collective-permute-start | bytes 589832 | tf_op jit(solution)/shard_map/ppermute | solution.py:50
  19.5 19.0 %collective-permute-start.11 = (bf16[2,128,384]{2,1,0:T(8,128)(2,1)S(1)}, bf16[2,128,384]{2,1,0:T(8,128)(2,1)S(1)}, u32[]{:S(2)}, u32[]{:S(2)}) collective-permute-start(bf16[2,128,384]{2,1,0:T(8,128)(2,1)S(1)} %get-tuple-element.69.refs_4_.refs_6_), channel_id=1, source_target_pairs={{4,0},{5,1},{6,2},{7,3},{0,4},{1,5},{2,6},{3,7},{12,8},{13,9},{14,... | collective-permute-start | bytes 589832 | tf_op jit(solution)/shard_map/ppermute | solution.py:50
  21.0 17.4 %collective-permute-start.10 = (bf16[2,128,384]{2,1,0:T(8,128)(2,1)S(1)}, bf16[2,128,384]{2,1,0:T(8,128)(2,1)S(1)}, u32[]{:S(2)}, u32[]{:S(2)}) collective-permute-start(bf16[2,128,384]{2,1,0:T(8,128)(2,1)S(1)} %collective-permute-done.9.refs_5_), channel_id=1, source_target_pairs={{4,0},{5,1},{6,2},{7,3},{0,4},{1,5},{2,6},{3,7},{12,8},{13,9},{14,... | collective-permute-start | bytes 589832 | tf_op jit(solution)/shard_map/ppermute | solution.py:50
  23.8 14.6 %collective-permute-start.7 = (bf16[2,128,256]{2,1,0:T(8,128)(2,1)S(1)}, bf16[2,128,256]{2,1,0:T(8,128)(2,1)S(1)}, u32[]{:S(2)}, u32[]{:S(2)}) collective-permute-start(bf16[2,128,256]{2,1,0:T(8,128)(2,1)S(1)} %collective-permute-done.2.refs_7_.refs_1_), channel_id=1, source_target_pairs={{4,0},{5,1},{6,2},{7,3},{0,4},{1,5},{2,6},{3,7},{12,8},{13,9},{14,... | collective-permute-start | bytes 393224 | tf_op jit(solution)/shard_map/ppermute | solution.py:50
  38.5 3.8 %collective-permute-start.16 = (bf16[256,2048]{1,0:T(8,128)(2,1)S(1)}, bf16[256,2048]{1,0:T(8,128)(2,1)S(1)}, u32[]{:S(2)}, u32[]{:S(2)}) collective-permute-start(bf16[256,2048]{1,0:T(8,128)(2,1)S(1)} %hidden_acts.1.refs_0_), channel_id=1, source_target_pairs={{0,1},{1,0},{2,3},{3,2},{4,5},{5,4},{6,7},{7,6},{8,9},{9,8},{10,11... | collective-permute-start | bytes 3145736 | tf_op jit(solution)/shard_map/ppermute | solution.py:45
  38.6 4.2 %collective-permute-start.17 = (bf16[256,2048]{1,0:T(8,128)(2,1)S(1)}, bf16[256,2048]{1,0:T(8,128)(2,1)S(1)}, u32[]{:S(2)}, u32[]{:S(2)}) collective-permute-start(bf16[256,2048]{1,0:T(8,128)(2,1)S(1)} %collective-permute-done.5.refs_2_), channel_id=1, source_target_pairs={{0,1},{1,0},{2,3},{3,2},{4,5},{5,4},{6,7},{7,6},{8,9},{9,8},{10,11... | collective-permute-start | bytes 3145736 | tf_op jit(solution)/shard_map/ppermute | solution.py:45
  39.1 7.1 %collective-permute-start.19 = (bf16[2,128,384]{2,1,0:T(8,128)(2,1)S(1)}, bf16[2,128,384]{2,1,0:T(8,128)(2,1)S(1)}, u32[]{:S(2)}, u32[]{:S(2)}) collective-permute-start(bf16[2,128,384]{2,1,0:T(8,128)(2,1)S(1)} %get-tuple-element.75), channel_id=1, source_target_pairs={{0,3},{1,2},{2,1},{3,0},{4,7},{5,6},{6,5},{7,4},{8,11},{9,10},{10,... | collective-permute-start | bytes 589832 | tf_op jit(solution)/shard_map/ppermute | solution.py:45
  39.3 11.2 %collective-permute-start.15 = (bf16[2,128,384]{2,1,0:T(8,128)(2,1)S(1)}, bf16[2,128,384]{2,1,0:T(8,128)(2,1)S(1)}, u32[]{:S(2)}, u32[]{:S(2)}) collective-permute-start(bf16[2,128,384]{2,1,0:T(8,128)(2,1)S(1)} %get-tuple-element.71), channel_id=1, source_target_pairs={{0,2},{1,3},{2,0},{3,1},{4,6},{5,7},{6,4},{7,5},{8,10},{9,11},{10,... | collective-permute-start | bytes 589832 | tf_op jit(solution)/shard_map/ppermute | solution.py:45
  40.8 11.7 %collective-permute-start.21 = (bf16[2,128,384]{2,1,0:T(8,128)(2,1)S(1)}, bf16[2,128,384]{2,1,0:T(8,128)(2,1)S(1)}, u32[]{:S(2)}, u32[]{:S(2)}) collective-permute-start(bf16[2,128,384]{2,1,0:T(8,128)(2,1)S(1)} %collective-permute-done.12.refs_5_.refs_7_), channel_id=1, source_target_pairs={{4,0},{5,1},{6,2},{7,3},{0,4},{1,5},{2,6},{3,7},{12,8},{13,9},{14,... | collective-permute-start | bytes 589832 | tf_op jit(solution)/shard_map/ppermute | solution.py:50
  42.3 10.8 %collective-permute-start.22 = (bf16[2,128,384]{2,1,0:T(8,128)(2,1)S(1)}, bf16[2,128,384]{2,1,0:T(8,128)(2,1)S(1)}, u32[]{:S(2)}, u32[]{:S(2)}) collective-permute-start(bf16[2,128,384]{2,1,0:T(8,128)(2,1)S(1)} %get-tuple-element.78.refs_4_.refs_8_), channel_id=1, source_target_pairs={{4,0},{5,1},{6,2},{7,3},{0,4},{1,5},{2,6},{3,7},{12,8},{13,9},{14,... | collective-permute-start | bytes 589832 | tf_op jit(solution)/shard_map/ppermute | solution.py:50
  44.5 19.4 %collective-permute-start.23 = (bf16[512,256]{1,0:T(8,128)(2,1)S(1)}, bf16[512,256]{1,0:T(8,128)(2,1)S(1)}, u32[]{:S(2)}, u32[]{:S(2)}) collective-permute-start(bf16[512,256]{1,0:T(8,128)(2,1)S(1)} %given_half.5), channel_id=1, source_target_pairs={{0,24},{8,16},{16,8},{24,0},{1,25},{9,17},{17,9},{25,1},{2,26},{10... | collective-permute-start | bytes 786440 | tf_op jit(solution)/shard_map/ppermute | solution.py:55
  50.5 7.8 %collective-permute-start.18 = (bf16[2,128,384]{2,1,0:T(8,128)(2,1)S(1)}, bf16[2,128,384]{2,1,0:T(8,128)(2,1)S(1)}, u32[]{:S(2)}, u32[]{:S(2)}) collective-permute-start(bf16[2,128,384]{2,1,0:T(8,128)(2,1)S(1)} %collective-permute-done.15.refs_6_.refs_12_), channel_id=1, source_target_pairs={{4,0},{5,1},{6,2},{7,3},{0,4},{1,5},{2,6},{3,7},{12,8},{13,9},{14,... | collective-permute-start | bytes 589832 | tf_op jit(solution)/shard_map/ppermute | solution.py:50
  52.0 9.4 %collective-permute-start.20 = (bf16[2,128,384]{2,1,0:T(8,128)(2,1)S(1)}, bf16[2,128,384]{2,1,0:T(8,128)(2,1)S(1)}, u32[]{:S(2)}, u32[]{:S(2)}) collective-permute-start(bf16[2,128,384]{2,1,0:T(8,128)(2,1)S(1)} %collective-permute-done.19.refs_7_.refs_13_), channel_id=1, source_target_pairs={{4,0},{5,1},{6,2},{7,3},{0,4},{1,5},{2,6},{3,7},{12,8},{13,9},{14,... | collective-permute-start | bytes 589832 | tf_op jit(solution)/shard_map/ppermute | solution.py:50
  52.5 11.4 %collective-permute-start.24 = (bf16[2,128,384]{2,1,0:T(8,128)(2,1)S(1)}, bf16[2,128,384]{2,1,0:T(8,128)(2,1)S(1)}, u32[]{:S(2)}, u32[]{:S(2)}) collective-permute-start(bf16[2,128,384]{2,1,0:T(8,128)(2,1)S(1)} %get-tuple-element.80), channel_id=1, source_target_pairs={{0,2},{1,3},{2,0},{3,1},{4,6},{5,7},{6,4},{7,5},{8,10},{9,11},{10,... | collective-permute-start | bytes 589832 | tf_op jit(solution)/shard_map/ppermute | solution.py:45
  53.1 10.9 %collective-permute-start.25 = (bf16[2,128,384]{2,1,0:T(8,128)(2,1)S(1)}, bf16[2,128,384]{2,1,0:T(8,128)(2,1)S(1)}, u32[]{:S(2)}, u32[]{:S(2)}) collective-permute-start(bf16[2,128,384]{2,1,0:T(8,128)(2,1)S(1)} %get-tuple-element.81), channel_id=1, source_target_pairs={{0,3},{1,2},{2,1},{3,0},{4,7},{5,6},{6,5},{7,4},{8,11},{9,10},{10,... | collective-permute-start | bytes 589832 | tf_op jit(solution)/shard_map/ppermute | solution.py:45
  63.9 7.9 %collective-permute-start.26 = (bf16[2,128,384]{2,1,0:T(8,128)(2,1)S(1)}, bf16[2,128,384]{2,1,0:T(8,128)(2,1)S(1)}, u32[]{:S(2)}, u32[]{:S(2)}) collective-permute-start(bf16[2,128,384]{2,1,0:T(8,128)(2,1)S(1)} %get-tuple-element.83), channel_id=1, source_target_pairs={{0,2},{1,3},{2,0},{3,1},{4,6},{5,7},{6,4},{7,5},{8,10},{9,11},{10,... | collective-permute-start | bytes 589832 | tf_op jit(solution)/shard_map/ppermute | solution.py:45
  64.5 9.5 %collective-permute-start.27 = (bf16[2,128,384]{2,1,0:T(8,128)(2,1)S(1)}, bf16[2,128,384]{2,1,0:T(8,128)(2,1)S(1)}, u32[]{:S(2)}, u32[]{:S(2)}) collective-permute-start(bf16[2,128,384]{2,1,0:T(8,128)(2,1)S(1)} %get-tuple-element.84), channel_id=1, source_target_pairs={{0,2},{1,3},{2,0},{3,1},{4,6},{5,7},{6,4},{7,5},{8,10},{9,11},{10,... | collective-permute-start | bytes 589832 | tf_op jit(solution)/shard_map/ppermute | solution.py:45
  66.0 9.5 %collective-permute-start.28 = (bf16[2,128,384]{2,1,0:T(8,128)(2,1)S(1)}, bf16[2,128,384]{2,1,0:T(8,128)(2,1)S(1)}, u32[]{:S(2)}, u32[]{:S(2)}) collective-permute-start(bf16[2,128,384]{2,1,0:T(8,128)(2,1)S(1)} %collective-permute-done.24.refs_6_.refs_14_), channel_id=1, source_target_pairs={{4,0},{5,1},{6,2},{7,3},{0,4},{1,5},{2,6},{3,7},{12,8},{13,9},{14,... | collective-permute-start | bytes 589832 | tf_op jit(solution)/shard_map/ppermute | solution.py:50
  67.5 10.5 %collective-permute-start.29 = (bf16[2,128,384]{2,1,0:T(8,128)(2,1)S(1)}, bf16[2,128,384]{2,1,0:T(8,128)(2,1)S(1)}, u32[]{:S(2)}, u32[]{:S(2)}) collective-permute-start(bf16[2,128,384]{2,1,0:T(8,128)(2,1)S(1)} %collective-permute-done.25.refs_7_.refs_15_), channel_id=1, source_target_pairs={{4,0},{5,1},{6,2},{7,3},{0,4},{1,5},{2,6},{3,7},{12,8},{13,9},{14,... | collective-permute-start | bytes 589832 | tf_op jit(solution)/shard_map/ppermute | solution.py:50
  68.0 18.0 %collective-permute-start.32 = (bf16[512,384]{1,0:T(8,128)(2,1)S(1)}, bf16[512,384]{1,0:T(8,128)(2,1)S(1)}, u32[]{:S(2)}, u32[]{:S(2)}) collective-permute-start(bf16[512,384]{1,0:T(8,128)(2,1)S(1)} %given_half.6), channel_id=1, source_target_pairs={{0,24},{8,16},{16,8},{24,0},{1,25},{9,17},{17,9},{25,1},{2,26},{10... | collective-permute-start | bytes 1179656 | tf_op jit(solution)/shard_map/ppermute | solution.py:55
  71.8 11.2 %collective-permute-start.30 = (bf16[2,128,384]{2,1,0:T(8,128)(2,1)S(1)}, bf16[2,128,384]{2,1,0:T(8,128)(2,1)S(1)}, u32[]{:S(2)}, u32[]{:S(2)}) collective-permute-start(bf16[2,128,384]{2,1,0:T(8,128)(2,1)S(1)} %collective-permute-done.13.refs_5_.refs_9_), channel_id=1, source_target_pairs={{4,0},{5,1},{6,2},{7,3},{0,4},{1,5},{2,6},{3,7},{12,8},{13,9},{14,... | collective-permute-start | bytes 589832 | tf_op jit(solution)/shard_map/ppermute | solution.py:50
  74.0 9.9 %collective-permute-start.31 = (bf16[2,128,384]{2,1,0:T(8,128)(2,1)S(1)}, bf16[2,128,384]{2,1,0:T(8,128)(2,1)S(1)}, u32[]{:S(2)}, u32[]{:S(2)}) collective-permute-start(bf16[2,128,384]{2,1,0:T(8,128)(2,1)S(1)} %get-tuple-element.89.refs_10_.refs_4_), channel_id=1, source_target_pairs={{4,0},{5,1},{6,2},{7,3},{0,4},{1,5},{2,6},{3,7},{12,8},{13,9},{14,... | collective-permute-start | bytes 589832 | tf_op jit(solution)/shard_map/ppermute | solution.py:50
  75.5 8.4 %collective-permute-start.33 = (bf16[2,128,384]{2,1,0:T(8,128)(2,1)S(1)}, bf16[2,128,384]{2,1,0:T(8,128)(2,1)S(1)}, u32[]{:S(2)}, u32[]{:S(2)}) collective-permute-start(bf16[2,128,384]{2,1,0:T(8,128)(2,1)S(1)} %get-tuple-element.90), channel_id=1, source_target_pairs={{0,3},{1,2},{2,1},{3,0},{4,7},{5,6},{6,5},{7,4},{8,11},{9,10},{10,... | collective-permute-start | bytes 589832 | tf_op jit(solution)/shard_map/ppermute | solution.py:45
  78.1 8.0 %collective-permute-start.34 = (bf16[2,128,384]{2,1,0:T(8,128)(2,1)S(1)}, bf16[2,128,384]{2,1,0:T(8,128)(2,1)S(1)}, u32[]{:S(2)}, u32[]{:S(2)}) collective-permute-start(bf16[2,128,384]{2,1,0:T(8,128)(2,1)S(1)} %get-tuple-element.91), channel_id=1, source_target_pairs={{0,3},{1,2},{2,1},{3,0},{4,7},{5,6},{6,5},{7,4},{8,11},{9,10},{10,... | collective-permute-start | bytes 589832 | tf_op jit(solution)/shard_map/ppermute | solution.py:45
  86.0 18.7 %collective-permute-start.38 = (bf16[512,384]{1,0:T(8,128)(2,1)S(1)}, bf16[512,384]{1,0:T(8,128)(2,1)S(1)}, u32[]{:S(2)}, u32[]{:S(2)}) collective-permute-start(bf16[512,384]{1,0:T(8,128)(2,1)S(1)} %given_half.7), channel_id=1, source_target_pairs={{0,24},{8,16},{16,8},{24,0},{1,25},{9,17},{17,9},{25,1},{2,26},{10... | collective-permute-start | bytes 1179656 | tf_op jit(solution)/shard_map/ppermute | solution.py:55
  87.6 11.6 %collective-permute-start.35 = (bf16[2,128,384]{2,1,0:T(8,128)(2,1)S(1)}, bf16[2,128,384]{2,1,0:T(8,128)(2,1)S(1)}, u32[]{:S(2)}, u32[]{:S(2)}) collective-permute-start(bf16[2,128,384]{2,1,0:T(8,128)(2,1)S(1)} %collective-permute-done.27.refs_6_.refs_16_), channel_id=1, source_target_pairs={{4,0},{5,1},{6,2},{7,3},{0,4},{1,5},{2,6},{3,7},{12,8},{13,9},{14,... | collective-permute-start | bytes 589832 | tf_op jit(solution)/shard_map/ppermute | solution.py:50
  88.5 11.2 %collective-permute-start.36 = (bf16[2,128,384]{2,1,0:T(8,128)(2,1)S(1)}, bf16[2,128,384]{2,1,0:T(8,128)(2,1)S(1)}, u32[]{:S(2)}, u32[]{:S(2)}) collective-permute-start(bf16[2,128,384]{2,1,0:T(8,128)(2,1)S(1)} %collective-permute-done.33.refs_7_.refs_17_), channel_id=1, source_target_pairs={{4,0},{5,1},{6,2},{7,3},{0,4},{1,5},{2,6},{3,7},{12,8},{13,9},{14,... | collective-permute-start | bytes 589832 | tf_op jit(solution)/shard_map/ppermute | solution.py:50
  89.7 12.5 %collective-permute-start.37 = (bf16[2,128,384]{2,1,0:T(8,128)(2,1)S(1)}, bf16[2,128,384]{2,1,0:T(8,128)(2,1)S(1)}, u32[]{:S(2)}, u32[]{:S(2)}) collective-permute-start(bf16[2,128,384]{2,1,0:T(8,128)(2,1)S(1)} %collective-permute-done.14.refs_11_.refs_5_), channel_id=1, source_target_pairs={{4,0},{5,1},{6,2},{7,3},{0,4},{1,5},{2,6},{3,7},{12,8},{13,9},{14,... | collective-permute-start | bytes 589832 | tf_op jit(solution)/shard_map/ppermute | solution.py:50
  90.5 3.3 %copy-start.3 = (bf16[1,1024,1792]{2,1,0:T(8,128)(2,1)S(1)}, bf16[1,1024,1792]{2,1,0:T(8,128)(2,1)}, u32[]{:S(2)}) copy-start(bf16[1,1024,1792]{2,1,0:T(8,128)(2,1)} %param.7) | copy-start | bytes 11010052
  99.2 7.5 %copy-start.4 = (f32[2,1024,256]{2,1,0:T(8,128)}, f32[2,1024,256]{2,1,0:T(8,128)S(1)}, u32[]{:S(2)}) copy-start(f32[2,1024,256]{2,1,0:T(8,128)S(1)} %get-tuple-element.107.keep_ref) | copy-start | bytes 6291460
  104.7 2.1 %collective-permute-start.42 = (bf16[512,256]{1,0:T(8,128)(2,1)S(1)}, bf16[512,256]{1,0:T(8,128)(2,1)S(1)}, u32[]{:S(2)}, u32[]{:S(2)}) collective-permute-start(bf16[512,256]{1,0:T(8,128)(2,1)S(1)} %get-tuple-element.108), channel_id=1, source_target_pairs={{0,1},{1,0},{2,3},{3,2},{4,5},{5,4},{6,7},{7,6},{8,9},{9,8},{10,11... | collective-permute-start | bytes 786440 | tf_op jit(solution)/shard_map/ppermute | solution.py:45
  104.7 2.1 %collective-permute-start.44 = (bf16[512,256]{1,0:T(8,128)(2,1)S(1)}, bf16[512,256]{1,0:T(8,128)(2,1)S(1)}, u32[]{:S(2)}, u32[]{:S(2)}) collective-permute-start(bf16[512,256]{1,0:T(8,128)(2,1)S(1)} %get-tuple-element.110), channel_id=1, source_target_pairs={{0,1},{1,0},{2,3},{3,2},{4,5},{5,4},{6,7},{7,6},{8,9},{9,8},{10,11... | collective-permute-start | bytes 786440 | tf_op jit(solution)/shard_map/ppermute | solution.py:45
  105.2 22.8 %collective-permute-start.41 = (bf16[512,384]{1,0:T(8,128)(2,1)S(1)}, bf16[512,384]{1,0:T(8,128)(2,1)S(1)}, u32[]{:S(2)}, u32[]{:S(2)}) collective-permute-start(bf16[512,384]{1,0:T(8,128)(2,1)S(1)} %given_half.8), channel_id=1, source_target_pairs={{0,24},{8,16},{16,8},{24,0},{1,25},{9,17},{17,9},{25,1},{2,26},{10... | collective-permute-start | bytes 1179656 | tf_op jit(solution)/shard_map/ppermute | solution.py:55
  106.9 21.1 %collective-permute-start.43 = (bf16[512,256]{1,0:T(8,128)(2,1)S(1)}, bf16[512,256]{1,0:T(8,128)(2,1)S(1)}, u32[]{:S(2)}, u32[]{:S(2)}) collective-permute-start(bf16[512,256]{1,0:T(8,128)(2,1)S(1)} %get-tuple-element.109), channel_id=1, source_target_pairs={{0,2},{1,3},{2,0},{3,1},{4,6},{5,7},{6,4},{7,5},{8,10},{9,11},{10,... | collective-permute-start | bytes 786440 | tf_op jit(solution)/shard_map/ppermute | solution.py:45
  109.3 18.8 %collective-permute-start.45 = (bf16[512,256]{1,0:T(8,128)(2,1)S(1)}, bf16[512,256]{1,0:T(8,128)(2,1)S(1)}, u32[]{:S(2)}, u32[]{:S(2)}) collective-permute-start(bf16[512,256]{1,0:T(8,128)(2,1)S(1)} %get-tuple-element.111), channel_id=1, source_target_pairs={{0,2},{1,3},{2,0},{3,1},{4,6},{5,7},{6,4},{7,5},{8,10},{9,11},{10,... | collective-permute-start | bytes 786440 | tf_op jit(solution)/shard_map/ppermute | solution.py:45
  109.4 7.8 %collective-permute-start.39 = (bf16[2,128,384]{2,1,0:T(8,128)(2,1)S(1)}, bf16[2,128,384]{2,1,0:T(8,128)(2,1)S(1)}, u32[]{:S(2)}, u32[]{:S(2)}) collective-permute-start(bf16[2,128,384]{2,1,0:T(8,128)(2,1)S(1)} %collective-permute-done.26.refs_18_.refs_6_), channel_id=1, source_target_pairs={{4,0},{5,1},{6,2},{7,3},{0,4},{1,5},{2,6},{3,7},{12,8},{13,9},{14,... | collective-permute-start | bytes 589832 | tf_op jit(solution)/shard_map/ppermute | solution.py:50
  109.9 10.2 %collective-permute-start.40 = (bf16[2,128,384]{2,1,0:T(8,128)(2,1)S(1)}, bf16[2,128,384]{2,1,0:T(8,128)(2,1)S(1)}, u32[]{:S(2)}, u32[]{:S(2)}) collective-permute-start(bf16[2,128,384]{2,1,0:T(8,128)(2,1)S(1)} %collective-permute-done.34.refs_19_.refs_7_), channel_id=1, source_target_pairs={{4,0},{5,1},{6,2},{7,3},{0,4},{1,5},{2,6},{3,7},{12,8},{13,9},{14,... | collective-permute-start | bytes 589832 | tf_op jit(solution)/shard_map/ppermute | solution.py:50
  128.0 8.7 %copy-start.6 = (f32[2,1024,256]{2,1,0:T(8,128)}, f32[2,1024,256]{2,1,0:T(8,128)S(1)}, u32[]{:S(2)}) copy-start(f32[2,1024,256]{2,1,0:T(8,128)S(1)} %get-tuple-element.105.keep_ref) | copy-start | bytes 6291460
  128.0 8.7 %copy-start.8 = (bf16[512,256]{1,0:T(8,128)(2,1)}, bf16[512,256]{1,0:T(8,128)(2,1)S(1)}, u32[]{:S(2)}) copy-start(bf16[512,256]{1,0:T(8,128)(2,1)S(1)} %collective-permute-done.43.refs_0_) | copy-start | bytes 786436
  128.1 8.6 %copy-start.10 = (bf16[512,256]{1,0:T(8,128)(2,1)}, bf16[512,256]{1,0:T(8,128)(2,1)S(1)}, u32[]{:S(2)}) copy-start(bf16[512,256]{1,0:T(8,128)(2,1)S(1)} %collective-permute-done.45.refs_1_) | copy-start | bytes 786436
  128.1 3.1 %collective-permute-start.47 = (bf16[512,256]{1,0:T(8,128)(2,1)S(1)}, bf16[512,256]{1,0:T(8,128)(2,1)S(1)}, u32[]{:S(2)}, u32[]{:S(2)}) collective-permute-start(bf16[512,256]{1,0:T(8,128)(2,1)S(1)} %get-tuple-element.116), channel_id=1, source_target_pairs={{0,1},{1,0},{2,3},{3,2},{4,5},{5,4},{6,7},{7,6},{8,9},{9,8},{10,11... | collective-permute-start | bytes 786440 | tf_op jit(solution)/shard_map/ppermute | solution.py:45
  128.1 3.0 %collective-permute-start.49 = (bf16[512,256]{1,0:T(8,128)(2,1)S(1)}, bf16[512,256]{1,0:T(8,128)(2,1)S(1)}, u32[]{:S(2)}, u32[]{:S(2)}) collective-permute-start(bf16[512,256]{1,0:T(8,128)(2,1)S(1)} %get-tuple-element.118), channel_id=1, source_target_pairs={{0,1},{1,0},{2,3},{3,2},{4,5},{5,4},{6,7},{7,6},{8,9},{9,8},{10,11... | collective-permute-start | bytes 786440 | tf_op jit(solution)/shard_map/ppermute | solution.py:45
  128.6 13.9 %collective-permute-start.51 = (bf16[1024,256]{1,0:T(8,128)(2,1)}, bf16[1024,256]{1,0:T(8,128)(2,1)}, u32[]{:S(2)}, u32[]{:S(2)}) collective-permute-start(bf16[1024,256]{1,0:T(8,128)(2,1)} %get-tuple-element.121), channel_id=1, source_target_pairs={{0,1},{1,0},{2,3},{3,2},{4,5},{5,4},{6,7},{7,6},{8,9},{9,8},{10,11... | collective-permute-start | bytes 1572872 | tf_op jit(solution)/shard_map/ppermute | solution.py:45
  129.5 11.2 %collective-permute-start.52 = (bf16[256,384]{1,0:T(8,128)(2,1)S(1)}, bf16[256,384]{1,0:T(8,128)(2,1)S(1)}, u32[]{:S(2)}, u32[]{:S(2)}) collective-permute-start(bf16[256,384]{1,0:T(8,128)(2,1)S(1)} %get-tuple-element.149), channel_id=1, source_target_pairs={{0,24},{8,16},{16,8},{24,0},{1,25},{9,17},{17,9},{25,1},{2,26},{10... | collective-permute-start | bytes 589832 | tf_op jit(solution)/shard_map/ppermute | solution.py:55
  131.1 19.2 %collective-permute-start.46 = (bf16[1024,256]{1,0:T(8,128)(2,1)}, bf16[1024,256]{1,0:T(8,128)(2,1)S(1)}, u32[]{:S(2)}, u32[]{:S(2)}) collective-permute-start(bf16[1024,256]{1,0:T(8,128)(2,1)} %get-tuple-element.115), channel_id=1, source_target_pairs={{0,1},{1,0},{2,3},{3,2},{4,5},{5,4},{6,7},{7,6},{8,9},{9,8},{10,11... | collective-permute-start | bytes 1572872 | tf_op jit(solution)/shard_map/ppermute | solution.py:45
  132.1 18.2 %collective-permute-start.48 = (bf16[512,256]{1,0:T(8,128)(2,1)}, bf16[512,256]{1,0:T(8,128)(2,1)}, u32[]{:S(2)}, u32[]{:S(2)}) collective-permute-start(bf16[512,256]{1,0:T(8,128)(2,1)} %get-tuple-element.117), channel_id=1, source_target_pairs={{0,2},{1,3},{2,0},{3,1},{4,6},{5,7},{6,4},{7,5},{8,10},{9,11},{10,... | collective-permute-start | bytes 786440 | tf_op jit(solution)/shard_map/ppermute | solution.py:45
  133.8 16.6 %collective-permute-start.50 = (bf16[512,256]{1,0:T(8,128)(2,1)}, bf16[512,256]{1,0:T(8,128)(2,1)}, u32[]{:S(2)}, u32[]{:S(2)}) collective-permute-start(bf16[512,256]{1,0:T(8,128)(2,1)} %get-tuple-element.119), channel_id=1, source_target_pairs={{0,2},{1,3},{2,0},{3,1},{4,6},{5,7},{6,4},{7,5},{8,10},{9,11},{10,... | collective-permute-start | bytes 786440 | tf_op jit(solution)/shard_map/ppermute | solution.py:45
  141.4 11.5 %collective-permute-start.53 = (bf16[256,384]{1,0:T(8,128)(2,1)}, bf16[256,384]{1,0:T(8,128)(2,1)S(1)}, u32[]{:S(2)}, u32[]{:S(2)}) collective-permute-start(bf16[256,384]{1,0:T(8,128)(2,1)} %get-tuple-element.123), channel_id=1, source_target_pairs={{0,24},{8,16},{16,8},{24,0},{1,25},{9,17},{17,9},{25,1},{2,26},{10... | collective-permute-start | bytes 589832 | tf_op jit(solution)/shard_map/ppermute | solution.py:55
  142.6 1.6 %copy-start.1 = (bf16[1,2,1024,512]{3,2,1,0:T(8,128)(2,1)S(1)}, bf16[1,2,1024,512]{3,2,1,0:T(8,128)(2,1)}, u32[]{:S(2)}) copy-start(bf16[1,2,1024,512]{3,2,1,0:T(8,128)(2,1)} %param.6) | copy-start | bytes 6291460
  147.7 2.7 %copy-start.2 = (bf16[1,2,1024,512]{3,2,1,0:T(8,128)(2,1)S(1)}, bf16[1,2,1024,512]{3,2,1,0:T(8,128)(2,1)}, u32[]{:S(2)}) copy-start(bf16[1,2,1024,512]{3,2,1,0:T(8,128)(2,1)} %param.6) | copy-start | bytes 6291460
  147.7 2.8 %copy-start.7 = (f32[2,1024,256]{2,1,0:T(8,128)S(1)}, f32[2,1024,256]{2,1,0:T(8,128)}, u32[]{:S(2)}) copy-start(f32[2,1024,256]{2,1,0:T(8,128)} %copy-done.6) | copy-start | bytes 6291460
  150.5 2.5 %copy-start.13 = (bf16[256,384]{1,0:T(8,128)(2,1)S(1)}, bf16[256,384]{1,0:T(8,128)(2,1)}, u32[]{:S(2)}) copy-start(bf16[256,384]{1,0:T(8,128)(2,1)} %copy-done.12) | copy-start | bytes 589828
  (4 other events, 4.2 us)

commit v4 on v3

--- a/solution.py
+++ b/solution.py
@@ -9,7 +9,9 @@
 
 TILE = 128
 GROUP = 4
+SIZES = [2,2,3,4,3]
 VMEM_BYTES = 17 * 1024 * 1024
+STORE_VMEM_BYTES = 60 * 1024 * 1024
 LARGE_VMEM_BYTES = 60 * 1024 * 1024
 ANY = pl.BlockSpec(memory_space=pltpu.MemorySpace.HBM)
 SMEM = pl.BlockSpec(memory_space=pltpu.SMEM)
@@ -26,9 +28,7 @@
 
 def column_chunks(width):
     tiles = width // TILE
-    sizes = [2]
-    while sum(sizes) < tiles:
-        sizes.append(min(3, tiles - sum(sizes)))
+    sizes = SIZES if tiles == sum(SIZES) else [tiles // 5] * 4 + [tiles - tiles // 5 * 4]
     chunks, offset = [], 0
     for size in sizes:
         chunks.append((offset * TILE, size * TILE))
@@ -432,7 +432,7 @@
             pltpu.SemaphoreType.DMA((micros * slots,)),
         ],
         input_output_aliases=aliases,
-        compiler_params=params(),
+        compiler_params=params(STORE_VMEM_BYTES),
         cost_estimate=cost(rows * units * 16, 8 * rows * units + stored.size * 4),
         name="store_grads",
     )(*operands)
@@ -533,7 +533,7 @@
     weight_grad = None
     store_grad = None
     ready = []
-    extra = {1: [(3, 1), (4, 0)], 2: [(4, 1)]}
+    extra = {1: [(3, 1)], 2: [(4, 0)], 3: [(4, 1)]}
     rounds = [[1], [2], [3], [4]]
     for i in range(last):
         payload = after(halves[i], *ready)
@@ -552,8 +552,9 @@
             weight_grad = kept(i - 1, weight_grad)
             ready.append(weight_grad)
         if i == 1:
-            for part in chunks[3:]:
-                ready += exchange(part, (2, 3), payload)
+            ready += exchange(chunks[3], (2, 3), payload)
+        if i == 2:
+            ready += exchange(chunks[4], (2, 3), payload)
         if i == last - 2:
             own_parts = partial(0, payload)
             ready += own_parts[2:]

time: 155 us -> 147 us (0.948)
  local copies, waits for them, and re-layouts: 12.6 us -> 7.64 us
  Pallas kernels: 45.4 us -> 42.9 us
    unnamed x28 -> x14, local copies, waits for them, and re-layouts: 7.47 us -> 1.62 us
    ppermute x6, waiting for transfers between devices: 3.2 us -> 6.64 us  [mirror(): return lax.ppermute(value, 'pipe', [(i, size - 1 - i) for i in range(size)])]
    ppermute x28, waiting for transfers between devices: 9.93 us -> 6.93 us  [swap(): return lax.ppermute(value, 'expert', [(i, i ^ mask) for i in range(size)])]
    ppermute x6, starting transfers between devices: 9.05 us -> 6.88 us  [mirror(): return lax.ppermute(value, 'pipe', [(i, size - 1 - i) for i in range(size)])]
    pallas_call x4, Pallas kernels: 12.3 us -> 10.6 us  [kept_half(): pl.pallas_call(functools.partial(kept_kernel, offsets, offset, total is n...]
    pallas_call x2, Pallas kernels: 5.12 us -> 6.85 us  [store_grads(): pl.pallas_call(functools.partial(store_kernel, total is None), grid=(1,),...]
    dynamic_slice x2 -> x4, local copies, waits for them, and re-layouts: 3.58 us -> 5.22 us  [own_slice(): return lax.dynamic_slice(rows, (0, 0, start), (micros, block_rows, width))]
    pallas_call x5, Pallas kernels: 11.8 us -> 10.2 us  [given_half(): pl.pallas_call(functools.partial(given_kernel, offsets), out_shape=jax.Sh...]
  transfers between devices with their start and end apart: 54 -> 54, of which waited for: 18 -> 25; matrix products, arithmetic and copies ran while one was open for 3% -> 4% of each run, Pallas kernels for 29% -> 29%
where the time goes in v4:
time: 147 us; the launch traced here: 146 us
  waiting for transfers between devices  48.8 us (33%)
  starting transfers between devices  44.8 us (30%)
  Pallas kernels  42.9 us (29%)
  local copies, waits for them, and re-layouts  7.64 us (5%)
    ppermute x20, waiting for transfers between devices, from_group(): lax.ppermute(value, 'expert', [((i + step * GROUP) % size, i) for i in ra...  35.2 us
    ppermute x20, starting transfers between devices, from_group(): lax.ppermute(value, 'expert', [((i + step * GROUP) % size, i) for i in ra...  23 us
    ppermute x28, starting transfers between devices, swap(): return lax.ppermute(value, 'expert', [(i, i ^ mask) for i in range(size)])  15 us
    pallas_call x2, Pallas kernels, partial_grads(): pl.pallas_call(functools.partial(partial_kernel, places), out_shape=(jax....  10.7 us
    pallas_call x4, Pallas kernels, kept_half(): pl.pallas_call(functools.partial(kept_kernel, offsets, offset, total is n...  10.6 us
    pallas_call x5, Pallas kernels, given_half(): pl.pallas_call(functools.partial(given_kernel, offsets), out_shape=jax.Sh...  10.2 us
    ppermute x28, waiting for transfers between devices, swap(): return lax.ppermute(value, 'expert', [(i, i ^ mask) for i in range(size)])  6.93 us
    ppermute x6, starting transfers between devices, mirror(): return lax.ppermute(value, 'pipe', [(i, size - 1 - i) for i in range(size)])  6.88 us
  transfers between devices with their start and end apart: 54, of which 25 were waited for; matrix products, arithmetic and copies ran while one was open for 4% of the time, Pallas kernels for 29%

profile of v4, /device:TPU:8, one launch (start us, length us, event | category | flops | bytes accessed | tf_op | source)
XLA Modules:
  0.0 146.4 jit_solution(3404213647537462284)
XLA Ops:
  0.7 1.1 dynamic-slice_bitcast_fusion
  1.9 1.6 %collective-permute-start.2 = (bf16[2,128,256]{2,1,0:T(8,128)(2,1)S(1)}, bf16[2,128,256]{2,1,0:T(8,128)(2,1)S(1)}, u32[]{:S(2)}, u32[]{:S(2)}) collective-permute-start(bf16[2,128,256]{2,1,0:T(8,128)(2,1)S(1)} %get-tuple-element.141), channel_id=1, source_target_pairs={{0,3},{1,2},{2,1},{3,0},{4,7},{5,6},{6,5},{7,4},{8,11},{9,10},{10,... | collective-permute-start | bytes 393224 | tf_op jit(solution)/shard_map/ppermute | solution.py:45
  4.0 1.5 %collective-permute-start = (bf16[2,128,256]{2,1,0:T(8,128)(2,1)S(1)}, bf16[2,128,256]{2,1,0:T(8,128)(2,1)S(1)}, u32[]{:S(2)}, u32[]{:S(2)}) collective-permute-start(bf16[2,128,256]{2,1,0:T(8,128)(2,1)S(1)} %get-tuple-element.143.refs_4_.refs_3_), channel_id=1, source_target_pairs={{4,0},{5,1},{6,2},{7,3},{0,4},{1,5},{2,6},{3,7},{12,8},{13,9},{14,... | collective-permute-start | bytes 393224 | tf_op jit(solution)/shard_map/ppermute | solution.py:50
  6.8 1.6 %copy-done = bf16[1,2,1024,512]{3,2,1,0:T(8,128)(2,1)S(1)} copy-done((bf16[1,2,1024,512]{3,2,1,0:T(8,128)(2,1)S(1)}, bf16[1,2,1024,512]{3,2,1,0:T(8,128)(2,1)}, u32[]{:S(2)}) %copy-start) | copy-done | bytes 2097176
  8.4 1.3 hidden_acts.1.refs_0_
  10.6 1.5 collective-permute-done.4.refs_9_.refs_1_
  12.0 1.5 %collective-permute-start.5 = (bf16[256,2048]{1,0:T(8,128)(2,1)S(1)}, bf16[256,2048]{1,0:T(8,128)(2,1)S(1)}, u32[]{:S(2)}, u32[]{:S(2)}) collective-permute-start(bf16[256,2048]{1,0:T(8,128)(2,1)S(1)} %hidden_acts.1.refs_0_), channel_id=1, source_target_pairs={{0,2},{1,3},{2,0},{3,1},{4,6},{5,7},{6,4},{7,5},{8,10},{9,11},{10,... | collective-permute-start | bytes 3145736 | tf_op jit(solution)/shard_map/ppermute | solution.py:45
  13.5 1.1 constant_dynamic-slice_fusion.4
  14.8 1.3 constant_dynamic-slice_fusion.1
  16.6 1.7 %constant_dynamic-slice_fusion = (bf16[2,128,384]{2,1,0:T(8,128)(2,1)S(1)}, bf16[2,128,384]{2,1,0:T(8,128)(2,1)S(1)}, bf16[2,128,384]{2,1,0:T(8,128)(2,1)S(1)}, ...) fusion(bf16[2,128,7168]{2,1,0:T(8,128)(2,1)} %bitcast.41, ...), kind=kLoop, calls=%fused_computation.12 | loop fusion | bytes 3145760 | tf_op jit(solution)/shard_map/dynamic_slice | solution.py:455
  18.8 1.5 %collective-permute-start.6 = (bf16[2,128,256]{2,1,0:T(8,128)(2,1)S(1)}, bf16[2,128,256]{2,1,0:T(8,128)(2,1)S(1)}, u32[]{:S(2)}, u32[]{:S(2)}) collective-permute-start(bf16[2,128,256]{2,1,0:T(8,128)(2,1)S(1)} %collective-permute-done.1.refs_6_.refs_0_), channel_id=1, source_target_pairs={{4,0},{5,1},{6,2},{7,3},{0,4},{1,5},{2,6},{3,7},{12,8},{13,9},{14,... | collective-permute-start | bytes 393224 | tf_op jit(solution)/shard_map/ppermute | solution.py:50
  20.4 0.9 collective-permute-start.11
  21.3 1.1 collective-permute-start.7
  22.4 0.9 collective-permute-start.8
  23.3 1.9 %collective-permute-done.6.refs_10_.refs_2_ = bf16[2,128,256]{2,1,0:T(8,128)(2,1)S(1)} collective-permute-done((bf16[2,128,256]{2,1,0:T(8,128)(2,1)S(1)}, bf16[2,128,256]{2,1,0:T(8,128)(2,1)S(1)}, u32[]{:S(2)}, u32[]{:S(2)}) %collective-permute-start.6) | collective-permute-done | bytes 131104 | tf_op jit(solution)/shard_map/ppermute | solution.py:50
  25.2 1.5 %collective-permute-start.10 = (bf16[2,128,256]{2,1,0:T(8,128)(2,1)S(1)}, bf16[2,128,256]{2,1,0:T(8,128)(2,1)S(1)}, u32[]{:S(2)}, u32[]{:S(2)}) collective-permute-start(bf16[2,128,256]{2,1,0:T(8,128)(2,1)S(1)} %collective-permute-done.9.refs_5_), channel_id=1, source_target_pairs={{4,0},{5,1},{6,2},{7,3},{0,4},{1,5},{2,6},{3,7},{12,8},{13,9},{14,... | collective-permute-start | bytes 393224 | tf_op jit(solution)/shard_map/ppermute | solution.py:50
  26.7 5.5 %collective-permute-done.7.refs_11_.refs_3_ = bf16[2,128,256]{2,1,0:T(8,128)(2,1)S(1)} collective-permute-done((bf16[2,128,256]{2,1,0:T(8,128)(2,1)S(1)}, bf16[2,128,256]{2,1,0:T(8,128)(2,1)S(1)}, u32[]{:S(2)}, u32[]{:S(2)}) %collective-permute-start.7) | collective-permute-done | bytes 131104 | tf_op jit(solution)/shard_map/ppermute | solution.py:50
  32.2 2.8 %collective-permute-done.8.refs_8_.refs_4_ = bf16[2,128,256]{2,1,0:T(8,128)(2,1)S(1)} collective-permute-done((bf16[2,128,256]{2,1,0:T(8,128)(2,1)S(1)}, bf16[2,128,256]{2,1,0:T(8,128)(2,1)S(1)}, u32[]{:S(2)}, u32[]{:S(2)}) %collective-permute-start.8) | collective-permute-done | bytes 131104 | tf_op jit(solution)/shard_map/ppermute | solution.py:50
  35.0 1.9 %collective-permute-done.10.refs_9_.refs_5_ = bf16[2,128,256]{2,1,0:T(8,128)(2,1)S(1)} collective-permute-done((bf16[2,128,256]{2,1,0:T(8,128)(2,1)S(1)}, bf16[2,128,256]{2,1,0:T(8,128)(2,1)S(1)}, u32[]{:S(2)}, u32[]{:S(2)}) %collective-permute-start.10) | collective-permute-done | bytes 131104 | tf_op jit(solution)/shard_map/ppermute | solution.py:50
  37.5 1.5 %collective-permute-start.23 = (bf16[2,128,512]{2,1,0:T(8,128)(2,1)S(1)}, bf16[2,128,512]{2,1,0:T(8,128)(2,1)S(1)}, u32[]{:S(2)}, u32[]{:S(2)}) collective-permute-start(bf16[2,128,512]{2,1,0:T(8,128)(2,1)S(1)} %get-tuple-element.79.refs_4_.refs_8_), channel_id=1, source_target_pairs={{4,0},{5,1},{6,2},{7,3},{0,4},{1,5},{2,6},{3,7},{12,8},{13,9},{14,... | collective-permute-start | bytes 786440 | tf_op jit(solution)/shard_map/ppermute | solution.py:50
  41.1 1.7 %given_half.5 = bf16[512,256]{1,0:T(8,128)(2,1)S(1)} custom-call(bf16[256,2048]{1,0:T(8,128)(2,1)S(1)} %hidden_acts.1.refs_0_, bf16[256,2048]{1,0:T(8,128)(2,1)S(1)} %collective-permute-done.15.refs_1_, bf16[256,2048]{1,0:T(8,128)(2,1)S(1)} %collective-permute-done.5.refs_2_, bf16[256,2048]{1,0:T(8,128)(2,1)S(1)} %collective-permute-done.16.refs_3_, ...), custom_call_target="tpu_custom_call" | custom-call | flops 1 | bytes 1 | tf_op jit(solution)/shard_map/given_half/pallas_call | solution.py:194
  42.8 1.6 %collective-permute-start.24 = (bf16[512,256]{1,0:T(8,128)(2,1)S(1)}, bf16[512,256]{1,0:T(8,128)(2,1)S(1)}, u32[]{:S(2)}, u32[]{:S(2)}) collective-permute-start(bf16[512,256]{1,0:T(8,128)(2,1)S(1)} %given_half.5), channel_id=1, source_target_pairs={{0,24},{8,16},{16,8},{24,0},{1,25},{9,17},{17,9},{25,1},{2,26},{10... | collective-permute-start | bytes 786440 | tf_op jit(solution)/shard_map/ppermute | solution.py:55
  44.4 1.4 collective-permute-done.18.refs_6_.refs_12_
  45.8 1.7 %collective-permute-start.25 = (bf16[2,128,384]{2,1,0:T(8,128)(2,1)S(1)}, bf16[2,128,384]{2,1,0:T(8,128)(2,1)S(1)}, u32[]{:S(2)}, u32[]{:S(2)}) collective-permute-start(bf16[2,128,384]{2,1,0:T(8,128)(2,1)S(1)} %get-tuple-element.81), channel_id=1, source_target_pairs={{0,3},{1,2},{2,1},{3,0},{4,7},{5,6},{6,5},{7,4},{8,11},{9,10},{10,... | collective-permute-start | bytes 589832 | tf_op jit(solution)/shard_map/ppermute | solution.py:45
  47.5 2.4 %collective-permute-done.22.refs_9_.refs_7_ = bf16[2,128,384]{2,1,0:T(8,128)(2,1)S(1)} collective-permute-done((bf16[2,128,384]{2,1,0:T(8,128)(2,1)S(1)}, bf16[2,128,384]{2,1,0:T(8,128)(2,1)S(1)}, u32[]{:S(2)}, u32[]{:S(2)}) %collective-permute-start.22) | collective-permute-done | bytes 196640 | tf_op jit(solution)/shard_map/ppermute | solution.py:50
  50.0 1.5 %collective-permute-start.19 = (bf16[2,128,256]{2,1,0:T(8,128)(2,1)S(1)}, bf16[2,128,256]{2,1,0:T(8,128)(2,1)S(1)}, u32[]{:S(2)}, u32[]{:S(2)}) collective-permute-start(bf16[2,128,256]{2,1,0:T(8,128)(2,1)S(1)} %collective-permute-done.18.refs_6_.refs_12_), channel_id=1, source_target_pairs={{4,0},{5,1},{6,2},{7,3},{0,4},{1,5},{2,6},{3,7},{12,8},{13,9},{14,... | collective-permute-start | bytes 393224 | tf_op jit(solution)/shard_map/ppermute | solution.py:50
  52.0 4.0 %collective-permute-done.19.refs_10_.refs_9_ = bf16[2,128,256]{2,1,0:T(8,128)(2,1)S(1)} collective-permute-done((bf16[2,128,256]{2,1,0:T(8,128)(2,1)S(1)}, bf16[2,128,256]{2,1,0:T(8,128)(2,1)S(1)}, u32[]{:S(2)}, u32[]{:S(2)}) %collective-permute-start.19) | collective-permute-done | bytes 131104 | tf_op jit(solution)/shard_map/ppermute | solution.py:50
  56.0 1.4 collective-permute-done.21.refs_11_.refs_10_
  57.4 1.7 %given_half.6 = bf16[512,256]{1,0:T(8,128)(2,1)S(1)} custom-call(bf16[256,2048]{1,0:T(8,128)(2,1)S(1)} %hidden_acts.1.refs_0_, bf16[256,2048]{1,0:T(8,128)(2,1)S(1)} %collective-permute-done.15.refs_1_, bf16[256,2048]{1,0:T(8,128)(2,1)S(1)} %collective-permute-done.5.refs_2_, bf16[256,2048]{1,0:T(8,128)(2,1)S(1)} %collective-permute-done.16.refs_3_, ...), custom_call_target="tpu_custom_call" | custom-call | flops 1 | bytes 1 | tf_op jit(solution)/shard_map/given_half/pallas_call | solution.py:194
  59.1 1.6 %collective-permute-start.26 = (bf16[2,128,384]{2,1,0:T(8,128)(2,1)S(1)}, bf16[2,128,384]{2,1,0:T(8,128)(2,1)S(1)}, u32[]{:S(2)}, u32[]{:S(2)}) collective-permute-start(bf16[2,128,384]{2,1,0:T(8,128)(2,1)S(1)} %collective-permute-done.17.refs_6_.refs_14_), channel_id=1, source_target_pairs={{4,0},{5,1},{6,2},{7,3},{0,4},{1,5},{2,6},{3,7},{12,8},{13,9},{14,... | collective-permute-start | bytes 589832 | tf_op jit(solution)/shard_map/ppermute | solution.py:50
  61.7 1.6 %collective-permute-start.29 = (bf16[512,256]{1,0:T(8,128)(2,1)S(1)}, bf16[512,256]{1,0:T(8,128)(2,1)S(1)}, u32[]{:S(2)}, u32[]{:S(2)}) collective-permute-start(bf16[512,256]{1,0:T(8,128)(2,1)S(1)} %given_half.6), channel_id=1, source_target_pairs={{0,24},{8,16},{16,8},{24,0},{1,25},{9,17},{17,9},{25,1},{2,26},{10... | collective-permute-start | bytes 786440 | tf_op jit(solution)/shard_map/ppermute | solution.py:55
  63.3 3.7 %collective-permute-done.26.refs_10_.refs_11_ = bf16[2,128,384]{2,1,0:T(8,128)(2,1)S(1)} collective-permute-done((bf16[2,128,384]{2,1,0:T(8,128)(2,1)S(1)}, bf16[2,128,384]{2,1,0:T(8,128)(2,1)S(1)}, u32[]{:S(2)}, u32[]{:S(2)}) %collective-permute-start.26) | collective-permute-done | bytes 196640 | tf_op jit(solution)/shard_map/ppermute | solution.py:50
  67.0 1.5 %collective-permute-start.27 = (bf16[2,128,384]{2,1,0:T(8,128)(2,1)S(1)}, bf16[2,128,384]{2,1,0:T(8,128)(2,1)S(1)}, u32[]{:S(2)}, u32[]{:S(2)}) collective-permute-start(bf16[2,128,384]{2,1,0:T(8,128)(2,1)S(1)} %collective-permute-done.25.refs_7_.refs_15_), channel_id=1, source_target_pairs={{4,0},{5,1},{6,2},{7,3},{0,4},{1,5},{2,6},{3,7},{12,8},{13,9},{14,... | collective-permute-start | bytes 589832 | tf_op jit(solution)/shard_map/ppermute | solution.py:50
  68.5 2.4 %kept_half.4.refs_13_ = bf16[512,1792]{1,0:T(8,128)(2,1)} custom-call(bf16[256,2048]{1,0:T(8,128)(2,1)S(1)} %hidden_acts.1.refs_0_, bf16[256,2048]{1,0:T(8,128)(2,1)S(1)} %collective-permute-done.15.refs_1_, bf16[256,2048]{1,0:T(8,128)(2,1)S(1)} %collective-permute-done.5.refs_2_, bf16[256,2048]{1,0:T(8,128)(2,1)S(1)} %collective-permute-done.16.refs_3_, ...), custom_call_target="tpu_custom_call" | custom-call | flops 1 | bytes 1 | tf_op jit(solution)/shard_map/kept_half/pallas_call | solution.py:278
  70.9 3.2 %collective-permute-done.27.refs_11_.refs_12_ = bf16[2,128,384]{2,1,0:T(8,128)(2,1)S(1)} collective-permute-done((bf16[2,128,384]{2,1,0:T(8,128)(2,1)S(1)}, bf16[2,128,384]{2,1,0:T(8,128)(2,1)S(1)}, u32[]{:S(2)}, u32[]{:S(2)}) %collective-permute-start.27) | collective-permute-done | bytes 196640 | tf_op jit(solution)/shard_map/ppermute | solution.py:50
  74.1 2.5 %given_half.7 = bf16[512,384]{1,0:T(8,128)(2,1)S(1)} custom-call(bf16[256,2048]{1,0:T(8,128)(2,1)S(1)} %hidden_acts.1.refs_0_, bf16[256,2048]{1,0:T(8,128)(2,1)S(1)} %collective-permute-done.15.refs_1_, bf16[256,2048]{1,0:T(8,128)(2,1)S(1)} %collective-permute-done.5.refs_2_, bf16[256,2048]{1,0:T(8,128)(2,1)S(1)} %collective-permute-done.16.refs_3_, ...), custom_call_target="tpu_custom_call" | custom-call | flops 1 | bytes 1 | tf_op jit(solution)/shard_map/given_half/pallas_call | solution.py:194
  76.7 1.0 collective-permute-start.32
  77.7 1.6 %collective-permute-start.36 = (bf16[512,384]{1,0:T(8,128)(2,1)S(1)}, bf16[512,384]{1,0:T(8,128)(2,1)S(1)}, u32[]{:S(2)}, u32[]{:S(2)}) collective-permute-start(bf16[512,384]{1,0:T(8,128)(2,1)S(1)} %given_half.7), channel_id=1, source_target_pairs={{0,24},{8,16},{16,8},{24,0},{1,25},{9,17},{17,9},{25,1},{2,26},{10... | collective-permute-start | bytes 1179656 | tf_op jit(solution)/shard_map/ppermute | solution.py:55
  79.3 1.5 %collective-permute-start.33 = (bf16[2,128,512]{2,1,0:T(8,128)(2,1)S(1)}, bf16[2,128,512]{2,1,0:T(8,128)(2,1)S(1)}, u32[]{:S(2)}, u32[]{:S(2)}) collective-permute-start(bf16[2,128,512]{2,1,0:T(8,128)(2,1)S(1)} %collective-permute-done.30.refs_6_.refs_16_), channel_id=1, source_target_pairs={{4,0},{5,1},{6,2},{7,3},{0,4},{1,5},{2,6},{3,7},{12,8},{13,9},{14,... | collective-permute-start | bytes 786440 | tf_op jit(solution)/shard_map/ppermute | solution.py:50
  81.3 1.9 %collective-permute-done.32.refs_18_.refs_6_ = bf16[2,128,384]{2,1,0:T(8,128)(2,1)S(1)} collective-permute-done((bf16[2,128,384]{2,1,0:T(8,128)(2,1)S(1)}, bf16[2,128,384]{2,1,0:T(8,128)(2,1)S(1)}, u32[]{:S(2)}, u32[]{:S(2)}) %collective-permute-start.32) | collective-permute-done | bytes 196640 | tf_op jit(solution)/shard_map/ppermute | solution.py:45
  83.2 1.5 %collective-permute-start.35 = (bf16[2,128,384]{2,1,0:T(8,128)(2,1)S(1)}, bf16[2,128,384]{2,1,0:T(8,128)(2,1)S(1)}, u32[]{:S(2)}, u32[]{:S(2)}) collective-permute-start(bf16[2,128,384]{2,1,0:T(8,128)(2,1)S(1)} %get-tuple-element.94.refs_10_.refs_4_), channel_id=1, source_target_pairs={{4,0},{5,1},{6,2},{7,3},{0,4},{1,5},{2,6},{3,7},{12,8},{13,9},{14,... | collective-permute-start | bytes 589832 | tf_op jit(solution)/shard_map/ppermute | solution.py:50
  84.7 2.4 %kept_half.5.refs_13_ = bf16[512,1792]{1,0:T(8,128)(2,1)} custom-call(bf16[256,2048]{1,0:T(8,128)(2,1)S(1)} %hidden_acts.1.refs_0_, bf16[256,2048]{1,0:T(8,128)(2,1)S(1)} %collective-permute-done.15.refs_1_, bf16[256,2048]{1,0:T(8,128)(2,1)S(1)} %collective-permute-done.5.refs_2_, ...), custom_call_target="tpu_custom_call", output_to_operand_aliasing={{}: (13, {})} | custom-call | flops 1 | bytes 1 | tf_op jit(solution)/shard_map/kept_half/pallas_call | solution.py:278
  87.1 1.1 collective-permute-done.37.refs_19_.refs_7_
  88.2 5.3 %partial_grads.2 = (f32[2,1024,256]{2,1,0:T(8,128)S(1)}, bf16[1024,256]{1,0:T(8,128)(2,1)}, bf16[512,256]{1,0:T(8,128)(2,1)S(1)}, bf16[512,256]{1,0:T(8,128)(2,1)S(1)}) custom-call(bf16[2,128,256]{2,1,0:T(8,128)(2,1)S(1)} %collective-permute-done.1.refs_6_.refs_0_, bf16[2,128,256]{2,1,0:T(8,128)(2,1)S(1)} %collective-permute-done.2.refs_7_.refs_1_, ...), custom_call_target="tpu_custom_call" | custom-call | flops 1 | bytes 1 | tf_op jit(solution)/shard_map/partial_grads/pallas_call | solution.py:332
  94.1 1.8 %given_half.8 = bf16[512,512]{1,0:T(8,128)(2,1)S(1)} custom-call(bf16[256,2048]{1,0:T(8,128)(2,1)S(1)} %hidden_acts.1.refs_0_, bf16[256,2048]{1,0:T(8,128)(2,1)S(1)} %collective-permute-done.15.refs_1_, bf16[256,2048]{1,0:T(8,128)(2,1)S(1)} %collective-permute-done.5.refs_2_, bf16[256,2048]{1,0:T(8,128)(2,1)S(1)} %collective-permute-done.16.refs_3_, ...), custom_call_target="tpu_custom_call" | custom-call | flops 1 | bytes 1 | tf_op jit(solution)/shard_map/given_half/pallas_call | solution.py:194
  97.9 1.5 %collective-permute-start.38 = (bf16[2,128,384]{2,1,0:T(8,128)(2,1)S(1)}, bf16[2,128,384]{2,1,0:T(8,128)(2,1)S(1)}, u32[]{:S(2)}, u32[]{:S(2)}) collective-permute-start(bf16[2,128,384]{2,1,0:T(8,128)(2,1)S(1)} %collective-permute-done.32.refs_18_.refs_6_), channel_id=1, source_target_pairs={{4,0},{5,1},{6,2},{7,3},{0,4},{1,5},{2,6},{3,7},{12,8},{13,9},{14,... | collective-permute-start | bytes 589832 | tf_op jit(solution)/shard_map/ppermute | solution.py:50
  99.5 1.6 %collective-permute-start.43 = (bf16[512,256]{1,0:T(8,128)(2,1)S(1)}, bf16[512,256]{1,0:T(8,128)(2,1)S(1)}, u32[]{:S(2)}, u32[]{:S(2)}) collective-permute-start(bf16[512,256]{1,0:T(8,128)(2,1)S(1)} %get-tuple-element.109), channel_id=1, source_target_pairs={{0,2},{1,3},{2,0},{3,1},{4,6},{5,7},{6,4},{7,5},{8,10},{9,11},{10,... | collective-permute-start | bytes 786440 | tf_op jit(solution)/shard_map/ppermute | solution.py:45
  102.3 3.3 %collective-permute-done.38.refs_10_.refs_17_ = bf16[2,128,384]{2,1,0:T(8,128)(2,1)S(1)} collective-permute-done((bf16[2,128,384]{2,1,0:T(8,128)(2,1)S(1)}, bf16[2,128,384]{2,1,0:T(8,128)(2,1)S(1)}, u32[]{:S(2)}, u32[]{:S(2)}) %collective-permute-start.38) | collective-permute-done | bytes 196640 | tf_op jit(solution)/shard_map/ppermute | solution.py:50
  105.7 1.5 %collective-permute-start.40 = (bf16[2,128,384]{2,1,0:T(8,128)(2,1)S(1)}, bf16[2,128,384]{2,1,0:T(8,128)(2,1)S(1)}, u32[]{:S(2)}, u32[]{:S(2)}) collective-permute-start(bf16[2,128,384]{2,1,0:T(8,128)(2,1)S(1)} %collective-permute-done.14.refs_11_.refs_5_), channel_id=1, source_target_pairs={{4,0},{5,1},{6,2},{7,3},{0,4},{1,5},{2,6},{3,7},{12,8},{13,9},{14,... | collective-permute-start | bytes 589832 | tf_op jit(solution)/shard_map/ppermute | solution.py:50
  107.2 3.3 %kept_half.6.refs_13_ = bf16[512,1792]{1,0:T(8,128)(2,1)} custom-call(bf16[256,2048]{1,0:T(8,128)(2,1)S(1)} %hidden_acts.1.refs_0_, bf16[256,2048]{1,0:T(8,128)(2,1)S(1)} %collective-permute-done.15.refs_1_, bf16[256,2048]{1,0:T(8,128)(2,1)S(1)} %collective-permute-done.5.refs_2_, ...), custom_call_target="tpu_custom_call", output_to_operand_aliasing={{}: (13, {})} | custom-call | flops 1 | bytes 1 | tf_op jit(solution)/shard_map/kept_half/pallas_call | solution.py:278
  110.5 2.3 %collective-permute-done.40.refs_9_.refs_19_ = bf16[2,128,384]{2,1,0:T(8,128)(2,1)S(1)} collective-permute-done((bf16[2,128,384]{2,1,0:T(8,128)(2,1)S(1)}, bf16[2,128,384]{2,1,0:T(8,128)(2,1)S(1)}, u32[]{:S(2)}, u32[]{:S(2)}) %collective-permute-start.40) | collective-permute-done | bytes 196640 | tf_op jit(solution)/shard_map/ppermute | solution.py:50
  112.8 2.5 %given_half.9.refs_12_ = bf16[512,384]{1,0:T(8,128)(2,1)S(1)} custom-call(bf16[256,2048]{1,0:T(8,128)(2,1)S(1)} %hidden_acts.1.refs_0_, bf16[256,2048]{1,0:T(8,128)(2,1)S(1)} %collective-permute-done.15.refs_1_, bf16[256,2048]{1,0:T(8,128)(2,1)S(1)} %collective-permute-done.5.refs_2_, bf16[256,2048]{1,0:T(8,128)(2,1)S(1)} %collective-permute-done.16.refs_3_, ...), custom_call_target="tpu_custom_call" | custom-call | flops 1 | bytes 1 | tf_op jit(solution)/shard_map/given_half/pallas_call | solution.py:194
  115.4 5.3 %partial_grads.3 = (f32[2,1024,256]{2,1,0:T(8,128)S(1)}, bf16[1024,256]{1,0:T(8,128)(2,1)}, bf16[512,256]{1,0:T(8,128)(2,1)S(1)}, bf16[512,256]{1,0:T(8,128)(2,1)S(1)}) custom-call(bf16[2,128,256]{2,1,0:T(8,128)(2,1)S(1)} %collective-permute-done.refs_8_.refs_0_, bf16[2,128,256]{2,1,0:T(8,128)(2,1)S(1)} %collective-permute-done.4.refs_9_.refs_1_, ...), custom_call_target="tpu_custom_call" | custom-call | flops 1 | bytes 1 | tf_op jit(solution)/shard_map/partial_grads/pallas_call | solution.py:332
  120.7 1.5 %collective-permute-done.41.refs_12_ = bf16[512,512]{1,0:T(8,128)(2,1)S(1)} collective-permute-done((bf16[512,512]{1,0:T(8,128)(2,1)S(1)}, bf16[512,512]{1,0:T(8,128)(2,1)S(1)}, u32[]{:S(2)}, u32[]{:S(2)}) %collective-permute-start.41) | collective-permute-done | bytes 524320 | tf_op jit(solution)/shard_map/ppermute | solution.py:55
  124.3 0.9 fusion
  125.2 1.1 collective-permute-start.48
  126.3 0.9 collective-permute-start.50
  127.2 2.5 %kept_dot.1.dot_ref = f32[512,384]{1,0:T(8,128)S(1)} custom-call(bf16[256,2048]{1,0:T(8,128)(2,1)S(1)} %hidden_acts.1.refs_0_, bf16[256,2048]{1,0:T(8,128)(2,1)S(1)} %collective-permute-done.15.refs_1_, bf16[256,2048]{1,0:T(8,128)(2,1)S(1)} %collective-permute-done.5.refs_2_, bf16[256,2048]{1,0:T(8,128)(2,1)S(1)} %collective-permute-done.16.refs_3_, ...), custom_call_target="tpu_custom_call" | custom-call | flops 1 | bytes 1 | tf_op jit(solution)/shard_map/kept_dot/pallas_call | solution.py:228
  129.7 2.5 %kept_half.7.refs_2_ = bf16[512,1792]{1,0:T(8,128)(2,1)} custom-call(bf16[256,2048]{1,0:T(8,128)(2,1)S(1)} %hidden_acts.1.refs_0_, bf16[256,2048]{1,0:T(8,128)(2,1)S(1)} %collective-permute-done.15.refs_1_, bf16[256,2048]{1,0:T(8,128)(2,1)S(1)} %collective-permute-done.5.refs_2_, ...), custom_call_target="tpu_custom_call", output_to_operand_aliasing={{}: (13, {})} | custom-call | flops 1 | bytes 1 | tf_op jit(solution)/shard_map/kept_half/pallas_call | solution.py:278
  132.3 2.2 %collective-permute-done.52.refs_0_ = bf16[256,384]{1,0:T(8,128)(2,1)S(1)} collective-permute-done((bf16[256,384]{1,0:T(8,128)(2,1)S(1)}, bf16[256,384]{1,0:T(8,128)(2,1)S(1)}, u32[]{:S(2)}, u32[]{:S(2)}) %collective-permute-start.52) | collective-permute-done | bytes 196640 | tf_op jit(solution)/shard_map/ppermute | solution.py:55
  135.2 3.6 %store_grads.2.refs_2_ = bf16[2,1024,512]{2,1,0:T(8,128)(2,1)} custom-call(s32[2,8,1]{2,1,0:T(8,128)} %copy-done.4, s32[1]{0:T(128)} %bitcast.13.group_ref, bf16[2,1024,512]{2,1,0:T(8,128)(2,1)} %bitcast.32, f32[2,1024,256]{2,1,0:T(8,128)} %copy-done.2, bf16[1024,256]{1,0:T(8,128)(2,1)} %collective-permute-done.51.core_ref, bf16[512,256]{1,0:T(8,128)(2,1)} %copy-done.5, ...), custom_call_target="tpu_custom_call" | custom-call | flops 1 | bytes 1 | tf_op jit(solution)/shard_map/store_grads/pallas_call | solution.py:422
  139.4 3.2 %store_grads.3 = bf16[2,1024,512]{2,1,0:T(8,128)(2,1)} custom-call(s32[2,8,1]{2,1,0:T(8,128)} %copy-done.4, s32[1]{0:T(128)} %bitcast.1.group_ref, bf16[2,1024,512]{2,1,0:T(8,128)(2,1)} %bitcast.33, f32[2,1024,256]{2,1,0:T(8,128)} %copy-done.3, bf16[1024,256]{1,0:T(8,128)(2,1)} %collective-permute-done.46.core_ref, ...), custom_call_target="tpu_custom_call", output_to_operand_aliasing={{}: (7, {})} | custom-call | flops 1 | bytes 1 | tf_op jit(solution)/shard_map/store_grads/pallas_call | solution.py:422
  142.7 2.7 %collective-permute-done.53.refs_1_ = bf16[256,384]{1,0:T(8,128)(2,1)S(1)} collective-permute-done((bf16[256,384]{1,0:T(8,128)(2,1)S(1)}, bf16[256,384]{1,0:T(8,128)(2,1)S(1)}, u32[]{:S(2)}, u32[]{:S(2)}) %collective-permute-start.53) | collective-permute-done | bytes 196640 | tf_op jit(solution)/shard_map/ppermute | solution.py:55
  145.4 0.8 kept_add.1
  (82 shorter events, 15.8 us)
Async XLA Ops:
  1.8 3.7 %collective-permute-start.3 = (bf16[2,128,256]{2,1,0:T(8,128)(2,1)S(1)}, bf16[2,128,256]{2,1,0:T(8,128)(2,1)S(1)}, u32[]{:S(2)}, u32[]{:S(2)}) collective-permute-start(bf16[2,128,256]{2,1,0:T(8,128)(2,1)S(1)} %get-tuple-element.140), channel_id=1, source_target_pairs={{0,1},{1,0},{2,3},{3,2},{4,5},{5,4},{6,7},{7,6},{8,9},{9,8},{10,11... | collective-permute-start | bytes 393224 | tf_op jit(solution)/shard_map/ppermute | solution.py:45
  1.9 7.9 %collective-permute-start.2 = (bf16[2,128,256]{2,1,0:T(8,128)(2,1)S(1)}, bf16[2,128,256]{2,1,0:T(8,128)(2,1)S(1)}, u32[]{:S(2)}, u32[]{:S(2)}) collective-permute-start(bf16[2,128,256]{2,1,0:T(8,128)(2,1)S(1)} %get-tuple-element.141), channel_id=1, source_target_pairs={{0,3},{1,2},{2,1},{3,0},{4,7},{5,6},{6,5},{7,4},{8,11},{9,10},{10,... | collective-permute-start | bytes 393224 | tf_op jit(solution)/shard_map/ppermute | solution.py:45
  3.5 7.1 %collective-permute-start.1 = (bf16[2,128,256]{2,1,0:T(8,128)(2,1)S(1)}, bf16[2,128,256]{2,1,0:T(8,128)(2,1)S(1)}, u32[]{:S(2)}, u32[]{:S(2)}) collective-permute-start(bf16[2,128,256]{2,1,0:T(8,128)(2,1)S(1)} %get-tuple-element.142), channel_id=1, source_target_pairs={{0,2},{1,3},{2,0},{3,1},{4,6},{5,7},{6,4},{7,5},{8,10},{9,11},{10,... | collective-permute-start | bytes 393224 | tf_op jit(solution)/shard_map/ppermute | solution.py:45
  4.0 6.5 %collective-permute-start = (bf16[2,128,256]{2,1,0:T(8,128)(2,1)S(1)}, bf16[2,128,256]{2,1,0:T(8,128)(2,1)S(1)}, u32[]{:S(2)}, u32[]{:S(2)}) collective-permute-start(bf16[2,128,256]{2,1,0:T(8,128)(2,1)S(1)} %get-tuple-element.143.refs_4_.refs_3_), channel_id=1, source_target_pairs={{4,0},{5,1},{6,2},{7,3},{0,4},{1,5},{2,6},{3,7},{12,8},{13,9},{14,... | collective-permute-start | bytes 393224 | tf_op jit(solution)/shard_map/ppermute | solution.py:50
  5.6 6.5 %collective-permute-start.4 = (bf16[2,128,256]{2,1,0:T(8,128)(2,1)S(1)}, bf16[2,128,256]{2,1,0:T(8,128)(2,1)S(1)}, u32[]{:S(2)}, u32[]{:S(2)}) collective-permute-start(bf16[2,128,256]{2,1,0:T(8,128)(2,1)S(1)} %collective-permute-done.3.refs_5_.refs_2_), channel_id=1, source_target_pairs={{4,0},{5,1},{6,2},{7,3},{0,4},{1,5},{2,6},{3,7},{12,8},{13,9},{14,... | collective-permute-start | bytes 393224 | tf_op jit(solution)/shard_map/ppermute | solution.py:50
  6.8 7.8 %copy-start.4 = (s32[2,8,1]{2,1,0:T(8,128)}, s32[2,8,1]{2,1,0:T(8,128)S(1)}, u32[]{:S(2)}) copy-start(s32[2,8,1]{2,1,0:T(8,128)S(1)} %copy.13.route_ref) | copy-start | bytes 196
  6.8 1.6 %copy-start = (bf16[1,2,1024,512]{3,2,1,0:T(8,128)(2,1)S(1)}, bf16[1,2,1024,512]{3,2,1,0:T(8,128)(2,1)}, u32[]{:S(2)}) copy-start(bf16[1,2,1024,512]{3,2,1,0:T(8,128)(2,1)} %param.6) | copy-start | bytes 6291460
  12.0 24.9 %collective-permute-start.5 = (bf16[256,2048]{1,0:T(8,128)(2,1)S(1)}, bf16[256,2048]{1,0:T(8,128)(2,1)S(1)}, u32[]{:S(2)}, u32[]{:S(2)}) collective-permute-start(bf16[256,2048]{1,0:T(8,128)(2,1)S(1)} %hidden_acts.1.refs_0_), channel_id=1, source_target_pairs={{0,2},{1,3},{2,0},{3,1},{4,6},{5,7},{6,4},{7,5},{8,10},{9,11},{10,... | collective-permute-start | bytes 3145736 | tf_op jit(solution)/shard_map/ppermute | solution.py:45
  14.7 4.2 %collective-permute-start.9 = (bf16[2,128,256]{2,1,0:T(8,128)(2,1)S(1)}, bf16[2,128,256]{2,1,0:T(8,128)(2,1)S(1)}, u32[]{:S(2)}, u32[]{:S(2)}) collective-permute-start(bf16[2,128,256]{2,1,0:T(8,128)(2,1)S(1)} %get-tuple-element.138), channel_id=1, source_target_pairs={{0,1},{1,0},{2,3},{3,2},{4,5},{5,4},{6,7},{7,6},{8,9},{9,8},{10,11... | collective-permute-start | bytes 393224 | tf_op jit(solution)/shard_map/ppermute | solution.py:45
  16.0 6.4 %collective-permute-start.13 = (bf16[2,128,512]{2,1,0:T(8,128)(2,1)S(1)}, bf16[2,128,512]{2,1,0:T(8,128)(2,1)S(1)}, u32[]{:S(2)}, u32[]{:S(2)}) collective-permute-start(bf16[2,128,512]{2,1,0:T(8,128)(2,1)S(1)} %get-tuple-element.134), channel_id=1, source_target_pairs={{0,1},{1,0},{2,3},{3,2},{4,5},{5,4},{6,7},{7,6},{8,9},{9,8},{10,11... | collective-permute-start | bytes 786440 | tf_op jit(solution)/shard_map/ppermute | solution.py:45
  18.3 2.1 %collective-permute-start.14 = (bf16[2,128,384]{2,1,0:T(8,128)(2,1)S(1)}, bf16[2,128,384]{2,1,0:T(8,128)(2,1)S(1)}, u32[]{:S(2)}, u32[]{:S(2)}) collective-permute-start(bf16[2,128,384]{2,1,0:T(8,128)(2,1)S(1)} %get-tuple-element.126), channel_id=1, source_target_pairs={{0,1},{1,0},{2,3},{3,2},{4,5},{5,4},{6,7},{7,6},{8,9},{9,8},{10,11... | collective-permute-start | bytes 589832 | tf_op jit(solution)/shard_map/ppermute | solution.py:45
  18.4 2.9 %collective-permute-start.12 = (bf16[2,128,384]{2,1,0:T(8,128)(2,1)S(1)}, bf16[2,128,384]{2,1,0:T(8,128)(2,1)S(1)}, u32[]{:S(2)}, u32[]{:S(2)}) collective-permute-start(bf16[2,128,384]{2,1,0:T(8,128)(2,1)S(1)} %get-tuple-element.128), channel_id=1, source_target_pairs={{0,1},{1,0},{2,3},{3,2},{4,5},{5,4},{6,7},{7,6},{8,9},{9,8},{10,11... | collective-permute-start | bytes 589832 | tf_op jit(solution)/shard_map/ppermute | solution.py:45
  18.8 6.4 %collective-permute-start.6 = (bf16[2,128,256]{2,1,0:T(8,128)(2,1)S(1)}, bf16[2,128,256]{2,1,0:T(8,128)(2,1)S(1)}, u32[]{:S(2)}, u32[]{:S(2)}) collective-permute-start(bf16[2,128,256]{2,1,0:T(8,128)(2,1)S(1)} %collective-permute-done.1.refs_6_.refs_0_), channel_id=1, source_target_pairs={{4,0},{5,1},{6,2},{7,3},{0,4},{1,5},{2,6},{3,7},{12,8},{13,9},{14,... | collective-permute-start | bytes 393224 | tf_op jit(solution)/shard_map/ppermute | solution.py:50
  20.4 16.6 %collective-permute-start.11 = (bf16[2,128,384]{2,1,0:T(8,128)(2,1)S(1)}, bf16[2,128,384]{2,1,0:T(8,128)(2,1)S(1)}, u32[]{:S(2)}, u32[]{:S(2)}) collective-permute-start(bf16[2,128,384]{2,1,0:T(8,128)(2,1)S(1)} %get-tuple-element.69.refs_4_.refs_6_), channel_id=1, source_target_pairs={{4,0},{5,1},{6,2},{7,3},{0,4},{1,5},{2,6},{3,7},{12,8},{13,9},{14,... | collective-permute-start | bytes 589832 | tf_op jit(solution)/shard_map/ppermute | solution.py:50
  21.3 10.9 %collective-permute-start.7 = (bf16[2,128,256]{2,1,0:T(8,128)(2,1)S(1)}, bf16[2,128,256]{2,1,0:T(8,128)(2,1)S(1)}, u32[]{:S(2)}, u32[]{:S(2)}) collective-permute-start(bf16[2,128,256]{2,1,0:T(8,128)(2,1)S(1)} %collective-permute-done.2.refs_7_.refs_1_), channel_id=1, source_target_pairs={{4,0},{5,1},{6,2},{7,3},{0,4},{1,5},{2,6},{3,7},{12,8},{13,9},{14,... | collective-permute-start | bytes 393224 | tf_op jit(solution)/shard_map/ppermute | solution.py:50
  22.4 12.6 %collective-permute-start.8 = (bf16[2,128,256]{2,1,0:T(8,128)(2,1)S(1)}, bf16[2,128,256]{2,1,0:T(8,128)(2,1)S(1)}, u32[]{:S(2)}, u32[]{:S(2)}) collective-permute-start(bf16[2,128,256]{2,1,0:T(8,128)(2,1)S(1)} %get-tuple-element.67.refs_4_), channel_id=1, source_target_pairs={{4,0},{5,1},{6,2},{7,3},{0,4},{1,5},{2,6},{3,7},{12,8},{13,9},{14,... | collective-permute-start | bytes 393224 | tf_op jit(solution)/shard_map/ppermute | solution.py:50
  25.2 11.8 %collective-permute-start.10 = (bf16[2,128,256]{2,1,0:T(8,128)(2,1)S(1)}, bf16[2,128,256]{2,1,0:T(8,128)(2,1)S(1)}, u32[]{:S(2)}, u32[]{:S(2)}) collective-permute-start(bf16[2,128,256]{2,1,0:T(8,128)(2,1)S(1)} %collective-permute-done.9.refs_5_), channel_id=1, source_target_pairs={{4,0},{5,1},{6,2},{7,3},{0,4},{1,5},{2,6},{3,7},{12,8},{13,9},{14,... | collective-permute-start | bytes 393224 | tf_op jit(solution)/shard_map/ppermute | solution.py:50
  37.0 3.1 %collective-permute-start.15 = (bf16[256,2048]{1,0:T(8,128)(2,1)S(1)}, bf16[256,2048]{1,0:T(8,128)(2,1)S(1)}, u32[]{:S(2)}, u32[]{:S(2)}) collective-permute-start(bf16[256,2048]{1,0:T(8,128)(2,1)S(1)} %hidden_acts.1.refs_0_), channel_id=1, source_target_pairs={{0,1},{1,0},{2,3},{3,2},{4,5},{5,4},{6,7},{7,6},{8,9},{9,8},{10,11... | collective-permute-start | bytes 3145736 | tf_op jit(solution)/shard_map/ppermute | solution.py:45
  37.0 4.2 %collective-permute-start.16 = (bf16[256,2048]{1,0:T(8,128)(2,1)S(1)}, bf16[256,2048]{1,0:T(8,128)(2,1)S(1)}, u32[]{:S(2)}, u32[]{:S(2)}) collective-permute-start(bf16[256,2048]{1,0:T(8,128)(2,1)S(1)} %collective-permute-done.5.refs_2_), channel_id=1, source_target_pairs={{0,1},{1,0},{2,3},{3,2},{4,5},{5,4},{6,7},{7,6},{8,9},{9,8},{10,11... | collective-permute-start | bytes 3145736 | tf_op jit(solution)/shard_map/ppermute | solution.py:45
  37.5 14.0 %collective-permute-start.23 = (bf16[2,128,512]{2,1,0:T(8,128)(2,1)S(1)}, bf16[2,128,512]{2,1,0:T(8,128)(2,1)S(1)}, u32[]{:S(2)}, u32[]{:S(2)}) collective-permute-start(bf16[2,128,512]{2,1,0:T(8,128)(2,1)S(1)} %get-tuple-element.79.refs_4_.refs_8_), channel_id=1, source_target_pairs={{4,0},{5,1},{6,2},{7,3},{0,4},{1,5},{2,6},{3,7},{12,8},{13,9},{14,... | collective-permute-start | bytes 786440 | tf_op jit(solution)/shard_map/ppermute | solution.py:50
  39.0 11.0 %collective-permute-start.22 = (bf16[2,128,384]{2,1,0:T(8,128)(2,1)S(1)}, bf16[2,128,384]{2,1,0:T(8,128)(2,1)S(1)}, u32[]{:S(2)}, u32[]{:S(2)}) collective-permute-start(bf16[2,128,384]{2,1,0:T(8,128)(2,1)S(1)} %collective-permute-done.12.refs_5_.refs_7_), channel_id=1, source_target_pairs={{4,0},{5,1},{6,2},{7,3},{0,4},{1,5},{2,6},{3,7},{12,8},{13,9},{14,... | collective-permute-start | bytes 589832 | tf_op jit(solution)/shard_map/ppermute | solution.py:50
  39.5 6.3 %collective-permute-start.18 = (bf16[2,128,256]{2,1,0:T(8,128)(2,1)S(1)}, bf16[2,128,256]{2,1,0:T(8,128)(2,1)S(1)}, u32[]{:S(2)}, u32[]{:S(2)}) collective-permute-start(bf16[2,128,256]{2,1,0:T(8,128)(2,1)S(1)} %get-tuple-element.74), channel_id=1, source_target_pairs={{0,2},{1,3},{2,0},{3,1},{4,6},{5,7},{6,4},{7,5},{8,10},{9,11},{10,... | collective-permute-start | bytes 393224 | tf_op jit(solution)/shard_map/ppermute | solution.py:45
  40.0 5.8 %collective-permute-start.20 = (bf16[2,128,256]{2,1,0:T(8,128)(2,1)S(1)}, bf16[2,128,256]{2,1,0:T(8,128)(2,1)S(1)}, u32[]{:S(2)}, u32[]{:S(2)}) collective-permute-start(bf16[2,128,256]{2,1,0:T(8,128)(2,1)S(1)} %get-tuple-element.76), channel_id=1, source_target_pairs={{0,3},{1,2},{2,1},{3,0},{4,7},{5,6},{6,5},{7,4},{8,11},{9,10},{10,... | collective-permute-start | bytes 393224 | tf_op jit(solution)/shard_map/ppermute | solution.py:45
  42.8 16.3 %collective-permute-start.24 = (bf16[512,256]{1,0:T(8,128)(2,1)S(1)}, bf16[512,256]{1,0:T(8,128)(2,1)S(1)}, u32[]{:S(2)}, u32[]{:S(2)}) collective-permute-start(bf16[512,256]{1,0:T(8,128)(2,1)S(1)} %given_half.5), channel_id=1, source_target_pairs={{0,24},{8,16},{16,8},{24,0},{1,25},{9,17},{17,9},{25,1},{2,26},{10... | collective-permute-start | bytes 786440 | tf_op jit(solution)/shard_map/ppermute | solution.py:55
  45.8 13.2 %collective-permute-start.17 = (bf16[2,128,384]{2,1,0:T(8,128)(2,1)S(1)}, bf16[2,128,384]{2,1,0:T(8,128)(2,1)S(1)}, u32[]{:S(2)}, u32[]{:S(2)}) collective-permute-start(bf16[2,128,384]{2,1,0:T(8,128)(2,1)S(1)} %get-tuple-element.73), channel_id=1, source_target_pairs={{0,2},{1,3},{2,0},{3,1},{4,6},{5,7},{6,4},{7,5},{8,10},{9,11},{10,... | collective-permute-start | bytes 589832 | tf_op jit(solution)/shard_map/ppermute | solution.py:45
  45.8 13.2 %collective-permute-start.25 = (bf16[2,128,384]{2,1,0:T(8,128)(2,1)S(1)}, bf16[2,128,384]{2,1,0:T(8,128)(2,1)S(1)}, u32[]{:S(2)}, u32[]{:S(2)}) collective-permute-start(bf16[2,128,384]{2,1,0:T(8,128)(2,1)S(1)} %get-tuple-element.81), channel_id=1, source_target_pairs={{0,3},{1,2},{2,1},{3,0},{4,7},{5,6},{6,5},{7,4},{8,11},{9,10},{10,... | collective-permute-start | bytes 589832 | tf_op jit(solution)/shard_map/ppermute | solution.py:45
  50.0 6.0 %collective-permute-start.19 = (bf16[2,128,256]{2,1,0:T(8,128)(2,1)S(1)}, bf16[2,128,256]{2,1,0:T(8,128)(2,1)S(1)}, u32[]{:S(2)}, u32[]{:S(2)}) collective-permute-start(bf16[2,128,256]{2,1,0:T(8,128)(2,1)S(1)} %collective-permute-done.18.refs_6_.refs_12_), channel_id=1, source_target_pairs={{4,0},{5,1},{6,2},{7,3},{0,4},{1,5},{2,6},{3,7},{12,8},{13,9},{14,... | collective-permute-start | bytes 393224 | tf_op jit(solution)/shard_map/ppermute | solution.py:50
  51.5 5.9 %collective-permute-start.21 = (bf16[2,128,256]{2,1,0:T(8,128)(2,1)S(1)}, bf16[2,128,256]{2,1,0:T(8,128)(2,1)S(1)}, u32[]{:S(2)}, u32[]{:S(2)}) collective-permute-start(bf16[2,128,256]{2,1,0:T(8,128)(2,1)S(1)} %collective-permute-done.20.refs_7_.refs_13_), channel_id=1, source_target_pairs={{4,0},{5,1},{6,2},{7,3},{0,4},{1,5},{2,6},{3,7},{12,8},{13,9},{14,... | collective-permute-start | bytes 393224 | tf_op jit(solution)/shard_map/ppermute | solution.py:50
  59.1 7.9 %collective-permute-start.26 = (bf16[2,128,384]{2,1,0:T(8,128)(2,1)S(1)}, bf16[2,128,384]{2,1,0:T(8,128)(2,1)S(1)}, u32[]{:S(2)}, u32[]{:S(2)}) collective-permute-start(bf16[2,128,384]{2,1,0:T(8,128)(2,1)S(1)} %collective-permute-done.17.refs_6_.refs_14_), channel_id=1, source_target_pairs={{4,0},{5,1},{6,2},{7,3},{0,4},{1,5},{2,6},{3,7},{12,8},{13,9},{14,... | collective-permute-start | bytes 589832 | tf_op jit(solution)/shard_map/ppermute | solution.py:50
  60.7 16.0 %collective-permute-start.28 = (bf16[2,128,512]{2,1,0:T(8,128)(2,1)S(1)}, bf16[2,128,512]{2,1,0:T(8,128)(2,1)S(1)}, u32[]{:S(2)}, u32[]{:S(2)}) collective-permute-start(bf16[2,128,512]{2,1,0:T(8,128)(2,1)S(1)} %collective-permute-done.13.refs_5_.refs_9_), channel_id=1, source_target_pairs={{4,0},{5,1},{6,2},{7,3},{0,4},{1,5},{2,6},{3,7},{12,8},{13,9},{14,... | collective-permute-start | bytes 786440 | tf_op jit(solution)/shard_map/ppermute | solution.py:50
  61.2 15.5 %collective-permute-start.30 = (bf16[2,128,512]{2,1,0:T(8,128)(2,1)S(1)}, bf16[2,128,512]{2,1,0:T(8,128)(2,1)S(1)}, u32[]{:S(2)}, u32[]{:S(2)}) collective-permute-start(bf16[2,128,512]{2,1,0:T(8,128)(2,1)S(1)} %get-tuple-element.87), channel_id=1, source_target_pairs={{0,2},{1,3},{2,0},{3,1},{4,6},{5,7},{6,4},{7,5},{8,10},{9,11},{10,... | collective-permute-start | bytes 786440 | tf_op jit(solution)/shard_map/ppermute | solution.py:45
  61.7 14.9 %collective-permute-start.31 = (bf16[2,128,512]{2,1,0:T(8,128)(2,1)S(1)}, bf16[2,128,512]{2,1,0:T(8,128)(2,1)S(1)}, u32[]{:S(2)}, u32[]{:S(2)}) collective-permute-start(bf16[2,128,512]{2,1,0:T(8,128)(2,1)S(1)} %get-tuple-element.88), channel_id=1, source_target_pairs={{0,3},{1,2},{2,1},{3,0},{4,7},{5,6},{6,5},{7,4},{8,11},{9,10},{10,... | collective-permute-start | bytes 786440 | tf_op jit(solution)/shard_map/ppermute | solution.py:45
  61.7 14.9 %collective-permute-start.29 = (bf16[512,256]{1,0:T(8,128)(2,1)S(1)}, bf16[512,256]{1,0:T(8,128)(2,1)S(1)}, u32[]{:S(2)}, u32[]{:S(2)}) collective-permute-start(bf16[512,256]{1,0:T(8,128)(2,1)S(1)} %given_half.6), channel_id=1, source_target_pairs={{0,24},{8,16},{16,8},{24,0},{1,25},{9,17},{17,9},{25,1},{2,26},{10... | collective-permute-start | bytes 786440 | tf_op jit(solution)/shard_map/ppermute | solution.py:55
  67.0 7.1 %collective-permute-start.27 = (bf16[2,128,384]{2,1,0:T(8,128)(2,1)S(1)}, bf16[2,128,384]{2,1,0:T(8,128)(2,1)S(1)}, u32[]{:S(2)}, u32[]{:S(2)}) collective-permute-start(bf16[2,128,384]{2,1,0:T(8,128)(2,1)S(1)} %collective-permute-done.25.refs_7_.refs_15_), channel_id=1, source_target_pairs={{4,0},{5,1},{6,2},{7,3},{0,4},{1,5},{2,6},{3,7},{12,8},{13,9},{14,... | collective-permute-start | bytes 589832 | tf_op jit(solution)/shard_map/ppermute | solution.py:50
  76.7 6.5 %collective-permute-start.32 = (bf16[2,128,384]{2,1,0:T(8,128)(2,1)S(1)}, bf16[2,128,384]{2,1,0:T(8,128)(2,1)S(1)}, u32[]{:S(2)}, u32[]{:S(2)}) collective-permute-start(bf16[2,128,384]{2,1,0:T(8,128)(2,1)S(1)} %get-tuple-element.90), channel_id=1, source_target_pairs={{0,2},{1,3},{2,0},{3,1},{4,6},{5,7},{6,4},{7,5},{8,10},{9,11},{10,... | collective-permute-start | bytes 589832 | tf_op jit(solution)/shard_map/ppermute | solution.py:45
  77.7 19.0 %collective-permute-start.36 = (bf16[512,384]{1,0:T(8,128)(2,1)S(1)}, bf16[512,384]{1,0:T(8,128)(2,1)S(1)}, u32[]{:S(2)}, u32[]{:S(2)}) collective-permute-start(bf16[512,384]{1,0:T(8,128)(2,1)S(1)} %given_half.7), channel_id=1, source_target_pairs={{0,24},{8,16},{16,8},{24,0},{1,25},{9,17},{17,9},{25,1},{2,26},{10... | collective-permute-start | bytes 1179656 | tf_op jit(solution)/shard_map/ppermute | solution.py:55
  79.3 14.2 %collective-permute-start.33 = (bf16[2,128,512]{2,1,0:T(8,128)(2,1)S(1)}, bf16[2,128,512]{2,1,0:T(8,128)(2,1)S(1)}, u32[]{:S(2)}, u32[]{:S(2)}) collective-permute-start(bf16[2,128,512]{2,1,0:T(8,128)(2,1)S(1)} %collective-permute-done.30.refs_6_.refs_16_), channel_id=1, source_target_pairs={{4,0},{5,1},{6,2},{7,3},{0,4},{1,5},{2,6},{3,7},{12,8},{13,9},{14,... | collective-permute-start | bytes 786440 | tf_op jit(solution)/shard_map/ppermute | solution.py:50
  80.8 13.3 %collective-permute-start.34 = (bf16[2,128,512]{2,1,0:T(8,128)(2,1)S(1)}, bf16[2,128,512]{2,1,0:T(8,128)(2,1)S(1)}, u32[]{:S(2)}, u32[]{:S(2)}) collective-permute-start(bf16[2,128,512]{2,1,0:T(8,128)(2,1)S(1)} %collective-permute-done.31.refs_7_.refs_17_), channel_id=1, source_target_pairs={{4,0},{5,1},{6,2},{7,3},{0,4},{1,5},{2,6},{3,7},{12,8},{13,9},{14,... | collective-permute-start | bytes 786440 | tf_op jit(solution)/shard_map/ppermute | solution.py:50
  81.3 6.9 %collective-permute-start.37 = (bf16[2,128,384]{2,1,0:T(8,128)(2,1)S(1)}, bf16[2,128,384]{2,1,0:T(8,128)(2,1)S(1)}, u32[]{:S(2)}, u32[]{:S(2)}) collective-permute-start(bf16[2,128,384]{2,1,0:T(8,128)(2,1)S(1)} %get-tuple-element.95), channel_id=1, source_target_pairs={{0,3},{1,2},{2,1},{3,0},{4,7},{5,6},{6,5},{7,4},{8,11},{9,10},{10,... | collective-permute-start | bytes 589832 | tf_op jit(solution)/shard_map/ppermute | solution.py:45
  83.2 13.4 %collective-permute-start.35 = (bf16[2,128,384]{2,1,0:T(8,128)(2,1)S(1)}, bf16[2,128,384]{2,1,0:T(8,128)(2,1)S(1)}, u32[]{:S(2)}, u32[]{:S(2)}) collective-permute-start(bf16[2,128,384]{2,1,0:T(8,128)(2,1)S(1)} %get-tuple-element.94.refs_10_.refs_4_), channel_id=1, source_target_pairs={{4,0},{5,1},{6,2},{7,3},{0,4},{1,5},{2,6},{3,7},{12,8},{13,9},{14,... | collective-permute-start | bytes 589832 | tf_op jit(solution)/shard_map/ppermute | solution.py:50
  84.7 3.5 %copy-start.1 = (bf16[1,1024,1792]{2,1,0:T(8,128)(2,1)S(1)}, bf16[1,1024,1792]{2,1,0:T(8,128)(2,1)}, u32[]{:S(2)}) copy-start(bf16[1,1024,1792]{2,1,0:T(8,128)(2,1)} %param.7) | copy-start | bytes 11010052
  93.5 5.9 %copy-start.2 = (f32[2,1024,256]{2,1,0:T(8,128)}, f32[2,1024,256]{2,1,0:T(8,128)S(1)}, u32[]{:S(2)}) copy-start(f32[2,1024,256]{2,1,0:T(8,128)S(1)} %get-tuple-element.107.keep_ref) | copy-start | bytes 6291460
  96.7 2.7 %collective-permute-start.42 = (bf16[512,256]{1,0:T(8,128)(2,1)S(1)}, bf16[512,256]{1,0:T(8,128)(2,1)S(1)}, u32[]{:S(2)}, u32[]{:S(2)}) collective-permute-start(bf16[512,256]{1,0:T(8,128)(2,1)S(1)} %get-tuple-element.108), channel_id=1, source_target_pairs={{0,1},{1,0},{2,3},{3,2},{4,5},{5,4},{6,7},{7,6},{8,9},{9,8},{10,11... | collective-permute-start | bytes 786440 | tf_op jit(solution)/shard_map/ppermute | solution.py:45
  96.7 2.7 %collective-permute-start.44 = (bf16[512,256]{1,0:T(8,128)(2,1)S(1)}, bf16[512,256]{1,0:T(8,128)(2,1)S(1)}, u32[]{:S(2)}, u32[]{:S(2)}) collective-permute-start(bf16[512,256]{1,0:T(8,128)(2,1)S(1)} %get-tuple-element.110), channel_id=1, source_target_pairs={{0,1},{1,0},{2,3},{3,2},{4,5},{5,4},{6,7},{7,6},{8,9},{9,8},{10,11... | collective-permute-start | bytes 786440 | tf_op jit(solution)/shard_map/ppermute | solution.py:45
  97.2 25.1 %collective-permute-start.41 = (bf16[512,512]{1,0:T(8,128)(2,1)S(1)}, bf16[512,512]{1,0:T(8,128)(2,1)S(1)}, u32[]{:S(2)}, u32[]{:S(2)}) collective-permute-start(bf16[512,512]{1,0:T(8,128)(2,1)S(1)} %given_half.8), channel_id=1, source_target_pairs={{0,24},{8,16},{16,8},{24,0},{1,25},{9,17},{17,9},{25,1},{2,26},{10... | collective-permute-start | bytes 1572872 | tf_op jit(solution)/shard_map/ppermute | solution.py:55
  97.9 7.8 %collective-permute-start.38 = (bf16[2,128,384]{2,1,0:T(8,128)(2,1)S(1)}, bf16[2,128,384]{2,1,0:T(8,128)(2,1)S(1)}, u32[]{:S(2)}, u32[]{:S(2)}) collective-permute-start(bf16[2,128,384]{2,1,0:T(8,128)(2,1)S(1)} %collective-permute-done.32.refs_18_.refs_6_), channel_id=1, source_target_pairs={{4,0},{5,1},{6,2},{7,3},{0,4},{1,5},{2,6},{3,7},{12,8},{13,9},{14,... | collective-permute-start | bytes 589832 | tf_op jit(solution)/shard_map/ppermute | solution.py:50
  99.5 22.7 %collective-permute-start.43 = (bf16[512,256]{1,0:T(8,128)(2,1)S(1)}, bf16[512,256]{1,0:T(8,128)(2,1)S(1)}, u32[]{:S(2)}, u32[]{:S(2)}) collective-permute-start(bf16[512,256]{1,0:T(8,128)(2,1)S(1)} %get-tuple-element.109), channel_id=1, source_target_pairs={{0,2},{1,3},{2,0},{3,1},{4,6},{5,7},{6,4},{7,5},{8,10},{9,11},{10,... | collective-permute-start | bytes 786440 | tf_op jit(solution)/shard_map/ppermute | solution.py:45
  101.1 21.2 %collective-permute-start.45 = (bf16[512,256]{1,0:T(8,128)(2,1)S(1)}, bf16[512,256]{1,0:T(8,128)(2,1)S(1)}, u32[]{:S(2)}, u32[]{:S(2)}) collective-permute-start(bf16[512,256]{1,0:T(8,128)(2,1)S(1)} %get-tuple-element.111), channel_id=1, source_target_pairs={{0,2},{1,3},{2,0},{3,1},{4,6},{5,7},{6,4},{7,5},{8,10},{9,11},{10,... | collective-permute-start | bytes 786440 | tf_op jit(solution)/shard_map/ppermute | solution.py:45
  101.6 8.9 %collective-permute-start.39 = (bf16[2,128,384]{2,1,0:T(8,128)(2,1)S(1)}, bf16[2,128,384]{2,1,0:T(8,128)(2,1)S(1)}, u32[]{:S(2)}, u32[]{:S(2)}) collective-permute-start(bf16[2,128,384]{2,1,0:T(8,128)(2,1)S(1)} %collective-permute-done.37.refs_19_.refs_7_), channel_id=1, source_target_pairs={{4,0},{5,1},{6,2},{7,3},{0,4},{1,5},{2,6},{3,7},{12,8},{13,9},{14,... | collective-permute-start | bytes 589832 | tf_op jit(solution)/shard_map/ppermute | solution.py:50
  105.7 7.2 %collective-permute-start.40 = (bf16[2,128,384]{2,1,0:T(8,128)(2,1)S(1)}, bf16[2,128,384]{2,1,0:T(8,128)(2,1)S(1)}, u32[]{:S(2)}, u32[]{:S(2)}) collective-permute-start(bf16[2,128,384]{2,1,0:T(8,128)(2,1)S(1)} %collective-permute-done.14.refs_11_.refs_5_), channel_id=1, source_target_pairs={{4,0},{5,1},{6,2},{7,3},{0,4},{1,5},{2,6},{3,7},{12,8},{13,9},{14,... | collective-permute-start | bytes 589832 | tf_op jit(solution)/shard_map/ppermute | solution.py:50
  120.7 9.0 %copy-start.3 = (f32[2,1024,256]{2,1,0:T(8,128)}, f32[2,1024,256]{2,1,0:T(8,128)S(1)}, u32[]{:S(2)}) copy-start(f32[2,1024,256]{2,1,0:T(8,128)S(1)} %get-tuple-element.105.keep_ref) | copy-start | bytes 6291460
  122.3 7.5 %copy-start.5 = (bf16[512,256]{1,0:T(8,128)(2,1)}, bf16[512,256]{1,0:T(8,128)(2,1)S(1)}, u32[]{:S(2)}) copy-start(bf16[512,256]{1,0:T(8,128)(2,1)S(1)} %collective-permute-done.43.refs_0_) | copy-start | bytes 786436
  122.3 7.5 %copy-start.6 = (bf16[512,256]{1,0:T(8,128)(2,1)}, bf16[512,256]{1,0:T(8,128)(2,1)S(1)}, u32[]{:S(2)}) copy-start(bf16[512,256]{1,0:T(8,128)(2,1)S(1)} %collective-permute-done.45.refs_1_) | copy-start | bytes 786436
  122.3 1.6 %collective-permute-start.47 = (bf16[512,256]{1,0:T(8,128)(2,1)S(1)}, bf16[512,256]{1,0:T(8,128)(2,1)S(1)}, u32[]{:S(2)}, u32[]{:S(2)}) collective-permute-start(bf16[512,256]{1,0:T(8,128)(2,1)S(1)} %get-tuple-element.116), channel_id=1, source_target_pairs={{0,1},{1,0},{2,3},{3,2},{4,5},{5,4},{6,7},{7,6},{8,9},{9,8},{10,11... | collective-permute-start | bytes 786440 | tf_op jit(solution)/shard_map/ppermute | solution.py:45
  122.4 1.9 %collective-permute-start.49 = (bf16[512,256]{1,0:T(8,128)(2,1)S(1)}, bf16[512,256]{1,0:T(8,128)(2,1)S(1)}, u32[]{:S(2)}, u32[]{:S(2)}) collective-permute-start(bf16[512,256]{1,0:T(8,128)(2,1)S(1)} %get-tuple-element.118), channel_id=1, source_target_pairs={{0,1},{1,0},{2,3},{3,2},{4,5},{5,4},{6,7},{7,6},{8,9},{9,8},{10,11... | collective-permute-start | bytes 786440 | tf_op jit(solution)/shard_map/ppermute | solution.py:45
  122.9 12.3 %collective-permute-start.51 = (bf16[1024,256]{1,0:T(8,128)(2,1)}, bf16[1024,256]{1,0:T(8,128)(2,1)}, u32[]{:S(2)}, u32[]{:S(2)}) collective-permute-start(bf16[1024,256]{1,0:T(8,128)(2,1)} %get-tuple-element.121), channel_id=1, source_target_pairs={{0,1},{1,0},{2,3},{3,2},{4,5},{5,4},{6,7},{7,6},{8,9},{9,8},{10,11... | collective-permute-start | bytes 1572872 | tf_op jit(solution)/shard_map/ppermute | solution.py:45
  123.0 11.5 %collective-permute-start.52 = (bf16[256,384]{1,0:T(8,128)(2,1)S(1)}, bf16[256,384]{1,0:T(8,128)(2,1)S(1)}, u32[]{:S(2)}, u32[]{:S(2)}) collective-permute-start(bf16[256,384]{1,0:T(8,128)(2,1)S(1)} %get-tuple-element.149), channel_id=1, source_target_pairs={{0,24},{8,16},{16,8},{24,0},{1,25},{9,17},{17,9},{25,1},{2,26},{10... | collective-permute-start | bytes 589832 | tf_op jit(solution)/shard_map/ppermute | solution.py:55
  123.7 15.1 %collective-permute-start.46 = (bf16[1024,256]{1,0:T(8,128)(2,1)}, bf16[1024,256]{1,0:T(8,128)(2,1)}, u32[]{:S(2)}, u32[]{:S(2)}) collective-permute-start(bf16[1024,256]{1,0:T(8,128)(2,1)} %get-tuple-element.115), channel_id=1, source_target_pairs={{0,1},{1,0},{2,3},{3,2},{4,5},{5,4},{6,7},{7,6},{8,9},{9,8},{10,11... | collective-permute-start | bytes 1572872 | tf_op jit(solution)/shard_map/ppermute | solution.py:45
  125.2 13.7 %collective-permute-start.48 = (bf16[512,256]{1,0:T(8,128)(2,1)}, bf16[512,256]{1,0:T(8,128)(2,1)}, u32[]{:S(2)}, u32[]{:S(2)}) collective-permute-start(bf16[512,256]{1,0:T(8,128)(2,1)} %get-tuple-element.117), channel_id=1, source_target_pairs={{0,2},{1,3},{2,0},{3,1},{4,6},{5,7},{6,4},{7,5},{8,10},{9,11},{10,... | collective-permute-start | bytes 786440 | tf_op jit(solution)/shard_map/ppermute | solution.py:45
  126.3 13.1 %collective-permute-start.50 = (bf16[512,256]{1,0:T(8,128)(2,1)}, bf16[512,256]{1,0:T(8,128)(2,1)}, u32[]{:S(2)}, u32[]{:S(2)}) collective-permute-start(bf16[512,256]{1,0:T(8,128)(2,1)} %get-tuple-element.119), channel_id=1, source_target_pairs={{0,2},{1,3},{2,0},{3,1},{4,6},{5,7},{6,4},{7,5},{8,10},{9,11},{10,... | collective-permute-start | bytes 786440 | tf_op jit(solution)/shard_map/ppermute | solution.py:45
  134.5 10.9 %collective-permute-start.53 = (bf16[256,384]{1,0:T(8,128)(2,1)S(1)}, bf16[256,384]{1,0:T(8,128)(2,1)S(1)}, u32[]{:S(2)}, u32[]{:S(2)}) collective-permute-start(bf16[256,384]{1,0:T(8,128)(2,1)S(1)} %get-tuple-element.123), channel_id=1, source_target_pairs={{0,24},{8,16},{16,8},{24,0},{1,25},{9,17},{17,9},{25,1},{2,26},{10... | collective-permute-start | bytes 589832 | tf_op jit(solution)/shard_map/ppermute | solution.py:55
